TPU v7x, 128 devices: a whole 4x4x4 slice. The times are simulated.
128 devices in a mesh: seq: 64 (over z, x, y), head: 2 (over core).
Axes of the slice: x: 4, y: 4, z: 4, core: 2. Of those that a mesh axis runs over, the one named last changes fastest.
Arguments:
- queries: float32 [32768, 4096], P('seq', 'head'), may hold values from -6 to 6
- keys: float32 [32768, 4096], P('seq', 'head'), may hold values from -6 to 6
- values: float32 [32768, 4096], P('seq', 'head'), may hold values from -6 to 6
- log_decay: float32 [32, 32768], P('head', 'seq'), may hold values from -1 to 0, as said below
- level_weights: float32 [32, 16, 32768], P('head', None, 'seq'), may hold values from 0.25 to 2.5
- norm_gain: float32 [4096], P('head'), may hold values from 0.1 to 1.9
- out_weight: float32 [4096, 2048], P('head', 'seq'), may hold values from -0.09375 to 0.09375
Outputs:
- mixed: float32 [32768, 2048], P('seq', 'head')
Inputs may be any that keep to these rules, and one draw needn't show every extreme that they name: `log_decay`: every entry is non-positive.
All inputs are finite; a program needn't handle non-finite values.
Results may differ from a plain program's by a relative error of at most 0.0003.
Values sent between devices are 32-bit elements; how exact they have to be, the bound alone decides.
No kernel may reach another device: no remote copies, remote signals or barrier semaphores. Data moves between devices by JAX's collectives and lax.ppermute only.
A program may use at most 192 MiB of HBM per device.

v0:
```python
import jax
import jax.numpy as jnp
from jax import lax
from jax.sharding import PartitionSpec as P

HIGH = lax.Precision.HIGHEST


def from_partner(value, axis, bit):
    mask = 2**bit
    pairs = [(source, source ^ mask) for source in range(lax.axis_size(axis))]
    return lax.ppermute(value, axis, pairs)


def laid_out(pieces, dim):
    shape = list(pieces.shape[1:])
    shape[dim] *= pieces.shape[0]
    return jnp.moveaxis(pieces, 0, dim).reshape(shape)


def on_gathered_pieces(array, axis, dim, work, out_dim):
    width = array.shape[dim]
    pieces = jnp.split(array, 2, axis=dim) if width % 2 == 0 else [array]
    leading = jnp.arange(lax.axis_size(axis)) * width
    blocks = [lax.all_gather(piece, axis) for piece in pieces]
    made = [jax.vmap(work)(b, leading + k * (width // len(pieces))) for k, b in enumerate(blocks)]
    return laid_out(jnp.concatenate(made, axis=out_dim + 1), out_dim)


def cut_along(array, dim, size):
    shape = array.shape
    pieces = array.reshape(*shape[:dim], size, shape[dim] // size, *shape[dim + 1 :])
    return jnp.moveaxis(pieces, dim, 0)


def sent_and_summed(array, axis, dim):
    pieces = cut_along(array, dim, lax.axis_size(axis))
    arrived = lax.all_to_all(pieces, axis, split_axis=0, concat_axis=0, tiled=True)
    return arrived.sum(axis=0)


def local(queries, keys, values, log_decay, level_weights, norm_gain, out_weight):
    head_count, tok_count = log_decay.shape
    feature_count = queries.shape[1]
    head_size = feature_count // head_count
    tok_bits = tok_count.bit_length() - 1
    seq_bits = lax.axis_size("seq").bit_length() - 1
    seq_index = lax.axis_index("seq")
    query_heads = queries.reshape(tok_count, head_count, head_size) * head_size ** (-0.5)
    key_heads = keys.reshape(tok_count, head_count, head_size)
    value_heads = values.reshape(tok_count, head_count, head_size)
    decay_sum = jnp.cumsum(log_decay, axis=1)
    span_decay = decay_sum[:, -1]
    positions = jnp.arange(tok_count, dtype=jnp.int32)
    mixed_bits = positions[:, None] ^ positions[None, :]
    level_ids = jnp.zeros((tok_count, tok_count), jnp.int32)
    for level_bit in range(tok_bits):
        level_ids = level_ids + (mixed_bits >> level_bit > 0).astype(jnp.int32)
    onehot = (level_ids[None] == jnp.arange(tok_bits + 1, dtype=jnp.int32)[:, None, None]).astype(
        jnp.float32
    )
    near = jnp.einsum("hli,lij->hij", level_weights[:, : tok_bits + 1, :], onehot, precision=HIGH)
    causal = positions[:, None] >= positions[None, :]
    gap = jnp.where(causal[None], decay_sum[:, :, None] - decay_sum[:, None, :], -jnp.inf)
    scores = (
        jnp.einsum("ihd,jhd->hij", query_heads, key_heads, precision=HIGH) * near * jnp.exp(gap)
    )
    local_out = jnp.einsum("hij,jhd->ihd", scores, value_heads, precision=HIGH)
    fade_weight = jnp.exp(span_decay[:, None] - decay_sum)
    own_state = jnp.einsum("jhd,hj,jhe->hde", key_heads, fade_weight, value_heads, precision=HIGH)
    level_states = []
    block_state = own_state
    block_total = span_decay
    before_sum = jnp.zeros_like(span_decay)
    for level_bit in range(seq_bits):
        other_state, other_total = from_partner((block_state, block_total), "seq", level_bit)
        is_upper = seq_index >> level_bit & 1 == 1
        reach = jnp.exp(jnp.where(is_upper, before_sum, -jnp.inf))
        level_states.append(reach[:, None, None] * other_state)
        low_state = jnp.where(is_upper, other_state, block_state)
        high_state = jnp.where(is_upper, block_state, other_state)
        high_total = jnp.where(is_upper, block_total, other_total)
        block_state = jnp.exp(high_total)[:, None, None] * low_state + high_state
        before_sum = before_sum + jnp.where(is_upper, other_total, jnp.zeros_like(other_total))
        block_total = block_total + other_total
    stacked = jnp.stack(level_states, axis=1)
    far_weight = level_weights[:, tok_bits + 1 :, :] * jnp.exp(decay_sum)[:, None, :]
    weighted = query_heads[:, :, None, :] * far_weight.transpose(2, 0, 1)[:, :, :, None]
    far_out = jnp.einsum("ihld,hlde->ihe", weighted, stacked, precision=HIGH)
    total_out = local_out + far_out
    root_mean = jnp.sqrt(jnp.mean(total_out * total_out, axis=-1, keepdims=True) + 1e-06)
    normed = (total_out / root_mean).reshape(tok_count, feature_count) * norm_gain

    def project(piece, start):
        return jnp.dot(normed, piece, precision=HIGH, preferred_element_type=jnp.float32)

    partials = on_gathered_pieces(out_weight, "seq", 1, project, 1)
    return sent_and_summed(partials, "head", 1)


def solution(mesh):
    return jax.shard_map(
        local,
        mesh=mesh,
        in_specs=(
            P("seq", "head"),
            P("seq", "head"),
            P("seq", "head"),
            P("head", "seq"),
            P("head", None, "seq"),
            P("head"),
            P("head", "seq"),
        ),
        out_specs=P("seq", "head"),
        check_vma=False,
    )
```

profile of v0, /device:TPU:25, one launch (start us, length us, event | category | flops | bytes accessed | tf_op | source)
XLA Modules:
  0.0 355.9 jit_solution(1349413895239266273)
XLA Ops:
  10.4 5.4 %copy.55 = f32[512,2048]{0,1:T(8,128)} copy(f32[512,2048]{1,0:T(8,128)} %param.9) | data formatting | bytes 8388608 | tf_op jit(solution)/shard_map/reshape | solution.py:51
  16.1 7.8 %fusion.41 = f32[16,128,128]{1,2,0:T(8,128)S(1)} fusion(f32[512,16,128]{0,2,1:T(8,128)} %bitcast.100, f32[512,16]{0,1:T(8,128)S(1)} %get-tuple-element.11, f32[512,2048]{1,0:T(8,128)} %param.8), kind=kOutput, calls=%fused_computation.42 | convolution fusion | flops 1611661312 | bytes 9469952 | tf_op jit(solution)/shard_map/jhd,hj,jhe->hde/dot_general | solution.py:70
  25.5 2.1 convert_add_fusion
  27.6 25.1 %collective-permute-done.1 = f32[16]{0:T(128)S(1)} collective-permute-done((f32[16]{0:T(128)S(1)}, f32[16]{0:T(128)S(1)}, u32[]{:S(2)}, u32[]{:S(2)}) %collective-permute-start.1) | collective-permute-done | bytes 96 | tf_op jit(solution)/shard_map/ppermute | solution.py:12
  54.2 4.6 %copy.43 = f32[16,10,512]{1,0,2:T(8,128)} copy(f32[16,10,512]{2,1,0:T(8,128)} %bitcast.108) | data formatting | bytes 655360 | tf_op jit(solution)/shard_map/slice | solution.py:62
  58.8 17.8 %fusion.9 = f32[512,512,16]{1,2,0:T(8,128)} fusion(f32[16,10,512]{1,0,2:T(8,128)} %copy.43, s32[512,512]{1,0:T(8,128)} %convert_add_fusion), kind=kOutput, calls=%fused_computation.10 | convolution fusion | flops 505937920 | bytes 18153472 | tf_op jit(solution)/shard_map/hli,lij->hij/dot_general | solution.py:62
  76.6 2.2 collective-permute-start.3
  78.8 5.9 %collective-permute-done.3 = f32[16]{0:T(128)S(1)} collective-permute-done((f32[16]{0:T(128)S(1)}, f32[16]{0:T(128)S(1)}, u32[]{:S(2)}, u32[]{:S(2)}) %collective-permute-start.3) | collective-permute-done | bytes 96 | tf_op jit(solution)/shard_map/ppermute | solution.py:12
  86.2 19.0 %fusion.19 = f32[16,512,512]{2,1,0:T(8,128)} fusion(f32[512,2048]{1,0:T(8,128)} %param.7, f32[512,2048]{1,0:T(8,128)} %param.8), kind=kOutput, calls=%fused_computation.20 | convolution fusion | flops 6443499520 | bytes 25165824 | tf_op jit(solution)/shard_map/ihd,jhd->hij/dot_general | solution.py:66
  106.8 3.4 collective-permute-done.5
  110.2 2.4 select_add_fusion.2
  113.3 38.4 %fusion.3 = f32[16,512,128]{1,2,0:T(8,128)} fusion(f32[512,16,128]{0,2,1:T(8,128)} %bitcast.101, f32[16,512,512]{2,1,0:T(8,128)} %fusion.19, f32[512,512,16]{1,2,0:T(8,128)} %fusion.9, f32[16,512]{1,0:T(8,128)S(1)} %copy_bitcast_fusion.1, pred[512,512]{1,0:T(8,128)(4,1)S(1)} %iota_compare_fusion.2), kind=kOutput, calls=%fused_computation.4 | convolution fusion | flops 6459228160 | bytes 42237952 | tf_op jit(solution)/shard_map/hij,jhd->ihd/dot_general | solution.py:68
  151.8 4.7 %copy_bitcast_fusion = f32[512,16,128]{2,0,1:T(8,128)} fusion(f32[512,2048]{1,0:T(8,128)} %param.7), kind=kLoop, calls=%fused_computation.22 | loop fusion | flops 1048576 | bytes 8388608 | tf_op jit(solution)/shard_map/mul | solution.py:49
  156.5 2.2 collective-permute-start.7
  160.4 2.8 select_add_fusion.1
  163.2 4.2 %collective-permute-start.8 = (f32[16,128,128]{1,2,0:T(8,128)}, f32[16,128,128]{1,2,0:T(8,128)}, u32[]{:S(2)}, u32[]{:S(2)}) collective-permute-start(f32[16,128,128]{1,2,0:T(8,128)} %select_add_fusion.1), channel_id=1, source_target_pairs={{0,32},{2,34},{4,36},{6,38},{8,40},{10,42},{12,44},{14,46},{16,48}... | collective-permute-start | bytes 3145736 | tf_op jit(solution)/shard_map/ppermute | solution.py:12
  168.7 15.4 %collective-permute-done.9 = f32[16]{0:T(128)S(1)} collective-permute-done((f32[16]{0:T(128)S(1)}, f32[16]{0:T(128)S(1)}, u32[]{:S(2)}, u32[]{:S(2)}) %collective-permute-start.9) | collective-permute-done | bytes 96 | tf_op jit(solution)/shard_map/ppermute | solution.py:12
  184.2 1.8 select_add_fusion
  186.0 24.7 %collective-permute-start.10 = (f32[16,128,128]{1,2,0:T(8,128)S(1)}, f32[16,128,128]{1,2,0:T(8,128)S(1)}, u32[]{:S(2)}, u32[]{:S(2)}) collective-permute-start(f32[16,128,128]{1,2,0:T(8,128)S(1)} %select_add_fusion), channel_id=1, source_target_pairs={{0,64},{2,66},{4,68},{6,70},{8,72},{10,74},{12,76},{14,78},{16,80}... | collective-permute-start | bytes 3145736 | tf_op jit(solution)/shard_map/ppermute | solution.py:12
  212.5 2.1 bitcast_dynamic-update-slice_fusion.1
  214.6 22.6 %collective-permute-done.10 = f32[16,128,128]{1,2,0:T(8,128)S(1)} collective-permute-done((f32[16,128,128]{1,2,0:T(8,128)S(1)}, f32[16,128,128]{1,2,0:T(8,128)S(1)}, u32[]{:S(2)}, u32[]{:S(2)}) %collective-permute-start.10) | collective-permute-done | bytes 1048608 | tf_op jit(solution)/shard_map/ppermute | solution.py:12
  237.4 31.7 %multiply_reduce_fusion = (f32[512,16]{0,1:T(8,128)S(1)}, f32[512,16,128]{0,2,1:T(8,128)S(1)}) fusion(f32[16,6,128,128]{2,3,0,1:T(8,128)S(1)} %bitcast_dynamic-update-slice_fusion, f32[512,16,6]{0,1,2:T(8,128)S(1)} %copy.51, f32[512,16,128]{2,0,1:T(8,128)S(1)} %copy-done.3, f32[16,512,128]{1,2,0:T(8,128)S(1)} %copy-done.2), kind=kOutput, calls=%fused_computation.29 | convolution fusion | flops 9673105408 | bytes 19103744 | tf_op jit(solution)/shard_map/ihld,hlde->ihe/dot_general | solution.py:89
  269.1 2.5 broadcast_divide_fusion
  271.6 5.4 %copy.52 = f32[512,2048]{1,0:T(8,128)} copy(f32[512,2048]{0,1:T(8,128)} %bitcast.102) | data formatting | bytes 8388608 | tf_op jit(solution)/shard_map/reshape | solution.py:92
  277.0 11.5 %copy.60 = f32[2,8,64,2048]{3,2,1,0:T(8,128)} copy(f32[2,8,64,2048]{3,1,2,0:T(8,128)} %bitcast.104) | data formatting | bytes 16777216
  288.5 8.4 %copy.61 = f32[2,8,64,2048]{3,2,1,0:T(8,128)S(1)} copy(f32[2,8,64,2048]{3,1,2,0:T(8,128)} %bitcast.105) | data formatting | bytes 16777216
  296.9 13.9 %fusion.35 = f32[64,512,16]{1,0,2:T(8,128)S(1)} fusion(f32[64,2048,16]{1,0,2:T(8,128)S(1)} %bitcast.106, f32[512,2048]{1,0:T(8,128)S(1)} %copy-done.5, f32[2048]{0:T(1024)S(1)} %copy-done.6), kind=kOutput, calls=%fused_computation.40 | convolution fusion | flops 12885950464 | bytes 14688256 | tf_op jit(solution)/shard_map/vmap()/dot_general | solution.py:95
  310.7 13.7 %fusion.38 = f32[64,512,16]{1,0,2:T(8,128)S(1)} fusion(f32[64,2048,16]{1,0,2:T(8,128)S(1)} %bitcast.107, f32[512,2048]{1,0:T(8,128)S(1)} %copy-done.5, f32[2048]{0:T(1024)S(1)} %copy-done.6), kind=kOutput, calls=%fused_computation.41 | convolution fusion | flops 12885950464 | bytes 14688256 | tf_op jit(solution)/shard_map/vmap()/dot_general | solution.py:95
  325.2 2.4 copy.53
  327.6 16.3 %all_to_all.5 = f32[2,512,1024]{1,2,0:T(8,128)} all-to-all(f32[2,512,1024]{1,2,0:T(8,128)S(1)} %bitcast.103), channel_id=1, replica_groups=mesh['seq'=64,'head'=2] {'head'}, dimensions={0} | all-to-all | bytes 8388608 | tf_op jit(solution)/shard_map/all_to_all | solution.py:38
  343.9 2.9 reduce_sum.19
  346.8 1.8 copy.54
  (61 shorter events, 16.7 us)
Async XLA Ops:
  6.5 2.5 copy-start
  6.5 270.5 %all-gather.5.cloned.1.call-start = ((), (), s32[]{:S(2)}) async-start(), calls=%async_computation.1 | async-start | bytes 8519680 | tf_op jit(solution)/shard_map/all_gather | solution.py:25
  8.3 280.2 %all-gather.7.cloned.1.call-start = ((), (), s32[]{:S(2)}) async-start(), calls=%async_computation.2 | async-start | bytes 8519680 | tf_op jit(solution)/shard_map/all_gather | solution.py:25
  23.9 28.8 %collective-permute-start = (f32[16,128,128]{1,2,0:T(8,128)S(1)}, f32[16,128,128]{1,2,0:T(8,128)S(1)}, u32[]{:S(2)}, u32[]{:S(2)}) collective-permute-start(f32[16,128,128]{1,2,0:T(8,128)S(1)} %fusion.41), channel_id=1, source_target_pairs={{0,2},{2,0},{4,6},{6,4},{8,10},{10,8},{12,14},{14,12},{16,18},{18,... | collective-permute-start | bytes 3145736 | tf_op jit(solution)/shard_map/ppermute | solution.py:12
  24.5 28.3 %collective-permute-start.1 = (f32[16]{0:T(128)S(1)}, f32[16]{0:T(128)S(1)}, u32[]{:S(2)}, u32[]{:S(2)}) collective-permute-start(f32[16]{0:T(128)S(1)} %slice_reduce_fusion.1), channel_id=1, source_target_pairs={{0,2},{2,0},{4,6},{6,4},{8,10},{10,8},{12,14},{14,12},{16,18},{18,... | collective-permute-start | bytes 200 | tf_op jit(solution)/shard_map/ppermute | solution.py:12
  53.0 31.6 %collective-permute-start.2 = (f32[16,128,128]{1,2,0:T(8,128)S(1)}, f32[16,128,128]{1,2,0:T(8,128)S(1)}, u32[]{:S(2)}, u32[]{:S(2)}) collective-permute-start(f32[16,128,128]{1,2,0:T(8,128)S(1)} %select_add_fusion.4), channel_id=1, source_target_pairs={{0,4},{2,6},{4,0},{6,2},{8,12},{10,14},{12,8},{14,10},{16,20},{18,... | collective-permute-start | bytes 3145736 | tf_op jit(solution)/shard_map/ppermute | solution.py:12
  76.6 8.0 %collective-permute-start.3 = (f32[16]{0:T(128)S(1)}, f32[16]{0:T(128)S(1)}, u32[]{:S(2)}, u32[]{:S(2)}) collective-permute-start(f32[16]{0:T(128)S(1)} %get-tuple-element.18), channel_id=1, source_target_pairs={{0,4},{2,6},{4,0},{6,2},{8,12},{10,14},{12,8},{14,10},{16,20},{18,... | collective-permute-start | bytes 200 | tf_op jit(solution)/shard_map/ppermute | solution.py:12
  85.8 24.4 %collective-permute-start.4 = (f32[16,128,128]{1,2,0:T(8,128)}, f32[16,128,128]{1,2,0:T(8,128)S(1)}, u32[]{:S(2)}, u32[]{:S(2)}) collective-permute-start(f32[16,128,128]{1,2,0:T(8,128)} %select_add_fusion.3), channel_id=1, source_target_pairs={{0,8},{2,10},{4,12},{6,14},{8,0},{10,2},{12,4},{14,6},{16,24},{18,... | collective-permute-start | bytes 3145736 | tf_op jit(solution)/shard_map/ppermute | solution.py:12
  105.3 5.0 %collective-permute-start.5 = (f32[16]{0:T(128)S(1)}, f32[16]{0:T(128)S(1)}, u32[]{:S(2)}, u32[]{:S(2)}) collective-permute-start(f32[16]{0:T(128)S(1)} %get-tuple-element.16), channel_id=1, source_target_pairs={{0,8},{2,10},{4,12},{6,14},{8,0},{10,2},{12,4},{14,6},{16,24},{18,... | collective-permute-start | bytes 200 | tf_op jit(solution)/shard_map/ppermute | solution.py:12
  112.7 47.8 %collective-permute-start.6 = (f32[16,128,128]{1,2,0:T(8,128)}, f32[16,128,128]{1,2,0:T(8,128)}, u32[]{:S(2)}, u32[]{:S(2)}) collective-permute-start(f32[16,128,128]{1,2,0:T(8,128)} %select_add_fusion.2), channel_id=1, source_target_pairs={{0,16},{2,18},{4,20},{6,22},{8,24},{10,26},{12,28},{14,30},{16,0},... | collective-permute-start | bytes 3145736 | tf_op jit(solution)/shard_map/ppermute | solution.py:12
  156.5 4.0 %collective-permute-start.7 = (f32[16]{0:T(128)S(1)}, f32[16]{0:T(128)S(1)}, u32[]{:S(2)}, u32[]{:S(2)}) collective-permute-start(f32[16]{0:T(128)S(1)} %get-tuple-element.15), channel_id=1, source_target_pairs={{0,16},{2,18},{4,20},{6,22},{8,24},{10,26},{12,28},{14,30},{16,0},... | collective-permute-start | bytes 200 | tf_op jit(solution)/shard_map/ppermute | solution.py:12
  163.2 21.0 %collective-permute-start.8 = (f32[16,128,128]{1,2,0:T(8,128)}, f32[16,128,128]{1,2,0:T(8,128)}, u32[]{:S(2)}, u32[]{:S(2)}) collective-permute-start(f32[16,128,128]{1,2,0:T(8,128)} %select_add_fusion.1), channel_id=1, source_target_pairs={{0,32},{2,34},{4,36},{6,38},{8,40},{10,42},{12,44},{14,46},{16,48}... | collective-permute-start | bytes 3145736 | tf_op jit(solution)/shard_map/ppermute | solution.py:12
  168.4 15.6 %collective-permute-start.9 = (f32[16]{0:T(128)S(1)}, f32[16]{0:T(128)S(1)}, u32[]{:S(2)}, u32[]{:S(2)}) collective-permute-start(f32[16]{0:T(128)S(1)} %get-tuple-element.13), channel_id=1, source_target_pairs={{0,32},{2,34},{4,36},{6,38},{8,40},{10,42},{12,44},{14,46},{16,48}... | collective-permute-start | bytes 200 | tf_op jit(solution)/shard_map/ppermute | solution.py:12
  186.0 51.2 %collective-permute-start.10 = (f32[16,128,128]{1,2,0:T(8,128)S(1)}, f32[16,128,128]{1,2,0:T(8,128)S(1)}, u32[]{:S(2)}, u32[]{:S(2)}) collective-permute-start(f32[16,128,128]{1,2,0:T(8,128)S(1)} %select_add_fusion), channel_id=1, source_target_pairs={{0,64},{2,66},{4,68},{6,70},{8,72},{10,74},{12,76},{14,78},{16,80}... | collective-permute-start | bytes 3145736 | tf_op jit(solution)/shard_map/ppermute | solution.py:12
  210.8 26.5 %copy-start.2 = (f32[16,512,128]{1,2,0:T(8,128)S(1)}, f32[16,512,128]{1,2,0:T(8,128)}, u32[]{:S(2)}) copy-start(f32[16,512,128]{1,2,0:T(8,128)} %fusion.3) | copy-start | bytes 12582916
  210.8 26.5 %copy-start.3 = (f32[512,16,128]{2,0,1:T(8,128)S(1)}, f32[512,16,128]{2,0,1:T(8,128)}, u32[]{:S(2)}) copy-start(f32[512,16,128]{2,0,1:T(8,128)} %copy_bitcast_fusion) | copy-start | bytes 12582916
  288.4 8.4 %copy-start.4 = (f32[2,8,64,2048]{3,2,1,0:T(8,128)S(1)}, f32[2,8,64,2048]{3,2,1,0:T(8,128)}, u32[]{:S(2)}) copy-start(f32[2,8,64,2048]{3,2,1,0:T(8,128)} %copy.60) | copy-start | bytes 25165828
  288.4 8.4 %copy-start.5 = (f32[512,2048]{1,0:T(8,128)S(1)}, f32[512,2048]{1,0:T(8,128)}, u32[]{:S(2)}) copy-start(f32[512,2048]{1,0:T(8,128)} %copy.52) | copy-start | bytes 12582916
  288.4 8.4 %copy-start.6 = (f32[2048]{0:T(1024)S(1)}, f32[2048]{0:T(1024)}, u32[]{:S(2)}) copy-start(f32[2048]{0:T(1024)} %param.12) | copy-start | bytes 24580
  327.6 21.0 %copy-start.1 = (f32[16,512]{1,0:T(8,128)S(1)}, f32[16,512]{1,0:T(8,128)}, u32[]{:S(2)}) copy-start(f32[16,512]{1,0:T(8,128)} %param.10) | copy-start | bytes 98308
Sparse Core Ops, SparseCore 0:
  10.2 92.3 all-gather.4
  105.6 108.1 all-gather.6
where the time goes:
time: 362 us; the launch traced here: 356 us
  matrix products  142 us (39%)
  waiting for transfers between devices  74.9 us (21%)
  local copies, waits for them, and re-layouts  41.7 us (12%)
  starting transfers between devices  38.7 us (11%)
  other arithmetic  27.9 us (8%)
  blocking collectives  16.3 us (5%)
  between operations  14.2 us (4%)
    ppermute x11, waiting for transfers between devices, from_partner(): return lax.ppermute(value, axis, pairs)  74.1 us
    ppermute x11, starting transfers between devices, from_partner(): return lax.ppermute(value, axis, pairs)  38.6 us
    dot_general x1, matrix products, local(): local_out = jnp.einsum('hij,jhd->ihd', scores, value_heads, precision=HIGH)  38.4 us
    dot_general x1, matrix products, local(): far_out = jnp.einsum('ihld,hlde->ihe', weighted, stacked, precision=HIGH)  31.7 us
    dot_general x2, matrix products, project(): jnp.dot(normed, piece, precision=HIGH, preferred_element_type=jnp.float32)  27.6 us
    unnamed x16, local copies, waits for them, and re-layouts  19.9 us
    dot_general x1, matrix products, local(): jnp.einsum('ihd,jhd->hij', query_heads, key_heads, precision=HIGH) * near  19 us
    dot_general x1, matrix products, local(): jnp.einsum('hli,lij->hij', level_weights[:, :tok_bits + 1, :], onehot, pr...  17.8 us
  transfers between devices with their start and end apart: 13, of which 6 were waited for; matrix products, arithmetic and copies ran while one was open for 47% of the time, Pallas kernels for 0%

commit v1 on v0

v1 whole, which is shorter than its diff:
```python
import functools

import jax
import jax.numpy as jnp
from jax import lax
from jax.experimental import pallas as pl
from jax.experimental.pallas import tpu as pltpu
from jax.sharding import PartitionSpec as P

HIGH = lax.Precision.HIGHEST
DH = 128
CHUNK = 128
ROWS = DH + 8
F32 = jnp.float32
BF16 = jnp.bfloat16
NT = (((1,), (1,)), ((), ()))
TN = (((0,), (0,)), ((), ()))
NN = (((1,), (0,)), ((), ()))
VMEM = pl.BlockSpec(memory_space=pltpu.VMEM)
SMEM = pl.BlockSpec(memory_space=pltpu.SMEM)


def params(mib=40):
    return pltpu.CompilerParams(vmem_limit_bytes=mib * 2**20)


def cost(flops, bytes_accessed):
    return pl.CostEstimate(flops=int(flops), bytes_accessed=int(bytes_accessed), transcendentals=0)


def split(x):
    hi = x.astype(BF16)
    return hi, (x - hi.astype(F32)).astype(BF16)


def mm(a, b, dims):
    return lax.dot_general(a, b, dims, preferred_element_type=F32)


def mm3(a, b, dims):
    a_hi, a_lo = split(a)
    b_hi, b_lo = split(b)
    return mm(a_hi, b_hi, dims) + (mm(a_hi, b_lo, dims) + mm(a_lo, b_hi, dims))


def outer_sum(k, v):
    made = mm(jnp.concatenate(split(k), axis=1), jnp.concatenate(split(v), axis=1), TN)
    return made[:DH, :DH] + (made[:DH, DH:] + made[DH:, :DH])


def state_kernel(k_ref, v_ref, ld_ref, out_ref):
    heads, tok = ld_ref.shape
    ld = ld_ref[...]
    hi = ld.astype(BF16)
    rest = ld - hi.astype(F32)
    mid = rest.astype(BF16)
    low = (rest - mid.astype(F32)).astype(BF16)
    later = lax.broadcasted_iota(jnp.int32, (tok, tok), 1) > lax.broadcasted_iota(jnp.int32, (tok, tok), 0)
    later = jnp.where(later, 1.0, 0.0).astype(BF16)
    fade = jnp.exp(mm(later, hi, NT) + (mm(later, mid, NT) + mm(later, low, NT)))
    total = jnp.sum(ld, axis=1, keepdims=True)
    for h in range(heads):
        cols = pl.ds(h * DH, DH)
        out_ref[h, :DH, :] = outer_sum(k_ref[:, cols] * fade[:, h : h + 1], v_ref[:, cols])
        out_ref[h, DH:, :] = jnp.broadcast_to(total[h : h + 1, :], (ROWS - DH, DH))


def own_state(keys, values, log_decay):
    heads, tok = log_decay.shape
    width = heads * DH
    return pl.pallas_call(
        state_kernel,
        out_shape=jax.ShapeDtypeStruct((heads, ROWS, DH), F32),
        in_specs=[VMEM] * 3,
        out_specs=VMEM,
        compiler_params=params(),
        cost_estimate=cost(8 * tok * width * DH, 4 * (2 * tok * width)),
        name="own_state",
    )(keys, values, log_decay)


def merge_kernel(upper_ref, mine_ref, other_ref, out_ref):
    upper = upper_ref[0] == 1
    for h in range(mine_ref.shape[0]):
        mine, other = mine_ref[h], other_ref[h]
        low = jnp.where(upper, other, mine)
        high = jnp.where(upper, mine, other)
        faded = jnp.exp(high[DH : DH + 1, :])
        out_ref[h, :DH, :] = faded * low[:DH] + high[:DH]
        out_ref[h, DH:, :] = low[DH:] + high[DH:]


def merged(upper, mine, other):
    return pl.pallas_call(
        merge_kernel,
        out_shape=jax.ShapeDtypeStruct(mine.shape, F32),
        in_specs=[SMEM, VMEM, VMEM],
        out_specs=VMEM,
        compiler_params=params(16),
        cost_estimate=cost(3 * mine.size, 12 * mine.size),
        name="merge",
    )(upper, mine, other)


def near_kernel(q_ref, k_ref, v_ref, cum_ref, total_ref, w_ref, out_ref):
    heads, tok = cum_ref.shape[1:]
    chunks = tok // CHUNK
    tile_bits = CHUNK.bit_length() - 1
    row = lax.broadcasted_iota(jnp.int32, (CHUNK, CHUNK), 0)
    col = lax.broadcasted_iota(jnp.int32, (CHUNK, CHUNK), 1)
    apart = row ^ col
    causal = row >= col
    for h in range(heads):
        cols = pl.ds(h * DH, DH)
        cum = cum_ref[0, h : h + 1, :]
        weight_cols = jnp.transpose(w_ref[h])
        cum_cols = jnp.transpose(jnp.concatenate([cum] * 8, axis=0))
        states = []
        ends = []
        outs = []
        for m in range(chunks):
            rows = pl.ds(m * CHUNK, CHUNK)
            at = slice(m * CHUNK, (m + 1) * CHUNK)
            q = q_ref[rows, cols] * DH**-0.5
            k = k_ref[rows, cols]
            v = v_ref[rows, cols]
            w = weight_cols[at]
            c = cum_cols[at, 0:1]
            near = jnp.broadcast_to(w[:, 0:1], (CHUNK, CHUNK))
            for bit in range(tile_bits):
                near = jnp.where(apart >= 2**bit, w[:, bit + 1 : bit + 2], near)
            gap = jnp.where(causal, c - cum[:, at], -1e30)
            scores = mm3(q, k, NT) * (near * jnp.exp(gap))
            out = mm3(scores, v, NN)
            for bit in range(2):
                if m >> bit & 1:
                    first = (m >> bit) - 1 << bit
                    seen = states[first]
                    for n in range(first + 1, first + 2**bit):
                        seen = jnp.exp(ends[n]) * seen + states[n]
                    out = out + w[:, tile_bits + 1 + bit : tile_bits + 2 + bit] * mm3(q, seen, NN)
            outs.append(out)
            if m < chunks - 1:
                end = total_ref[h, m : m + 1, :]
                states.append(outer_sum(k * jnp.exp(end[:, 0:1] - c), v))
                ends.append(end)
        for m in range(chunks):
            out_ref[pl.ds(m * CHUNK, CHUNK), cols] = outs[m]


def near_part(queries, keys, values, cum, totals, weights, first, heads):
    tok = queries.shape[0]
    width = heads * DH
    chunks = totals.shape[1]
    wide = pl.BlockSpec((tok, width), lambda i: (0, first // heads))
    return pl.pallas_call(
        near_kernel,
        out_shape=jax.ShapeDtypeStruct((tok, width), F32),
        grid=(1,),
        in_specs=[
            wide,
            wide,
            wide,
            pl.BlockSpec((1, heads, tok), lambda i: (first // heads, 0, 0)),
            pl.BlockSpec((heads, chunks, DH), lambda i: (first // heads, 0, 0)),
            pl.BlockSpec((heads, weights.shape[1], tok), lambda i: (first // heads, 0, 0)),
        ],
        out_specs=pl.BlockSpec((tok, width), lambda i: (0, 0)),
        compiler_params=params(),
        cost_estimate=cost(60 * tok * width * DH, 16 * tok * width),
        name="near",
    )(queries, keys, values, cum.reshape(-1, heads, tok), totals, weights)


def far_kernel(upper_ref, q_ref, near_ref, w_ref, gain_ref, *refs):
    *state_refs, hi_ref, lo_ref = refs
    first = w_ref.shape[1] - len(state_refs)
    q_hi, q_lo = split(q_ref[...] * DH**-0.5)
    q_both = jnp.concatenate([q_hi, q_lo], axis=1)
    weight_cols = jnp.transpose(w_ref[0])
    out = near_ref[...]
    before = jnp.zeros((1, DH), F32)
    for level, ref in enumerate(state_refs):
        upper = upper_ref[level] == 1
        reach = jnp.where(upper, jnp.exp(before), 0.0)
        s_hi, s_lo = split(ref[0, :DH, :] * reach)
        before = before + jnp.where(upper, ref[0, DH : DH + 1, :], 0.0)
        made = mm(q_both, jnp.concatenate([s_hi, s_hi], axis=0), NN) + mm(q_hi, s_lo, NN)
        out = out + weight_cols[:, first + level : first + level + 1] * made
    mean = jnp.mean(out * out, axis=1, keepdims=True)
    out = out * (1.0 / jnp.sqrt(mean + 1e-06)) * gain_ref[...]
    hi, lo = split(out)
    hi_ref[...] = hi
    lo_ref[...] = lo


def far_and_norm(upper, queries, near, weights, gain, states, first):
    heads = states[0].shape[0]
    tok = queries.shape[0]
    levels = weights.shape[1]
    out = jax.ShapeDtypeStruct((tok, heads * DH), BF16)
    return pl.pallas_call(
        far_kernel,
        out_shape=(out, out),
        grid=(heads,),
        in_specs=[
            SMEM,
            pl.BlockSpec((tok, DH), lambda h: (0, first + h)),
            pl.BlockSpec((tok, DH), lambda h: (0, h)),
            pl.BlockSpec((1, levels, tok), lambda h: (first + h, 0, 0)),
            pl.BlockSpec((1, DH), lambda h: (0, first + h)),
        ]
        + [pl.BlockSpec((1, ROWS, DH), lambda h: (h, 0, 0))] * len(states),
        out_specs=[pl.BlockSpec((tok, DH), lambda h: (0, h))] * 2,
        compiler_params=params(),
        cost_estimate=cost(8 * len(states) * tok * heads * DH * DH, 16 * tok * heads * DH),
        name="far",
    )(upper, queries, near, weights, gain, *states)


def project_kernel(side_ref, hi_ref, lo_ref, w_ref, *refs):
    out_ref = refs[-1]
    w_hi, w_lo = split(w_ref[...])
    x_hi, x_lo = hi_ref[...], lo_ref[...]
    made = mm(x_hi, w_hi, NT) + (mm(x_hi, w_lo, NT) + mm(x_lo, w_hi, NT))
    if len(refs) == 2:
        made = made + refs[0][...]
    out_ref[...] = made


def project(side, x_hi, x_lo, weight, part, sides, so_far=None):
    tok, depth = x_hi.shape
    width = weight.shape[0] // sides
    tile = 256
    steps = width // tile
    whole = pl.BlockSpec((tok, depth), lambda i, side: (0, 0))
    moving = pl.BlockSpec((tok, tile), lambda i, side: (0, i))
    more = [] if so_far is None else [so_far]
    return pl.pallas_call(
        project_kernel,
        out_shape=jax.ShapeDtypeStruct((tok, width), F32),
        grid_spec=pltpu.PrefetchScalarGridSpec(
            num_scalar_prefetch=1,
            grid=(steps,),
            in_specs=[
                whole,
                whole,
                pl.BlockSpec((tile, depth), lambda i, side: (side[0] * steps + i, part)),
            ]
            + [moving] * len(more),
            out_specs=moving,
        ),
        compiler_params=params(),
        cost_estimate=cost(6 * tok * depth * width, 4 * (depth * width + 2 * tok * width)),
        name="project",
    )(side, x_hi, x_lo, weight, *more)


def local(queries, keys, values, log_decay, level_weights, norm_gain, out_weight):
    head_count, tok = log_decay.shape
    chunks = tok // CHUNK
    n_seq = lax.axis_size("seq")
    sides = lax.axis_size("head")
    seq_bits = n_seq.bit_length() - 1
    near_levels = tok.bit_length()
    seq_index = lax.axis_index("seq")
    groups = 2
    size = head_count // groups

    weight = lax.all_gather(out_weight.T, "seq", axis=0, tiled=True)

    upper = (seq_index >> jnp.arange(seq_bits, dtype=jnp.int32)) & 1
    blocks = []
    for g in range(groups):
        cols = slice(g * size * DH, (g + 1) * size * DH)
        blocks.append(own_state(keys[:, cols], values[:, cols], log_decay[g * size : (g + 1) * size]))

    upto = jnp.triu(jnp.ones((CHUNK, CHUNK), F32))
    cum = jnp.dot(log_decay.reshape(head_count * chunks, CHUNK), upto, precision=HIGH)
    cum = cum.reshape(head_count, chunks, CHUNK)
    ends = cum[:, :, -1:]
    totals = jnp.broadcast_to(ends, (head_count, chunks, DH))
    starts = [jnp.zeros_like(ends[:, :1])]
    for m in range(chunks - 1):
        starts.append(starts[-1] + ends[:, m : m + 1])
    start = jnp.concatenate(starts, axis=1)
    past = jnp.concatenate([jnp.zeros_like(ends[:, :3]), ends[:, 2:3]], axis=1)
    position = jnp.arange(chunks, dtype=jnp.int32)[None, :, None]
    odd = jnp.where(position % 2 == 1, jnp.exp(cum), 0.0).reshape(head_count, 1, tok)
    late = jnp.where(position >= 2, jnp.exp(cum + past), 0.0).reshape(head_count, 1, tok)
    far = jnp.exp(cum + start).reshape(head_count, 1, tok)
    weights = jnp.concatenate(
        [
            level_weights[:, : near_levels - 2],
            level_weights[:, near_levels - 2 : near_levels - 1] * odd,
            level_weights[:, near_levels - 1 : near_levels] * late,
            level_weights[:, near_levels:] * far,
        ],
        axis=1,
    )
    cum = cum.reshape(head_count, tok)

    near = []
    small = 4
    for g in range(groups):
        parts = [
            near_part(queries, keys, values, cum, totals, weights, first, small)
            for first in range(g * size, (g + 1) * size, small)
        ]
        near.append(jnp.concatenate(parts, axis=1))

    arrived = [[] for _ in range(groups)]
    for bit in range(seq_bits):
        last = bit == seq_bits - 1
        pairs = [(s, s ^ 2**bit) for s in range(n_seq) if not last or not s >> bit & 1]
        for g in range(groups):
            other = lax.ppermute(blocks[g], "seq", pairs)
            arrived[g].append(other)
            if not last:
                blocks[g] = merged(upper[bit : bit + 1], blocks[g], other)

    me = lax.axis_index("head").astype(jnp.int32)
    mine = me.reshape(1)
    theirs = (sides - 1 - me).reshape(1)
    gain = norm_gain.reshape(1, -1)
    to_send = to_keep = None
    for g in range(groups):
        x_hi, x_lo = far_and_norm(upper, queries, near[g], weights, gain, arrived[g], g * size)
        to_send = project(theirs, x_hi, x_lo, weight, g, sides, to_send)
        if g == groups - 1:
            came = lax.ppermute(to_send, "head", [(s, sides - 1 - s) for s in range(sides)])
        to_keep = project(mine, x_hi, x_lo, weight, g, sides, to_keep)
    return to_keep + came


def solution(mesh):
    return jax.shard_map(
        local,
        mesh=mesh,
        in_specs=(
            P("seq", "head"),
            P("seq", "head"),
            P("seq", "head"),
            P("head", "seq"),
            P("head", None, "seq"),
            P("head"),
            P("head", "seq"),
        ),
        out_specs=P("seq", "head"),
        check_vma=False,
    )
```

time: 362 us -> 265 us (0.73)
  the two profiles are of different devices: /device:TPU:25 before, /device:TPU:1 now
where the time goes in v1:
time: 265 us; the launch traced here: 264 us
  waiting for transfers between devices  98.8 us (37%)
  Pallas kernels  82.7 us (31%)
  starting transfers between devices  35.1 us (13%)
  local copies, waits for them, and re-layouts  27.7 us (10%)
  between operations  13.8 us (5%)
  other arithmetic  5.21 us (2%)
    ppermute x12, waiting for transfers between devices, local(): other = lax.ppermute(blocks[g], 'seq', pairs)  98.1 us
    ppermute x12, starting transfers between devices, local(): other = lax.ppermute(blocks[g], 'seq', pairs)  28.8 us
    pallas_call x4, Pallas kernels, project(): pl.pallas_call(project_kernel, out_shape=jax.ShapeDtypeStruct((tok, width...  22.9 us
    pallas_call x4, Pallas kernels, near_part(): pl.pallas_call(near_kernel, out_shape=jax.ShapeDtypeStruct((tok, width),...  22.1 us
    unnamed x58, local copies, waits for them, and re-layouts  20.2 us
    pallas_call x2, Pallas kernels, far_and_norm(): pl.pallas_call(far_kernel, out_shape=(out, out), grid=(heads,), in_specs=...  19.5 us
    pallas_call x10, Pallas kernels, merged(): pl.pallas_call(merge_kernel, out_shape=jax.ShapeDtypeStruct(mine.shape, F...  13.3 us
    ppermute x1, starting transfers between devices, local(): lax.ppermute(to_send, 'head', [(s, sides - 1 - s) for s in range(sides)])  6.3 us
  transfers between devices with their start and end apart: 14, of which 7 were waited for; matrix products, arithmetic and copies ran while one was open for 4% of the time, Pallas kernels for 27%

profile of v1, /device:TPU:1, one launch (start us, length us, event | category | flops | bytes accessed | tf_op | source)
XLA Modules:
  0.0 263.6 jit_solution(10938344376880676592)
XLA Ops:
  8.0 4.3 %fusion.12 = (f32[512,1024]{1,0:T(8,128)S(1)}, f32[512,1024]{1,0:T(8,128)S(1)}, f32[512,1024]{1,0:T(8,128)S(1)}, f32[512,1024]{1,0:T(8,128)S(1)}) fusion(f32[512,2048]{1,0:T(8,128)} %v_ref.7, f32[512,2048]{1,0:T(8,128)} %k_ref.7), kind=kLoop, calls=%fused_computation.28 | loop fusion | bytes 16777216 | tf_op jit(solution)/shard_map/slice | solution.py:276
  12.3 2.5 own_state.2.mine_ref
  14.8 2.2 collective-permute-start
  17.0 2.5 own_state.3.mine_ref
  20.3 9.6 %collective-permute-done.other_ref.refs_0_ = f32[8,136,128]{2,1,0:T(8,128)S(1)} collective-permute-done((f32[8,136,128]{2,1,0:T(8,128)S(1)}, f32[8,136,128]{2,1,0:T(8,128)S(1)}, u32[]{:S(2)}, u32[]{:S(2)}) %collective-permute-start) | collective-permute-done | bytes 557088 | tf_op jit(solution)/shard_map/ppermute | solution.py:317
  30.6 3.3 %collective-permute-start.1 = (f32[8,136,128]{2,1,0:T(8,128)S(1)}, f32[8,136,128]{2,1,0:T(8,128)S(1)}, u32[]{:S(2)}, u32[]{:S(2)}) collective-permute-start(f32[8,136,128]{2,1,0:T(8,128)S(1)} %merge.10.mine_ref), channel_id=1, source_target_pairs={{0,4},{2,6},{4,0},{6,2},{8,12},{10,14},{12,8},{14,10},{16,20},{18,... | collective-permute-start | bytes 1671176 | tf_op jit(solution)/shard_map/ppermute | solution.py:317
  34.5 9.1 %collective-permute-done.6.other_ref.refs_0_ = f32[8,136,128]{2,1,0:T(8,128)S(1)} collective-permute-done((f32[8,136,128]{2,1,0:T(8,128)S(1)}, f32[8,136,128]{2,1,0:T(8,128)S(1)}, u32[]{:S(2)}, u32[]{:S(2)}) %collective-permute-start.6) | collective-permute-done | bytes 557088 | tf_op jit(solution)/shard_map/ppermute | solution.py:317
  44.5 3.3 %collective-permute-start.7 = (f32[8,136,128]{2,1,0:T(8,128)S(1)}, f32[8,136,128]{2,1,0:T(8,128)}, u32[]{:S(2)}, u32[]{:S(2)}) collective-permute-start(f32[8,136,128]{2,1,0:T(8,128)S(1)} %merge.15.mine_ref), channel_id=1, source_target_pairs={{0,4},{2,6},{4,0},{6,2},{8,12},{10,14},{12,8},{14,10},{16,20},{18,... | collective-permute-start | bytes 1671176 | tf_op jit(solution)/shard_map/ppermute | solution.py:317
  47.7 19.5 %collective-permute-done.1.other_ref.refs_1_ = f32[8,136,128]{2,1,0:T(8,128)S(1)} collective-permute-done((f32[8,136,128]{2,1,0:T(8,128)S(1)}, f32[8,136,128]{2,1,0:T(8,128)S(1)}, u32[]{:S(2)}, u32[]{:S(2)}) %collective-permute-start.1) | collective-permute-done | bytes 557088 | tf_op jit(solution)/shard_map/ppermute | solution.py:317
  69.7 12.0 %collective-permute-done.7.other_ref.refs_1_ = f32[8,136,128]{2,1,0:T(8,128)} collective-permute-done((f32[8,136,128]{2,1,0:T(8,128)S(1)}, f32[8,136,128]{2,1,0:T(8,128)}, u32[]{:S(2)}, u32[]{:S(2)}) %collective-permute-start.7) | collective-permute-done | bytes 557088 | tf_op jit(solution)/shard_map/ppermute | solution.py:317
  85.6 2.5 collective-permute-start.3
  89.9 19.7 %collective-permute-done.8.other_ref.refs_2_ = f32[8,136,128]{2,1,0:T(8,128)S(1)} collective-permute-done((f32[8,136,128]{2,1,0:T(8,128)S(1)}, f32[8,136,128]{2,1,0:T(8,128)S(1)}, u32[]{:S(2)}, u32[]{:S(2)}) %collective-permute-start.8) | collective-permute-done | bytes 557088 | tf_op jit(solution)/shard_map/ppermute | solution.py:317
  110.4 2.8 %collective-permute-start.9 = (f32[8,136,128]{2,1,0:T(8,128)S(1)}, f32[8,136,128]{2,1,0:T(8,128)}, u32[]{:S(2)}, u32[]{:S(2)}) collective-permute-start(f32[8,136,128]{2,1,0:T(8,128)S(1)} %merge.17.mine_ref), channel_id=1, source_target_pairs={{0,16},{2,18},{4,20},{6,22},{8,24},{10,26},{12,28},{14,30},{16,0},... | collective-permute-start | bytes 1671176 | tf_op jit(solution)/shard_map/ppermute | solution.py:317
  113.3 22.2 %collective-permute-done.3.other_ref.refs_3_ = f32[8,136,128]{2,1,0:T(8,128)S(1)} collective-permute-done((f32[8,136,128]{2,1,0:T(8,128)S(1)}, f32[8,136,128]{2,1,0:T(8,128)S(1)}, u32[]{:S(2)}, u32[]{:S(2)}) %collective-permute-start.3) | collective-permute-done | bytes 557088 | tf_op jit(solution)/shard_map/ppermute | solution.py:317
  136.2 2.6 collective-permute-start.4
  141.5 2.2 copy-done
  148.1 5.5 %near.5 = f32[512,512]{1,0:T(8,128)S(1)} custom-call(f32[512,2048]{1,0:T(8,128)S(1)} %copy-done.4, f32[512,2048]{1,0:T(8,128)S(1)} %copy-done, f32[512,2048]{1,0:T(8,128)S(1)} %copy-done.2, f32[4,4,512]{2,1,0:T(4,128)S(1)} %reshape_reshape_reshape.2.cum_ref, f32[16,4,128]{2,1,0:T(4,128)S(1)} %broadcast_in_dim.45.total_ref, ...), custom_call_target="tpu_custom_call" | custom-call | flops 2013265920 | bytes 4194304 | tf_op jit(solution)/shard_map/near/pallas_call | solution.py:156
  153.6 5.9 %collective-permute-done.9.other_ref.refs_3_ = f32[8,136,128]{2,1,0:T(8,128)} collective-permute-done((f32[8,136,128]{2,1,0:T(8,128)S(1)}, f32[8,136,128]{2,1,0:T(8,128)}, u32[]{:S(2)}, u32[]{:S(2)}) %collective-permute-start.9) | collective-permute-done | bytes 557088 | tf_op jit(solution)/shard_map/ppermute | solution.py:317
  159.5 2.5 merge.18.mine_ref
  162.1 2.3 collective-permute-start.10
  164.4 5.5 %near.4 = f32[512,512]{1,0:T(8,128)S(1)} custom-call(f32[512,2048]{1,0:T(8,128)S(1)} %copy-done.4, f32[512,2048]{1,0:T(8,128)S(1)} %copy-done, f32[512,2048]{1,0:T(8,128)S(1)} %copy-done.2, f32[4,4,512]{2,1,0:T(4,128)S(1)} %reshape_reshape_reshape.2.cum_ref, f32[16,4,128]{2,1,0:T(4,128)S(1)} %broadcast_in_dim.45.total_ref, ...), custom_call_target="tpu_custom_call" | custom-call | flops 2013265920 | bytes 4194304 | tf_op jit(solution)/shard_map/near/pallas_call | solution.py:156
  169.9 2.5 merge.14
  172.4 5.4 %collective-permute-start.5 = (f32[8,136,128]{2,1,0:T(8,128)}, f32[8,136,128]{2,1,0:T(8,128)S(1)}, u32[]{:S(2)}, u32[]{:S(2)}) collective-permute-start(f32[8,136,128]{2,1,0:T(8,128)} %merge.14), channel_id=1, source_target_pairs={{0,64},{2,66},{4,68},{6,70},{8,72},{10,74},{12,76},{14,78},{16,80}... | collective-permute-start | bytes 1671176 | tf_op jit(solution)/shard_map/ppermute | solution.py:317
  177.9 5.5 %near.7 = f32[512,512]{1,0:T(8,128)S(1)} custom-call(f32[512,2048]{1,0:T(8,128)S(1)} %copy-done.4, f32[512,2048]{1,0:T(8,128)S(1)} %copy-done, f32[512,2048]{1,0:T(8,128)S(1)} %copy-done.2, f32[4,4,512]{2,1,0:T(4,128)S(1)} %reshape_reshape_reshape.2.cum_ref, f32[16,4,128]{2,1,0:T(4,128)S(1)} %broadcast_in_dim.45.total_ref, ...), custom_call_target="tpu_custom_call" | custom-call | flops 2013265920 | bytes 4194304 | tf_op jit(solution)/shard_map/near/pallas_call | solution.py:156
  191.0 5.5 %near.6 = f32[512,512]{1,0:T(8,128)S(1)} custom-call(f32[512,2048]{1,0:T(8,128)S(1)} %copy-done.5, f32[512,2048]{1,0:T(8,128)S(1)} %copy-done.1, f32[512,2048]{1,0:T(8,128)S(1)} %copy-done.3, f32[4,4,512]{2,1,0:T(4,128)S(1)} %reshape_reshape_reshape.2.cum_ref, f32[16,4,128]{2,1,0:T(4,128)S(1)} %broadcast_in_dim.45.total_ref, ...), custom_call_target="tpu_custom_call" | custom-call | flops 2013265920 | bytes 4194304 | tf_op jit(solution)/shard_map/near/pallas_call | solution.py:156
  201.9 9.8 %far.2 = (bf16[512,1024]{1,0:T(8,128)(2,1)S(1)}, bf16[512,1024]{1,0:T(8,128)(2,1)S(1)}) custom-call(s32[6]{0:T(128)S(1)} %shift-right-arithmetic_and_fusion.upper_ref, f32[512,2048]{1,0:T(8,128)S(1)} %copy-done.5, f32[512,1024]{1,0:T(8,128)S(1)} %pad_maximum_fusion.near_ref, f32[16,16,512]{2,1,0:T(8,128)S(1)} %pad_maximum_fusion.2.w_ref, ...), custom_call_target="tpu_custom_call" | custom-call | flops 3221225472 | bytes 8388608 | tf_op jit(solution)/shard_map/far/pallas_call | solution.py:202
  211.8 9.7 %far.3 = (bf16[512,1024]{1,0:T(8,128)(2,1)S(1)}, bf16[512,1024]{1,0:T(8,128)(2,1)S(1)}) custom-call(s32[6]{0:T(128)S(1)} %shift-right-arithmetic_and_fusion.upper_ref, f32[512,2048]{1,0:T(8,128)S(1)} %copy-done.5, f32[512,1024]{1,0:T(8,128)S(1)} %pad_maximum_fusion.1.near_ref, f32[16,16,512]{2,1,0:T(8,128)S(1)} %pad_maximum_fusion.2.w_ref, ...), custom_call_target="tpu_custom_call" | custom-call | flops 3221225472 | bytes 8388608 | tf_op jit(solution)/shard_map/far/pallas_call | solution.py:202
  225.8 5.7 %project.6.refs_0_ = f32[512,1024]{1,0:T(8,128)S(1)} custom-call(s32[1]{0:T(128)} %bitcast.14.side_ref, bf16[512,1024]{1,0:T(8,128)(2,1)S(1)} %copy-done.7, bf16[512,1024]{1,0:T(8,128)(2,1)S(1)} %copy-done.9, f32[2048,2048]{1,0:T(8,128)} %all-gather.2.cloned.1.call-done.w_ref), custom_call_target="tpu_custom_call" | custom-call | flops 3221225472 | bytes 8388608 | tf_op jit(solution)/shard_map/project/pallas_call | solution.py:239
  231.5 5.8 %project.7 = f32[512,1024]{1,0:T(8,128)S(1)} custom-call(s32[1]{0:T(128)} %bitcast.14.side_ref, bf16[512,1024]{1,0:T(8,128)(2,1)S(1)} %get-tuple-element.9.hi_ref, bf16[512,1024]{1,0:T(8,128)(2,1)S(1)} %get-tuple-element.10.lo_ref, f32[2048,2048]{1,0:T(8,128)} %all-gather.2.cloned.1.call-done.w_ref, f32[512,1024]{1,0:T(8,128)S(1)} %project.6.refs_0_), custom_call_target="tpu_custom_call" | custom-call | flops 3221225472 | bytes 8388608 | tf_op jit(solution)/shard_map/project/pallas_call | solution.py:239
  237.3 6.3 %collective-permute-start.12 = (f32[512,1024]{1,0:T(8,128)S(1)}, f32[512,1024]{1,0:T(8,128)S(1)}, u32[]{:S(2)}, u32[]{:S(2)}) collective-permute-start(f32[512,1024]{1,0:T(8,128)S(1)} %project.7), channel_id=1, source_target_pairs={{0,1},{1,0},{2,3},{3,2},{4,5},{5,4},{6,7},{7,6},{8,9},{9,8},{10,11... | collective-permute-start | bytes 6291464 | tf_op jit(solution)/shard_map/ppermute | solution.py:331
  243.6 5.7 %project.4.refs_0_ = f32[512,1024]{1,0:T(8,128)S(1)} custom-call(s32[1]{0:T(128)} %bitcast.side_ref, bf16[512,1024]{1,0:T(8,128)(2,1)S(1)} %copy-done.7, bf16[512,1024]{1,0:T(8,128)(2,1)S(1)} %copy-done.9, f32[2048,2048]{1,0:T(8,128)} %all-gather.2.cloned.1.call-done.w_ref), custom_call_target="tpu_custom_call" | custom-call | flops 3221225472 | bytes 8388608 | tf_op jit(solution)/shard_map/project/pallas_call | solution.py:239
  249.3 5.8 %project.5 = f32[512,1024]{1,0:T(8,128)S(1)} custom-call(s32[1]{0:T(128)} %bitcast.side_ref, bf16[512,1024]{1,0:T(8,128)(2,1)S(1)} %get-tuple-element.9.hi_ref, bf16[512,1024]{1,0:T(8,128)(2,1)S(1)} %get-tuple-element.10.lo_ref, f32[2048,2048]{1,0:T(8,128)} %all-gather.2.cloned.1.call-done.w_ref, f32[512,1024]{1,0:T(8,128)S(1)} %project.4.refs_0_), custom_call_target="tpu_custom_call" | custom-call | flops 3221225472 | bytes 8388608 | tf_op jit(solution)/shard_map/project/pallas_call | solution.py:239
  (109 shorter events, 40.1 us)
Async XLA Ops:
  6.5 216.9 %all-gather.2.cloned.1.call-start = ((), (), s32[]{:S(2)}) async-start(), calls=%async_computation | async-start | bytes 17039360 | tf_op jit(solution)/shard_map/all_gather | solution.py:270
  14.8 15.1 %collective-permute-start = (f32[8,136,128]{2,1,0:T(8,128)S(1)}, f32[8,136,128]{2,1,0:T(8,128)S(1)}, u32[]{:S(2)}, u32[]{:S(2)}) collective-permute-start(f32[8,136,128]{2,1,0:T(8,128)S(1)} %own_state.2.mine_ref), channel_id=1, source_target_pairs={{0,2},{2,0},{4,6},{6,4},{8,10},{10,8},{12,14},{14,12},{16,18},{18,... | collective-permute-start | bytes 1671176 | tf_op jit(solution)/shard_map/ppermute | solution.py:317
  17.0 2.6 copy-start.26
  19.5 24.2 %collective-permute-start.6 = (f32[8,136,128]{2,1,0:T(8,128)S(1)}, f32[8,136,128]{2,1,0:T(8,128)S(1)}, u32[]{:S(2)}, u32[]{:S(2)}) collective-permute-start(f32[8,136,128]{2,1,0:T(8,128)S(1)} %own_state.3.mine_ref), channel_id=1, source_target_pairs={{0,2},{2,0},{4,6},{6,4},{8,10},{10,8},{12,14},{14,12},{16,18},{18,... | collective-permute-start | bytes 1671176 | tf_op jit(solution)/shard_map/ppermute | solution.py:317
  29.9 38.1 %copy-start.14 = (f32[8,136,128]{2,1,0:T(8,128)}, f32[8,136,128]{2,1,0:T(8,128)S(1)}, u32[]{:S(2)}) copy-start(f32[8,136,128]{2,1,0:T(8,128)S(1)} %collective-permute-done.other_ref.refs_0_) | copy-start | bytes 1671172
  30.6 36.6 %collective-permute-start.1 = (f32[8,136,128]{2,1,0:T(8,128)S(1)}, f32[8,136,128]{2,1,0:T(8,128)S(1)}, u32[]{:S(2)}, u32[]{:S(2)}) collective-permute-start(f32[8,136,128]{2,1,0:T(8,128)S(1)} %merge.10.mine_ref), channel_id=1, source_target_pairs={{0,4},{2,6},{4,0},{6,2},{8,12},{10,14},{12,8},{14,10},{16,20},{18,... | collective-permute-start | bytes 1671176 | tf_op jit(solution)/shard_map/ppermute | solution.py:317
  43.7 39.8 %copy-start.12 = (f32[8,136,128]{2,1,0:T(8,128)}, f32[8,136,128]{2,1,0:T(8,128)S(1)}, u32[]{:S(2)}) copy-start(f32[8,136,128]{2,1,0:T(8,128)S(1)} %collective-permute-done.6.other_ref.refs_0_) | copy-start | bytes 1671172
  44.5 37.2 %collective-permute-start.7 = (f32[8,136,128]{2,1,0:T(8,128)S(1)}, f32[8,136,128]{2,1,0:T(8,128)}, u32[]{:S(2)}, u32[]{:S(2)}) collective-permute-start(f32[8,136,128]{2,1,0:T(8,128)S(1)} %merge.15.mine_ref), channel_id=1, source_target_pairs={{0,4},{2,6},{4,0},{6,2},{8,12},{10,14},{12,8},{14,10},{16,20},{18,... | collective-permute-start | bytes 1671176 | tf_op jit(solution)/shard_map/ppermute | solution.py:317
  67.2 18.3 %copy-start.16 = (f32[8,136,128]{2,1,0:T(8,128)}, f32[8,136,128]{2,1,0:T(8,128)S(1)}, u32[]{:S(2)}) copy-start(f32[8,136,128]{2,1,0:T(8,128)S(1)} %collective-permute-done.1.other_ref.refs_1_) | copy-start | bytes 1671172
  68.0 16.8 %collective-permute-start.2 = (f32[8,136,128]{2,1,0:T(8,128)S(1)}, f32[8,136,128]{2,1,0:T(8,128)S(1)}, u32[]{:S(2)}, u32[]{:S(2)}) collective-permute-start(f32[8,136,128]{2,1,0:T(8,128)S(1)} %merge.11.mine_ref), channel_id=1, source_target_pairs={{0,8},{2,10},{4,12},{6,14},{8,0},{10,2},{12,4},{14,6},{16,24},{18,... | collective-permute-start | bytes 1671176 | tf_op jit(solution)/shard_map/ppermute | solution.py:317
  83.5 26.1 %collective-permute-start.8 = (f32[8,136,128]{2,1,0:T(8,128)S(1)}, f32[8,136,128]{2,1,0:T(8,128)S(1)}, u32[]{:S(2)}, u32[]{:S(2)}) collective-permute-start(f32[8,136,128]{2,1,0:T(8,128)S(1)} %merge.16.mine_ref), channel_id=1, source_target_pairs={{0,8},{2,10},{4,12},{6,14},{8,0},{10,2},{12,4},{14,6},{16,24},{18,... | collective-permute-start | bytes 1671176 | tf_op jit(solution)/shard_map/ppermute | solution.py:317
  84.8 5.1 %copy-start.18 = (f32[8,136,128]{2,1,0:T(8,128)}, f32[8,136,128]{2,1,0:T(8,128)S(1)}, u32[]{:S(2)}) copy-start(f32[8,136,128]{2,1,0:T(8,128)S(1)} %collective-permute-done.2.other_ref.refs_2_) | copy-start | bytes 1671172
  85.6 50.0 %collective-permute-start.3 = (f32[8,136,128]{2,1,0:T(8,128)S(1)}, f32[8,136,128]{2,1,0:T(8,128)S(1)}, u32[]{:S(2)}, u32[]{:S(2)}) collective-permute-start(f32[8,136,128]{2,1,0:T(8,128)S(1)} %merge.12.mine_ref), channel_id=1, source_target_pairs={{0,16},{2,18},{4,20},{6,22},{8,24},{10,26},{12,28},{14,30},{16,0},... | collective-permute-start | bytes 1671176 | tf_op jit(solution)/shard_map/ppermute | solution.py:317
  109.6 26.0 %copy-start.20 = (f32[8,136,128]{2,1,0:T(8,128)}, f32[8,136,128]{2,1,0:T(8,128)S(1)}, u32[]{:S(2)}) copy-start(f32[8,136,128]{2,1,0:T(8,128)S(1)} %collective-permute-done.8.other_ref.refs_2_) | copy-start | bytes 1671172
  109.6 31.7 %copy-start.25 = (f32[16,6,512]{2,1,0:T(8,128)S(1)}, f32[16,6,512]{2,1,0:T(8,128)}, u32[]{:S(2)}) copy-start(f32[16,6,512]{2,1,0:T(8,128)} %slice_multiply_fusion) | copy-start | bytes 589828
  110.4 49.1 %collective-permute-start.9 = (f32[8,136,128]{2,1,0:T(8,128)S(1)}, f32[8,136,128]{2,1,0:T(8,128)}, u32[]{:S(2)}, u32[]{:S(2)}) collective-permute-start(f32[8,136,128]{2,1,0:T(8,128)S(1)} %merge.17.mine_ref), channel_id=1, source_target_pairs={{0,16},{2,18},{4,20},{6,22},{8,24},{10,26},{12,28},{14,30},{16,0},... | collective-permute-start | bytes 1671176 | tf_op jit(solution)/shard_map/ppermute | solution.py:317
  135.5 5.8 %copy-start.22 = (f32[8,136,128]{2,1,0:T(8,128)}, f32[8,136,128]{2,1,0:T(8,128)S(1)}, u32[]{:S(2)}) copy-start(f32[8,136,128]{2,1,0:T(8,128)S(1)} %collective-permute-done.3.other_ref.refs_3_) | copy-start | bytes 1671172
  136.2 33.7 %collective-permute-start.4 = (f32[8,136,128]{2,1,0:T(8,128)S(1)}, f32[8,136,128]{2,1,0:T(8,128)}, u32[]{:S(2)}, u32[]{:S(2)}) collective-permute-start(f32[8,136,128]{2,1,0:T(8,128)S(1)} %merge.13.mine_ref), channel_id=1, source_target_pairs={{0,32},{2,34},{4,36},{6,38},{8,40},{10,42},{12,44},{14,46},{16,48}... | collective-permute-start | bytes 1671176 | tf_op jit(solution)/shard_map/ppermute | solution.py:317
  141.5 2.2 copy-start
  143.7 2.2 copy-start.2
  145.9 2.2 copy-start.4
  162.1 34.4 %collective-permute-start.10 = (f32[8,136,128]{2,1,0:T(8,128)}, f32[8,136,128]{2,1,0:T(8,128)}, u32[]{:S(2)}, u32[]{:S(2)}) collective-permute-start(f32[8,136,128]{2,1,0:T(8,128)} %merge.18.mine_ref), channel_id=1, source_target_pairs={{0,32},{2,34},{4,36},{6,38},{8,40},{10,42},{12,44},{14,46},{16,48}... | collective-permute-start | bytes 1671176 | tf_op jit(solution)/shard_map/ppermute | solution.py:317
  172.4 28.1 %collective-permute-start.5 = (f32[8,136,128]{2,1,0:T(8,128)}, f32[8,136,128]{2,1,0:T(8,128)S(1)}, u32[]{:S(2)}, u32[]{:S(2)}) collective-permute-start(f32[8,136,128]{2,1,0:T(8,128)} %merge.14), channel_id=1, source_target_pairs={{0,64},{2,66},{4,68},{6,70},{8,72},{10,74},{12,76},{14,78},{16,80}... | collective-permute-start | bytes 1671176 | tf_op jit(solution)/shard_map/ppermute | solution.py:317
  184.4 2.2 copy-start.1
  186.6 2.2 copy-start.3
  188.8 2.2 copy-start.5
  198.4 1.9 copy-start.11
  198.4 13.3 %collective-permute-start.11 = (f32[8,136,128]{2,1,0:T(8,128)S(1)}, f32[8,136,128]{2,1,0:T(8,128)S(1)}, u32[]{:S(2)}, u32[]{:S(2)}) collective-permute-start(f32[8,136,128]{2,1,0:T(8,128)S(1)} %merge.19), channel_id=1, source_target_pairs={{0,64},{2,66},{4,68},{6,70},{8,72},{10,74},{12,76},{14,78},{16,80}... | collective-permute-start | bytes 1671176 | tf_op jit(solution)/shard_map/ppermute | solution.py:317
  200.3 1.5 copy-start.23
  201.9 9.9 %copy-start.13 = (f32[8,136,128]{2,1,0:T(8,128)S(1)}, f32[8,136,128]{2,1,0:T(8,128)}, u32[]{:S(2)}) copy-start(f32[8,136,128]{2,1,0:T(8,128)} %copy-done.12) | copy-start | bytes 1671172
  201.9 9.9 %copy-start.21 = (f32[8,136,128]{2,1,0:T(8,128)S(1)}, f32[8,136,128]{2,1,0:T(8,128)}, u32[]{:S(2)}) copy-start(f32[8,136,128]{2,1,0:T(8,128)} %copy-done.20) | copy-start | bytes 1671172
  237.3 17.8 %collective-permute-start.12 = (f32[512,1024]{1,0:T(8,128)S(1)}, f32[512,1024]{1,0:T(8,128)S(1)}, u32[]{:S(2)}, u32[]{:S(2)}) collective-permute-start(f32[512,1024]{1,0:T(8,128)S(1)} %project.7), channel_id=1, source_target_pairs={{0,1},{1,0},{2,3},{3,2},{4,5},{5,4},{6,7},{7,6},{8,9},{9,8},{10,11... | collective-permute-start | bytes 6291464 | tf_op jit(solution)/shard_map/ppermute | solution.py:331
  (9 other events, 10.5 us)
Sparse Core Ops, SparseCore 0:
  10.2 153.5 all-gather.1

commit v2 on v1

v2 whole, which is shorter than its diff:
```python
import functools

import jax
import jax.numpy as jnp
from jax import lax
from jax.experimental import pallas as pl
from jax.experimental.pallas import tpu as pltpu
from jax.sharding import PartitionSpec as P

HIGH = lax.Precision.HIGHEST
DH = 128
CHUNK = 128
ROWS = DH + 8
F32 = jnp.float32
BF16 = jnp.bfloat16
NT = (((1,), (1,)), ((), ()))
TN = (((0,), (0,)), ((), ()))
NN = (((1,), (0,)), ((), ()))
ANY = pl.BlockSpec(memory_space=pl.ANY)
VMEM = pl.BlockSpec(memory_space=pltpu.VMEM)
SMEM = pl.BlockSpec(memory_space=pltpu.SMEM)


def params(mib=52):
    return pltpu.CompilerParams(vmem_limit_bytes=mib * 2**20)


def cost(flops, bytes_accessed):
    return pl.CostEstimate(flops=int(flops), bytes_accessed=int(bytes_accessed), transcendentals=0)


def split(x):
    hi = x.astype(BF16)
    return hi, (x - hi.astype(F32)).astype(BF16)


def split3(x):
    hi = x.astype(BF16)
    rest = x - hi.astype(F32)
    mid = rest.astype(BF16)
    return hi, mid, (rest - mid.astype(F32)).astype(BF16)


def mm(a, b, dims):
    return lax.dot_general(a, b, dims, preferred_element_type=F32)


def mm3(a, b, dims):
    a_hi, a_lo = split(a)
    b_hi, b_lo = split(b)
    return mm(a_hi, b_hi, dims) + (mm(a_hi, b_lo, dims) + mm(a_lo, b_hi, dims))


def outer_sum(k, v):
    made = mm(jnp.concatenate(split(k), axis=1), jnp.concatenate(split(v), axis=1), TN)
    return made[:DH, :DH] + (made[:DH, DH:] + made[DH:, :DH])


def state_kernel(k_ref, v_ref, ld_ref, *refs):
    out_ref, fade_ref = refs[-2:]
    heads, tok = ld_ref.shape
    step = k_ref.shape[1] // DH
    i = pl.program_id(0)

    @pl.when(i == 0)
    def _():
        ld = ld_ref[...]
        later = lax.broadcasted_iota(jnp.int32, (tok, tok), 1) > lax.broadcasted_iota(jnp.int32, (tok, tok), 0)
        later = jnp.where(later, 1.0, 0.0).astype(BF16)
        made = mm(later, jnp.concatenate(split3(ld), axis=0), NT)
        fade = jnp.exp(made[:, :heads] + (made[:, heads : 2 * heads] + made[:, 2 * heads :]))
        for j in range(heads // step):
            fade_ref[j] = fade[:, j * step : (j + 1) * step]

    fade = fade_ref[i]
    for h in range(step):
        cols = pl.ds(h * DH, DH)
        out_ref[h, :DH, :] = outer_sum(k_ref[:, cols] * fade[:, h : h + 1], v_ref[:, cols])
        total = jnp.sum(ld_ref[pl.ds(i * step + h, 1), :], axis=1, keepdims=True)
        out_ref[h, DH:, :] = jnp.broadcast_to(total, (ROWS - DH, DH))


def own_state(keys, values, log_decay, group, heads, after=()):
    tok = keys.shape[0]
    step = 2
    steps = heads // step
    wide = pl.BlockSpec((tok, step * DH), lambda i: (0, group * steps + i))
    return pl.pallas_call(
        state_kernel,
        out_shape=jax.ShapeDtypeStruct((heads, ROWS, DH), F32),
        grid=(steps,),
        in_specs=[wide, wide, pl.BlockSpec((heads, tok), lambda i: (group, 0))] + [ANY] * len(after),
        out_specs=pl.BlockSpec((step, ROWS, DH), lambda i: (i, 0, 0)),
        scratch_shapes=[pltpu.VMEM((steps, tok, step), F32)],
        compiler_params=params(),
        cost_estimate=cost(8 * tok * heads * DH * DH, 8 * tok * heads * DH),
        name="own_state",
    )(keys, values, log_decay, *after)


def merge_kernel(bit, upper_ref, mine_ref, other_ref, *refs):
    out_ref = refs[-1]
    upper = upper_ref[bit] == 1
    for h in range(mine_ref.shape[0]):
        mine, other = mine_ref[h], other_ref[h]
        low = jnp.where(upper, other, mine)
        high = jnp.where(upper, mine, other)
        faded = jnp.exp(high[DH : DH + 1, :])
        out_ref[h, :DH, :] = faded * low[:DH] + high[:DH]
        out_ref[h, DH:, :] = low[DH:] + high[DH:]


def merged(bit, upper, mine, other, after=()):
    return pl.pallas_call(
        functools.partial(merge_kernel, bit),
        out_shape=jax.ShapeDtypeStruct(mine.shape, F32),
        in_specs=[SMEM, VMEM, VMEM] + [ANY] * len(after),
        out_specs=VMEM,
        compiler_params=params(16),
        cost_estimate=cost(3 * mine.size, 12 * mine.size),
        name="merge",
    )(upper, mine, other, *after)


def prepare_kernel(ld_ref, w_ref, *refs):
    sums_ref, cols_ref, weights_ref = refs[-3:]
    heads, tok = ld_ref.shape
    levels = w_ref.shape[1]
    chunks = tok // CHUNK
    near_levels = tok.bit_length()
    row = lax.broadcasted_iota(jnp.int32, (CHUNK, CHUNK), 0)
    col = lax.broadcasted_iota(jnp.int32, (CHUNK, CHUNK), 1)
    upto = jnp.where(row <= col, 1.0, 0.0).astype(BF16)
    sums = []
    for m in range(chunks):
        hi, mid, low = split3(ld_ref[:, m * CHUNK : (m + 1) * CHUNK])
        sums.append(mm(hi, upto, NN) + (mm(mid, upto, NN) + mm(low, upto, NN)))
    start = jnp.zeros((heads, 1), F32)
    fulls = []
    halves = []
    for m in range(chunks):
        fulls.append(sums[m] + start)
        halves.append(sums[m] + (sums[m - 1][:, CHUNK - 1 :] if m % 4 == 3 else 0.0))
        start = start + sums[m][:, CHUNK - 1 :]
    cum = jnp.concatenate(sums, axis=1)
    one = jnp.exp(cum)
    two = jnp.exp(jnp.concatenate(halves, axis=1))
    far = jnp.exp(jnp.concatenate(fulls, axis=1))
    for h in range(heads):
        sums_ref[h] = cum[h : h + 1]
    fill = jnp.zeros((CHUNK - heads, tok), F32)
    cols_ref[...] = jnp.transpose(jnp.concatenate([cum, fill], axis=0))
    level = lax.broadcasted_iota(jnp.int32, (levels, tok), 0)
    per = CHUNK // levels
    for g in range(heads // per):
        made = []
        for h in range(g * per, (g + 1) * per):
            decay = jnp.where(level >= near_levels, far[h : h + 1], two[h : h + 1])
            decay = jnp.where(level == near_levels - 2, one[h : h + 1], decay)
            decay = jnp.where(level < near_levels - 2, 1.0, decay)
            made.append(w_ref[h] * decay)
        weights_ref[:, g * CHUNK : (g + 1) * CHUNK] = jnp.transpose(jnp.concatenate(made, axis=0))


def prepare(log_decay, level_weights, after=()):
    heads, tok = log_decay.shape
    levels = level_weights.shape[1]
    return pl.pallas_call(
        prepare_kernel,
        out_shape=(
            jax.ShapeDtypeStruct((heads, 1, tok), F32),
            jax.ShapeDtypeStruct((tok, CHUNK), F32),
            jax.ShapeDtypeStruct((tok, heads * levels), F32),
        ),
        in_specs=[VMEM, VMEM] + [ANY] * len(after),
        out_specs=[VMEM] * 3,
        compiler_params=params(),
        cost_estimate=cost(0, 8 * heads * levels * tok),
        name="prepare",
    )(log_decay, level_weights, *after)


def near_kernel(first, levels, q_ref, k_ref, v_ref, sums_ref, cols_ref, w_ref, *refs):
    out_ref, token_ref = refs[-2:]
    tok = q_ref.shape[0]
    chunks = tok // CHUNK
    tile_bits = CHUNK.bit_length() - 1
    row = lax.broadcasted_iota(jnp.int32, (CHUNK, CHUNK), 0)
    col = lax.broadcasted_iota(jnp.int32, (CHUNK, CHUNK), 1)
    apart = row ^ col
    causal = row >= col
    head = first + pl.program_id(0)
    per = CHUNK // levels
    token_ref[...] = jnp.zeros_like(token_ref)
    states = []
    ends = []
    for m in range(chunks):
        rows = pl.ds(m * CHUNK, CHUNK)
        q = q_ref[rows, :] * DH**-0.5
        k = k_ref[rows, :]
        v = v_ref[rows, :]
        w = pltpu.roll(w_ref[rows, :], (per - head % per) * levels, 1)
        c_cols = pltpu.roll(cols_ref[rows, :], CHUNK - head, 1)
        c = c_cols[:, 0:1]
        near = jnp.broadcast_to(w[:, 0:1], (CHUNK, CHUNK))
        for bit in range(tile_bits):
            near = jnp.where(apart >= 2**bit, w[:, bit + 1 : bit + 2], near)
        gap = jnp.where(causal, c - sums_ref[0, :, m * CHUNK : (m + 1) * CHUNK], -1e30)
        q_hi, q_lo = split(q)
        k_hi, k_lo = split(k)
        q_both = jnp.concatenate([q_hi, q_lo], axis=1)
        scores = mm(q_both, jnp.concatenate([k_hi, k_hi], axis=1), NT) + mm(q_hi, k_lo, NT)
        scores = scores * (near * jnp.exp(gap))
        s_hi, s_lo = split(scores)
        v_hi, v_lo = split(v)
        s_both = jnp.concatenate([s_hi, s_lo], axis=1)
        out = mm(s_both, jnp.concatenate([v_hi, v_hi], axis=0), NN) + mm(s_hi, v_lo, NN)
        for bit in range(2):
            if m >> bit & 1:
                at = (m >> bit) - 1 << bit
                seen = states[at]
                for n in range(at + 1, at + 2**bit):
                    seen = jnp.exp(ends[n]) * seen + states[n]
                level = tile_bits + 1 + bit
                s_hi, s_lo = split(seen)
                made = mm(q_both, jnp.concatenate([s_hi, s_hi], axis=0), NN) + mm(q_hi, s_lo, NN)
                out = out + w[:, level : level + 1] * made
        out_ref[rows, :] = out
        if m < chunks - 1:
            end = c[CHUNK - 1 : CHUNK]
            states.append(outer_sum(k * jnp.exp(end - c), v))
            ends.append(end)


def near_part(queries, keys, values, sums, cols, weights, levels, first, heads, so_far=None, after=()):
    tok = queries.shape[0]
    per = CHUNK // levels
    one = pl.BlockSpec((tok, DH), lambda h: (0, first + h))
    more = [] if so_far is None else [so_far]
    return pl.pallas_call(
        functools.partial(near_kernel, first, levels),
        out_shape=(
            jax.ShapeDtypeStruct(queries.shape, F32),
            jax.ShapeDtypeStruct((8, CHUNK), F32),
        ),
        grid=(heads,),
        in_specs=[
            one,
            one,
            one,
            pl.BlockSpec((1, 1, tok), lambda h: (first + h, 0, 0)),
            pl.BlockSpec(cols.shape, lambda h: (0, 0)),
            pl.BlockSpec((tok, CHUNK), lambda h: (0, (first + h) // per)),
        ]
        + [ANY] * (len(more) + len(after)),
        out_specs=[one, pl.BlockSpec((8, CHUNK), lambda h: (0, 0))],
        input_output_aliases={6: 0} if more else {},
        compiler_params=params(),
        cost_estimate=cost(60 * tok * heads * DH * DH, 16 * tok * heads * DH),
        name="near",
    )(queries, keys, values, sums, cols, weights, *more, *after)


def far_kernel(first, levels, skip, last, count, upper_ref, q_ref, near_ref, w_ref, gain_ref, *refs):
    step = q_ref.shape[1] // DH
    outs = 3 if last else 2
    out_refs, token_ref = refs[-outs:-1], refs[-1]
    per = CHUNK // levels
    total = upper_ref.shape[0]
    head = first + pl.program_id(0) * step
    token_ref[...] = jnp.zeros_like(token_ref)
    w = pltpu.roll(w_ref[...], (per - head % per) * levels, 1)
    for h in range(step):
        cols = pl.ds(h * DH, DH)
        q_hi, q_lo = split(q_ref[:, cols] * DH**-0.5)
        out = near_ref[:, cols]
        before = jnp.zeros((1, DH), F32)
        used = []
        states = []
        for level in range(count):
            ref = refs[level]
            upper = upper_ref[level] == 1
            end = ref.shape[1] - (ROWS - DH)
            if level >= skip:
                reach = jnp.where(upper, jnp.exp(before), 0.0)
                hi, lo = split(ref[h, :DH, :] * reach)
                states.append(jnp.concatenate([hi, hi, lo], axis=0))
                used.append(h * levels + levels - total + level)
            before = before + jnp.where(upper, ref[h, end : end + 1, :], 0.0)
        made = mm(jnp.concatenate([q_hi, q_lo, q_hi], axis=1), jnp.concatenate(states, axis=1), NN)
        for n, at in enumerate(used):
            out = out + w[:, at : at + 1] * made[:, n * DH : (n + 1) * DH]
        if last:
            squares = jnp.concatenate(split(out * out), axis=1)
            mean = mm(squares, jnp.full((2 * DH, DH), 1.0 / DH, BF16), NN)
            out = out * lax.rsqrt(mean + 1e-06) * gain_ref[:, cols]
            hi, lo = split(out)
            out_refs[0][:, cols] = hi
            out_refs[1][:, cols] = lo
        else:
            out_refs[0][:, cols] = out


def far_part(upper, queries, so_far, at, weights, levels, gain, states, first, skip, last, after=()):
    heads = states[0].shape[0]
    tok = queries.shape[0]
    per = CHUNK // levels
    step = 2
    out = jax.ShapeDtypeStruct((tok, heads * DH), BF16 if last else F32)
    outs = 2 if last else 1
    tail = ROWS - DH
    return pl.pallas_call(
        functools.partial(far_kernel, first, levels, skip, last, len(states)),
        out_shape=(out,) * outs + (jax.ShapeDtypeStruct((8, CHUNK), F32),),
        grid=(heads // step,),
        in_specs=[
            SMEM,
            pl.BlockSpec((tok, step * DH), lambda i: (0, first // step + i)),
            pl.BlockSpec((tok, step * DH), lambda i: (0, at // step + i)),
            pl.BlockSpec((tok, CHUNK), lambda i: (0, (first + i * step) // per)),
            pl.BlockSpec((1, step * DH), lambda i: (0, first // step + i)),
        ]
        + [
            pl.BlockSpec((step, ROWS, DH), lambda i: (i, 0, 0))
            if level >= skip
            else pl.BlockSpec((step, tail, DH), lambda i: (i, DH // tail, 0))
            for level in range(len(states))
        ]
        + [ANY] * len(after),
        out_specs=[pl.BlockSpec((tok, step * DH), lambda i: (0, i))] * outs
        + [pl.BlockSpec((8, CHUNK), lambda i: (0, 0))],
        compiler_params=params(),
        cost_estimate=cost(8 * len(states) * tok * heads * DH * DH, 16 * tok * heads * DH),
        name="far",
    )(upper, queries, so_far, weights, gain, *states, *after)


def project_kernel(has_more, side_ref, hi_ref, lo_ref, w_ref, *refs):
    out_ref = refs[-1]
    w_hi, w_lo = split(w_ref[...])
    x_hi, x_lo = hi_ref[...], lo_ref[...]
    made = mm(x_hi, w_hi, NT) + (mm(x_hi, w_lo, NT) + mm(x_lo, w_hi, NT))
    if has_more:
        made = made + refs[0][...]
    out_ref[...] = made


def project(side, x_hi, x_lo, weight, part, sides, so_far=None, after=()):
    tok, depth = x_hi.shape
    width = weight.shape[0] // sides
    tile = 256
    steps = width // tile
    whole = pl.BlockSpec((tok, depth), lambda i, side: (0, 0))
    moving = pl.BlockSpec((tok, tile), lambda i, side: (0, i))
    more = [] if so_far is None else [so_far]
    return pl.pallas_call(
        functools.partial(project_kernel, bool(more)),
        out_shape=jax.ShapeDtypeStruct((tok, width), F32),
        grid_spec=pltpu.PrefetchScalarGridSpec(
            num_scalar_prefetch=1,
            grid=(steps,),
            in_specs=[
                whole,
                whole,
                pl.BlockSpec((tile, depth), lambda i, side: (side[0] * steps + i, part)),
            ]
            + [moving] * len(more)
            + [ANY] * len(after),
            out_specs=moving,
        ),
        compiler_params=params(),
        cost_estimate=cost(6 * tok * depth * width, 4 * (depth * width + 2 * tok * width)),
        name="project",
    )(side, x_hi, x_lo, weight, *more, *after)


def local(queries, keys, values, log_decay, level_weights, norm_gain, out_weight):
    head_count = log_decay.shape[0]
    levels = level_weights.shape[1]
    n_seq = lax.axis_size("seq")
    sides = lax.axis_size("head")
    seq_bits = n_seq.bit_length() - 1
    seq_index = lax.axis_index("seq")
    size = head_count // 2

    weight = lax.all_gather(out_weight.T, "seq", axis=0, tiled=True)
    upper = (seq_index >> jnp.arange(seq_bits, dtype=jnp.int32)) & 1
    gain = norm_gain.reshape(1, -1)

    def send(block, bit):
        def wanted(s):
            above = s >> bit
            return not (bit == seq_bits - 1 and above & 1) and not (bit == seq_bits - 2 and above == 3)

        return lax.ppermute(block, "seq", [(s, s ^ 2**bit) for s in range(n_seq) if wanted(s)])

    small = size // 2
    early = 4

    def near(n, so_far, *after):
        return near_part(
            queries, keys, values, sums, cols, weights, levels, n * small, small, so_far, after
        )

    def far(so_far, at, states, group, skip, last, *after):
        return far_part(
            upper, queries, so_far, at, weights, levels, gain, states, group * size, skip, last, after
        )

    a, came_a, b, came_b = [], [], [], []

    def go(blocks, came, *after):
        bit = len(blocks) - 1
        blocks.append(merged(bit, upper, blocks[bit], came[bit], after))
        came.append(send(blocks[-1], bit + 1))

    a.append(own_state(keys, values, log_decay, 0, size))
    came_a.append(send(a[0], 0))
    sums, cols, weights = prepare(log_decay, level_weights, (a[0],))
    close, token = near(0, None)
    go(a, came_a, token)
    close, token = near(1, close, a[1])
    go(a, came_a, token)
    b.append(own_state(keys, values, log_decay, 1, size, (a[2],)))
    came_b.append(send(b[0], 0))
    close, token = near(2, close, b[0])
    go(a, came_a, token)
    go(b, came_b, a[3])
    close, token = near(3, close, b[1])
    go(a, came_a, token)
    go(b, came_b, a[4])
    far_a, token = far(close, 0, came_a[:early], 0, 0, False, b[2])
    go(a, came_a, token)
    go(b, came_b, a[5])
    go(b, came_b)
    a_hi, a_lo, token = far(far_a, 0, came_a, 0, early, True, b[4])
    far_b, token = far(close, size, came_b[:early], 1, 0, False, token)
    go(b, came_b, token)

    me = lax.axis_index("head").astype(jnp.int32)
    mine = me.reshape(1)
    theirs = (sides - 1 - me).reshape(1)
    to_send = project(theirs, a_hi, a_lo, weight, 0, sides, None, (b[5],))
    to_keep = project(mine, a_hi, a_lo, weight, 0, sides, None, (b[5],))
    b_hi, b_lo, _ = far(far_b, 0, came_b, 1, early, True, to_send, to_keep)
    to_send = project(theirs, b_hi, b_lo, weight, 1, sides, to_send)
    came = lax.ppermute(to_send, "head", [(s, sides - 1 - s) for s in range(sides)])
    to_keep = project(mine, b_hi, b_lo, weight, 1, sides, to_keep)
    return to_keep + came


def solution(mesh):
    return jax.shard_map(
        local,
        mesh=mesh,
        in_specs=(
            P("seq", "head"),
            P("seq", "head"),
            P("seq", "head"),
            P("head", "seq"),
            P("head", None, "seq"),
            P("head"),
            P("head", "seq"),
        ),
        out_specs=P("seq", "head"),
        check_vma=False,
    )
```

time: 265 us -> 227 us (0.86)
  waiting for transfers between devices: 98.8 us -> 64 us
  Pallas kernels: 82.7 us -> 108 us
  local copies, waits for them, and re-layouts: 27.7 us -> 6.69 us
  starting transfers between devices: 35.1 us -> 29.4 us
    ppermute x12, waiting for transfers between devices: 98.1 us -> 58.2 us  [send(): lax.ppermute(block, 'seq', [(s, s ^ 2 ** bit) for s in range(n_seq) if wa...]
    pallas_call x20 -> x23, Pallas kernels: 77.7 us -> 98.7 us  [the longest x4 34.2 us: near_part(): pl.pallas_call(functools.partial(near_kernel, first, levels), out_shape=(...]
    unnamed x58 -> x36, local copies, waits for them, and re-layouts: 20.2 us -> 6.69 us
    slice x6 -> x0, local copies, waits for them, and re-layouts: 6.89 us -> none  [the longest x1 4.31 us: local(): values[:, cols]]
    ppermute x12, starting transfers between devices: 28.8 us -> 22.9 us  [send(): lax.ppermute(block, 'seq', [(s, s ^ 2 ** bit) for s in range(n_seq) if wa...]
    all_gather x1, waiting for transfers between devices: 0.01 us -> 5.02 us  [local(): weight = lax.all_gather(out_weight.T, 'seq', axis=0, tiled=True)]
    pallas_call x2, Pallas kernels: 4.94 us -> 9.55 us  [own_state(): pl.pallas_call(state_kernel, out_shape=jax.ShapeDtypeStruct((heads, ROWS,...]
    mul x2 -> x0, other arithmetic: 2.89 us -> none  [the longest x1 1.71 us: local(): level_weights[:, near_levels:] * far]
  transfers between devices with their start and end apart: 14 -> 14, of which waited for: 7 -> 9; matrix products, arithmetic and copies ran while one was open for 4% -> 0% of each run, Pallas kernels for 27% -> 42%
where the time goes in v2:
time: 227 us; the launch traced here: 225 us
  Pallas kernels  108 us (48%)
  waiting for transfers between devices  64 us (28%)
  starting transfers between devices  29.4 us (13%)
  between operations  13.6 us (6%)
  local copies, waits for them, and re-layouts  6.69 us (3%)
  other arithmetic  3.57 us (2%)
    ppermute x12, waiting for transfers between devices, send(): lax.ppermute(block, 'seq', [(s, s ^ 2 ** bit) for s in range(n_seq) if wa...  58.2 us
    pallas_call x4, Pallas kernels, near_part(): pl.pallas_call(functools.partial(near_kernel, first, levels), out_shape=(...  34.2 us
    pallas_call x4, Pallas kernels, project(): pl.pallas_call(functools.partial(project_kernel, bool(more)), out_shape=j...  28.7 us
    pallas_call x4, Pallas kernels, far_part(): pl.pallas_call(functools.partial(far_kernel, first, levels, skip, last, l...  26.3 us
    ppermute x12, starting transfers between devices, send(): lax.ppermute(block, 'seq', [(s, s ^ 2 ** bit) for s in range(n_seq) if wa...  22.9 us
    pallas_call x2, Pallas kernels, own_state(): pl.pallas_call(state_kernel, out_shape=jax.ShapeDtypeStruct((heads, ROWS,...  9.55 us
    pallas_call x10, Pallas kernels, merged(): pl.pallas_call(functools.partial(merge_kernel, bit), out_shape=jax.ShapeD...  8.88 us
    unnamed x36, local copies, waits for them, and re-layouts  6.69 us
  transfers between devices with their start and end apart: 14, of which 9 were waited for; matrix products, arithmetic and copies ran while one was open for 0% of the time, Pallas kernels for 42%

profile of v2, /device:TPU:1, one launch (start us, length us, event | category | flops | bytes accessed | tf_op | source)
XLA Modules:
  0.0 225.5 jit_solution(2277795973776464155)
XLA Ops:
  8.0 4.8 %own_state.2.refs_0_.mine_ref = f32[8,136,128]{2,1,0:T(8,128)S(1)} custom-call(f32[512,2048]{1,0:T(8,128)} %k_ref.11, f32[512,2048]{1,0:T(8,128)} %v_ref.11, f32[16,512]{1,0:T(8,128)S(1)} %copy-done.14), custom_call_target="tpu_custom_call" | custom-call | flops 536870912 | bytes 4194304 | tf_op jit(solution)/shard_map/own_state/pallas_call | solution.py:88
  12.8 2.2 collective-permute-start
  15.6 8.5 %near.4 = (f32[512,2048]{1,0:T(8,128)}, f32[8,128]{1,0:T(8,128)S(1)}) custom-call(f32[512,2048]{1,0:T(8,128)} %q_ref.15, f32[512,2048]{1,0:T(8,128)} %k_ref.11, f32[512,2048]{1,0:T(8,128)} %v_ref.11, f32[16,1,512]{2,1,0:T(1,128)S(1)} %get-tuple-element.25.sums_ref, f32[512,128]{1,0:T(8,128)S(1)} %get-tuple-element.26.cols_ref, ...), custom_call_target="tpu_custom_call" | custom-call | flops 2013265920 | bytes 4194304 | tf_op jit(solution)/shard_map/near/pallas_call | solution.py:240
  24.1 3.1 %collective-permute-done.other_ref.refs_0_ = f32[8,136,128]{2,1,0:T(8,128)S(1)} collective-permute-done((f32[8,136,128]{2,1,0:T(8,128)S(1)}, f32[8,136,128]{2,1,0:T(8,128)S(1)}, u32[]{:S(2)}, u32[]{:S(2)}) %collective-permute-start) | collective-permute-done | bytes 557088 | tf_op jit(solution)/shard_map/ppermute | solution.py:395
  27.9 3.6 %collective-permute-start.1 = (f32[8,136,128]{2,1,0:T(8,128)S(1)}, f32[8,136,128]{2,1,0:T(8,128)S(1)}, u32[]{:S(2)}, u32[]{:S(2)}) collective-permute-start(f32[8,136,128]{2,1,0:T(8,128)S(1)} %merge.10.refs_1_.mine_ref), channel_id=1, source_target_pairs={{0,4},{2,6},{4,0},{6,2},{8,12},{10,14},{12,8},{14,10},{16,20},{18,... | collective-permute-start | bytes 1671176 | tf_op jit(solution)/shard_map/ppermute | solution.py:395
  31.5 8.6 %near.5 = (f32[512,2048]{1,0:T(8,128)}, f32[8,128]{1,0:T(8,128)S(1)}) custom-call(f32[512,2048]{1,0:T(8,128)} %q_ref.15, f32[512,2048]{1,0:T(8,128)} %k_ref.11, f32[512,2048]{1,0:T(8,128)} %v_ref.11, f32[16,1,512]{2,1,0:T(1,128)S(1)} %get-tuple-element.25.sums_ref, f32[512,128]{1,0:T(8,128)S(1)} %get-tuple-element.26.cols_ref, ...), custom_call_target="tpu_custom_call", output_to_operand_aliasing={{0}: (6, {})} | custom-call | flops 2013265920 | bytes 4194304 | tf_op jit(solution)/shard_map/near/pallas_call | solution.py:240
  40.1 5.2 %collective-permute-done.1.other_ref.refs_1_ = f32[8,136,128]{2,1,0:T(8,128)S(1)} collective-permute-done((f32[8,136,128]{2,1,0:T(8,128)S(1)}, f32[8,136,128]{2,1,0:T(8,128)S(1)}, u32[]{:S(2)}, u32[]{:S(2)}) %collective-permute-start.1) | collective-permute-done | bytes 557088 | tf_op jit(solution)/shard_map/ppermute | solution.py:395
  46.7 4.8 %own_state.3.refs_1_.mine_ref = f32[8,136,128]{2,1,0:T(8,128)S(1)} custom-call(f32[512,2048]{1,0:T(8,128)} %k_ref.11, f32[512,2048]{1,0:T(8,128)} %v_ref.11, f32[16,512]{1,0:T(8,128)S(1)} %copy-done.15, f32[8,136,128]{2,1,0:T(8,128)S(1)} %merge.11.refs_0_.mine_ref), custom_call_target="tpu_custom_call" | custom-call | flops 536870912 | bytes 4194304 | tf_op jit(solution)/shard_map/own_state/pallas_call | solution.py:88
  52.8 8.6 %near.6 = (f32[512,2048]{1,0:T(8,128)}, f32[8,128]{1,0:T(8,128)S(1)}) custom-call(f32[512,2048]{1,0:T(8,128)} %q_ref.15, f32[512,2048]{1,0:T(8,128)} %k_ref.11, f32[512,2048]{1,0:T(8,128)} %v_ref.11, f32[16,1,512]{2,1,0:T(1,128)S(1)} %get-tuple-element.25.sums_ref, f32[512,128]{1,0:T(8,128)S(1)} %get-tuple-element.26.cols_ref, ...), custom_call_target="tpu_custom_call", output_to_operand_aliasing={{0}: (6, {})} | custom-call | flops 2013265920 | bytes 4194304 | tf_op jit(solution)/shard_map/near/pallas_call | solution.py:240
  62.0 2.5 %collective-permute-start.5 = (f32[8,136,128]{2,1,0:T(8,128)S(1)}, f32[8,136,128]{2,1,0:T(8,128)S(1)}, u32[]{:S(2)}, u32[]{:S(2)}) collective-permute-start(f32[8,136,128]{2,1,0:T(8,128)S(1)} %merge.12.refs_0_.mine_ref), channel_id=1, source_target_pairs={{0,16},{2,18},{4,20},{6,22},{8,24},{10,26},{12,28},{14,30},{16,0},... | collective-permute-start | bytes 1671176 | tf_op jit(solution)/shard_map/ppermute | solution.py:395
  64.6 8.4 %collective-permute-done.2.other_ref.refs_0_ = f32[8,136,128]{2,1,0:T(8,128)S(1)} collective-permute-done((f32[8,136,128]{2,1,0:T(8,128)S(1)}, f32[8,136,128]{2,1,0:T(8,128)S(1)}, u32[]{:S(2)}, u32[]{:S(2)}) %collective-permute-start.2) | collective-permute-done | bytes 557088 | tf_op jit(solution)/shard_map/ppermute | solution.py:395
  73.9 8.6 %near.7 = (f32[512,2048]{1,0:T(8,128)}, f32[8,128]{1,0:T(8,128)S(1)}) custom-call(f32[512,2048]{1,0:T(8,128)} %q_ref.15, f32[512,2048]{1,0:T(8,128)} %k_ref.11, f32[512,2048]{1,0:T(8,128)} %v_ref.11, f32[16,1,512]{2,1,0:T(1,128)S(1)} %get-tuple-element.25.sums_ref, f32[512,128]{1,0:T(8,128)S(1)} %get-tuple-element.26.cols_ref, ...), custom_call_target="tpu_custom_call", output_to_operand_aliasing={{0}: (6, {})} | custom-call | flops 2013265920 | bytes 4194304 | tf_op jit(solution)/shard_map/near/pallas_call | solution.py:240
  84.0 4.1 %collective-permute-start.7 = (f32[8,136,128]{2,1,0:T(8,128)S(1)}, f32[8,136,128]{2,1,0:T(8,128)S(1)}, u32[]{:S(2)}, u32[]{:S(2)}) collective-permute-start(f32[8,136,128]{2,1,0:T(8,128)S(1)} %merge.14.refs_0_.mine_ref), channel_id=1, source_target_pairs={{0,32},{2,34},{4,36},{6,38},{8,40},{10,42},{12,44},{14,46},{16,48}... | collective-permute-start | bytes 1671176 | tf_op jit(solution)/shard_map/ppermute | solution.py:395
  89.6 6.5 %far.4 = (f32[512,1024]{1,0:T(8,128)}, f32[8,128]{1,0:T(8,128)S(1)}) custom-call(s32[6]{0:T(128)S(1)} %shift-right-arithmetic_and_fusion.upper_ref, f32[512,2048]{1,0:T(8,128)} %q_ref.15, f32[512,2048]{1,0:T(8,128)} %get-tuple-element.34.near_ref, f32[512,256]{1,0:T(8,128)S(1)} %get-tuple-element.27.w_ref, f32[1,2048]{1,0:T(1,128)S(1)} %bitcast.4, ...), custom_call_target="tpu_custom_call" | custom-call | flops 2147483648 | bytes 8388608 | tf_op jit(solution)/shard_map/far/pallas_call | solution.py:312
  96.1 3.7 %collective-permute-done.7.other_ref.refs_4_ = f32[8,136,128]{2,1,0:T(8,128)S(1)} collective-permute-done((f32[8,136,128]{2,1,0:T(8,128)S(1)}, f32[8,136,128]{2,1,0:T(8,128)S(1)}, u32[]{:S(2)}, u32[]{:S(2)}) %collective-permute-start.7) | collective-permute-done | bytes 557088 | tf_op jit(solution)/shard_map/ppermute | solution.py:395
  99.8 1.5 merge.16.refs_0_
  101.3 4.4 %collective-permute-done.6.other_ref.refs_2_ = f32[8,136,128]{2,1,0:T(8,128)S(1)} collective-permute-done((f32[8,136,128]{2,1,0:T(8,128)S(1)}, f32[8,136,128]{2,1,0:T(8,128)S(1)}, u32[]{:S(2)}, u32[]{:S(2)}) %collective-permute-start.6) | collective-permute-done | bytes 557088 | tf_op jit(solution)/shard_map/ppermute | solution.py:395
  107.5 4.6 %collective-permute-start.9 = (f32[8,136,128]{2,1,0:T(8,128)}, f32[8,136,128]{2,1,0:T(8,128)}, u32[]{:S(2)}, u32[]{:S(2)}) collective-permute-start(f32[8,136,128]{2,1,0:T(8,128)} %merge.16.refs_0_), channel_id=1, source_target_pairs={{0,64},{2,66},{4,68},{6,70},{8,72},{10,74},{12,76},{14,78},{16,80}... | collective-permute-start | bytes 1671176 | tf_op jit(solution)/shard_map/ppermute | solution.py:395
  112.1 21.2 %collective-permute-done.8.other_ref.refs_3_ = f32[8,136,128]{2,1,0:T(8,128)S(1)} collective-permute-done((f32[8,136,128]{2,1,0:T(8,128)S(1)}, f32[8,136,128]{2,1,0:T(8,128)S(1)}, u32[]{:S(2)}, u32[]{:S(2)}) %collective-permute-start.8) | collective-permute-done | bytes 557088 | tf_op jit(solution)/shard_map/ppermute | solution.py:395
  133.3 1.5 merge.18.refs_6_.mine_ref
  134.7 1.9 collective-permute-start.10
  137.7 6.9 %far.5 = (bf16[512,1024]{1,0:T(8,128)(2,1)}, bf16[512,1024]{1,0:T(8,128)(2,1)}, f32[8,128]{1,0:T(8,128)S(1)}) custom-call(s32[6]{0:T(128)S(1)} %shift-right-arithmetic_and_fusion.upper_ref, f32[512,2048]{1,0:T(8,128)} %q_ref.15, f32[512,1024]{1,0:T(8,128)} %get-tuple-element.37.near_ref, f32[512,256]{1,0:T(8,128)S(1)} %get-tuple-element.27.w_ref, ...), custom_call_target="tpu_custom_call" | custom-call | flops 3221225472 | bytes 8388608 | tf_op jit(solution)/shard_map/far/pallas_call | solution.py:312
  144.7 6.1 %far.6 = (f32[512,1024]{1,0:T(8,128)}, f32[8,128]{1,0:T(8,128)S(1)}) custom-call(s32[6]{0:T(128)S(1)} %shift-right-arithmetic_and_fusion.upper_ref, f32[512,2048]{1,0:T(8,128)} %q_ref.15, f32[512,2048]{1,0:T(8,128)} %get-tuple-element.34.near_ref, f32[512,256]{1,0:T(8,128)S(1)} %get-tuple-element.27.w_ref, f32[1,2048]{1,0:T(1,128)S(1)} %bitcast.6, ...), custom_call_target="tpu_custom_call" | custom-call | flops 2147483648 | bytes 8388608 | tf_op jit(solution)/shard_map/far/pallas_call | solution.py:312
  150.7 11.3 %collective-permute-done.10.other_ref.refs_4_ = f32[8,136,128]{2,1,0:T(8,128)} collective-permute-done((f32[8,136,128]{2,1,0:T(8,128)}, f32[8,136,128]{2,1,0:T(8,128)}, u32[]{:S(2)}, u32[]{:S(2)}) %collective-permute-start.10) | collective-permute-done | bytes 557088 | tf_op jit(solution)/shard_map/ppermute | solution.py:395
  164.7 5.0 %all-gather.2.cloned.1.call-done.w_ref = f32[2048,2048]{1,0:T(8,128)} async-done(((f32[32,2048]{1,0:T(8,128)}), f32[2048,2048]{1,0:T(8,128)}) %all-gather.2.cloned.1.call-update) | async-done | bytes 16777232 | tf_op jit(solution)/shard_map/all_gather | solution.py:386
  170.9 7.0 %project.5.refs_7_.refs_0_ = f32[512,1024]{1,0:T(8,128)} custom-call(s32[1]{0:T(128)} %bitcast.side_ref, bf16[512,1024]{1,0:T(8,128)(2,1)S(1)} %copy-done.4, bf16[512,1024]{1,0:T(8,128)(2,1)} %get-tuple-element.42.lo_ref, f32[2048,2048]{1,0:T(8,128)} %all-gather.2.cloned.1.call-done.w_ref, f32[8,136,128]{2,1,0:T(8,128)S(1)} %merge.19.refs_0_), custom_call_target="tpu_custom_call" | custom-call | flops 3221225472 | bytes 8388608 | tf_op jit(solution)/shard_map/project/pallas_call | solution.py:356
  178.0 7.0 %project.4.refs_6_.refs_0_ = f32[512,1024]{1,0:T(8,128)} custom-call(s32[1]{0:T(128)} %bitcast.2.side_ref, bf16[512,1024]{1,0:T(8,128)(2,1)S(1)} %copy-done.4, bf16[512,1024]{1,0:T(8,128)(2,1)} %get-tuple-element.42.lo_ref, f32[2048,2048]{1,0:T(8,128)} %all-gather.2.cloned.1.call-done.w_ref, f32[8,136,128]{2,1,0:T(8,128)S(1)} %merge.19.refs_0_), custom_call_target="tpu_custom_call" | custom-call | flops 3221225472 | bytes 8388608 | tf_op jit(solution)/shard_map/project/pallas_call | solution.py:356
  185.8 6.9 %far.7 = (bf16[512,1024]{1,0:T(8,128)(2,1)}, bf16[512,1024]{1,0:T(8,128)(2,1)}, f32[8,128]{1,0:T(8,128)}) custom-call(s32[6]{0:T(128)S(1)} %shift-right-arithmetic_and_fusion.upper_ref, f32[512,2048]{1,0:T(8,128)} %q_ref.15, f32[512,1024]{1,0:T(8,128)} %get-tuple-element.39.near_ref, f32[512,256]{1,0:T(8,128)S(1)} %get-tuple-element.27.w_ref, ...), custom_call_target="tpu_custom_call" | custom-call | flops 3221225472 | bytes 8388608 | tf_op jit(solution)/shard_map/far/pallas_call | solution.py:312
  193.9 7.3 %project.7 = f32[512,1024]{1,0:T(8,128)} custom-call(s32[1]{0:T(128)} %bitcast.2.side_ref, bf16[512,1024]{1,0:T(8,128)(2,1)S(1)} %copy-done.5, bf16[512,1024]{1,0:T(8,128)(2,1)} %get-tuple-element.44.lo_ref, f32[2048,2048]{1,0:T(8,128)} %all-gather.2.cloned.1.call-done.w_ref, f32[512,1024]{1,0:T(8,128)} %project.4.refs_6_.refs_0_), custom_call_target="tpu_custom_call" | custom-call | flops 3221225472 | bytes 8388608 | tf_op jit(solution)/shard_map/project/pallas_call | solution.py:356
  201.2 6.5 %collective-permute-start.12 = (f32[512,1024]{1,0:T(8,128)}, f32[512,1024]{1,0:T(8,128)S(1)}, u32[]{:S(2)}, u32[]{:S(2)}) collective-permute-start(f32[512,1024]{1,0:T(8,128)} %project.7), channel_id=1, source_target_pairs={{0,1},{1,0},{2,3},{3,2},{4,5},{5,4},{6,7},{7,6},{8,9},{9,8},{10,11... | collective-permute-start | bytes 6291464 | tf_op jit(solution)/shard_map/ppermute | solution.py:447
  207.7 7.3 %project.6 = f32[512,1024]{1,0:T(8,128)} custom-call(s32[1]{0:T(128)} %bitcast.side_ref, bf16[512,1024]{1,0:T(8,128)(2,1)S(1)} %copy-done.5, bf16[512,1024]{1,0:T(8,128)(2,1)} %get-tuple-element.44.lo_ref, f32[2048,2048]{1,0:T(8,128)} %all-gather.2.cloned.1.call-done.w_ref, f32[512,1024]{1,0:T(8,128)} %project.5.refs_7_.refs_0_), custom_call_target="tpu_custom_call" | custom-call | flops 3221225472 | bytes 8388608 | tf_op jit(solution)/shard_map/project/pallas_call | solution.py:356
  215.1 3.6 %add.3 = f32[512,1024]{1,0:T(8,128)} add(f32[512,1024]{1,0:T(8,128)} %project.6, f32[512,1024]{1,0:T(8,128)S(1)} %collective-permute-done.12) | non-fusion elementwise | flops 524288 | bytes 6291456 | tf_op jit(solution)/shard_map/add | solution.py:449
  (60 shorter events, 18.8 us)
Async XLA Ops:
  6.5 163.2 %all-gather.2.cloned.1.call-start = ((), (), s32[]{:S(2)}) async-start(), calls=%async_computation | async-start | bytes 17039360 | tf_op jit(solution)/shard_map/all_gather | solution.py:386
  7.3 0.8 copy-start.14
  8.0 7.0 %copy-start.13 = (f32[16,16,512]{2,1,0:T(8,128)S(1)}, f32[16,16,512]{2,1,0:T(8,128)}, u32[]{:S(2)}) copy-start(f32[16,16,512]{2,1,0:T(8,128)} %w_ref.1) | copy-start | bytes 1572868
  8.0 7.0 %copy-start.15 = (f32[16,512]{1,0:T(8,128)S(1)}, f32[16,512]{1,0:T(8,128)}, u32[]{:S(2)}) copy-start(f32[16,512]{1,0:T(8,128)} %ld_ref.5) | copy-start | bytes 98308
  12.8 14.4 %collective-permute-start = (f32[8,136,128]{2,1,0:T(8,128)S(1)}, f32[8,136,128]{2,1,0:T(8,128)S(1)}, u32[]{:S(2)}, u32[]{:S(2)}) collective-permute-start(f32[8,136,128]{2,1,0:T(8,128)S(1)} %own_state.2.refs_0_.mine_ref), channel_id=1, source_target_pairs={{0,2},{2,0},{4,6},{6,4},{8,10},{10,8},{12,14},{14,12},{16,18},{18,... | collective-permute-start | bytes 1671176 | tf_op jit(solution)/shard_map/ppermute | solution.py:395
  27.3 12.8 %copy-start.6 = (f32[8,136,128]{2,1,0:T(8,128)}, f32[8,136,128]{2,1,0:T(8,128)S(1)}, u32[]{:S(2)}) copy-start(f32[8,136,128]{2,1,0:T(8,128)S(1)} %collective-permute-done.other_ref.refs_0_) | copy-start | bytes 1671172
  27.9 17.3 %collective-permute-start.1 = (f32[8,136,128]{2,1,0:T(8,128)S(1)}, f32[8,136,128]{2,1,0:T(8,128)S(1)}, u32[]{:S(2)}, u32[]{:S(2)}) collective-permute-start(f32[8,136,128]{2,1,0:T(8,128)S(1)} %merge.10.refs_1_.mine_ref), channel_id=1, source_target_pairs={{0,4},{2,6},{4,0},{6,2},{8,12},{10,14},{12,8},{14,10},{16,20},{18,... | collective-permute-start | bytes 1671176 | tf_op jit(solution)/shard_map/ppermute | solution.py:395
  45.3 43.8 %copy-start.8 = (f32[8,136,128]{2,1,0:T(8,128)}, f32[8,136,128]{2,1,0:T(8,128)S(1)}, u32[]{:S(2)}) copy-start(f32[8,136,128]{2,1,0:T(8,128)S(1)} %collective-permute-done.1.other_ref.refs_1_) | copy-start | bytes 1671172
  45.9 15.4 %collective-permute-start.3 = (f32[8,136,128]{2,1,0:T(8,128)S(1)}, f32[8,136,128]{2,1,0:T(8,128)S(1)}, u32[]{:S(2)}, u32[]{:S(2)}) collective-permute-start(f32[8,136,128]{2,1,0:T(8,128)S(1)} %merge.11.refs_0_.mine_ref), channel_id=1, source_target_pairs={{0,8},{2,10},{4,12},{6,14},{8,0},{10,2},{12,4},{14,6},{16,24},{18,... | collective-permute-start | bytes 1671176 | tf_op jit(solution)/shard_map/ppermute | solution.py:395
  51.5 21.5 %collective-permute-start.2 = (f32[8,136,128]{2,1,0:T(8,128)S(1)}, f32[8,136,128]{2,1,0:T(8,128)S(1)}, u32[]{:S(2)}, u32[]{:S(2)}) collective-permute-start(f32[8,136,128]{2,1,0:T(8,128)S(1)} %own_state.3.refs_1_.mine_ref), channel_id=1, source_target_pairs={{0,2},{2,0},{4,6},{6,4},{8,10},{10,8},{12,14},{14,12},{16,18},{18,... | collective-permute-start | bytes 1671176 | tf_op jit(solution)/shard_map/ppermute | solution.py:395
  61.4 21.1 %copy-start.10 = (f32[8,136,128]{2,1,0:T(8,128)}, f32[8,136,128]{2,1,0:T(8,128)S(1)}, u32[]{:S(2)}) copy-start(f32[8,136,128]{2,1,0:T(8,128)S(1)} %collective-permute-done.3.other_ref.refs_2_) | copy-start | bytes 1671172
  62.0 21.3 %collective-permute-start.5 = (f32[8,136,128]{2,1,0:T(8,128)S(1)}, f32[8,136,128]{2,1,0:T(8,128)S(1)}, u32[]{:S(2)}, u32[]{:S(2)}) collective-permute-start(f32[8,136,128]{2,1,0:T(8,128)S(1)} %merge.12.refs_0_.mine_ref), channel_id=1, source_target_pairs={{0,16},{2,18},{4,20},{6,22},{8,24},{10,26},{12,28},{14,30},{16,0},... | collective-permute-start | bytes 1671176 | tf_op jit(solution)/shard_map/ppermute | solution.py:395
  73.7 14.5 %collective-permute-start.4 = (f32[8,136,128]{2,1,0:T(8,128)S(1)}, f32[8,136,128]{2,1,0:T(8,128)S(1)}, u32[]{:S(2)}, u32[]{:S(2)}) collective-permute-start(f32[8,136,128]{2,1,0:T(8,128)S(1)} %merge.13.refs_1_.mine_ref), channel_id=1, source_target_pairs={{0,4},{2,6},{4,0},{6,2},{8,12},{10,14},{12,8},{14,10},{16,20},{18,... | collective-permute-start | bytes 1671176 | tf_op jit(solution)/shard_map/ppermute | solution.py:395
  73.9 15.8 %copy-start.16 = (f32[2048]{0:T(1024)S(1)}, f32[2048]{0:T(1024)}, u32[]{:S(2)}) copy-start(f32[2048]{0:T(1024)} %param.12) | copy-start | bytes 24580
  82.4 7.2 %copy-start.7 = (f32[8,136,128]{2,1,0:T(8,128)S(1)}, f32[8,136,128]{2,1,0:T(8,128)}, u32[]{:S(2)}) copy-start(f32[8,136,128]{2,1,0:T(8,128)} %copy-done.6) | copy-start | bytes 1671172
  83.4 5.7 %copy-start.11 = (f32[8,136,128]{2,1,0:T(8,128)}, f32[8,136,128]{2,1,0:T(8,128)S(1)}, u32[]{:S(2)}) copy-start(f32[8,136,128]{2,1,0:T(8,128)S(1)} %collective-permute-done.5.other_ref.refs_3_) | copy-start | bytes 1671172
  84.0 15.8 %collective-permute-start.7 = (f32[8,136,128]{2,1,0:T(8,128)S(1)}, f32[8,136,128]{2,1,0:T(8,128)S(1)}, u32[]{:S(2)}, u32[]{:S(2)}) collective-permute-start(f32[8,136,128]{2,1,0:T(8,128)S(1)} %merge.14.refs_0_.mine_ref), channel_id=1, source_target_pairs={{0,32},{2,34},{4,36},{6,38},{8,40},{10,42},{12,44},{14,46},{16,48}... | collective-permute-start | bytes 1671176 | tf_op jit(solution)/shard_map/ppermute | solution.py:395
  88.8 0.8 copy-start
  88.8 16.9 %collective-permute-start.6 = (f32[8,136,128]{2,1,0:T(8,128)S(1)}, f32[8,136,128]{2,1,0:T(8,128)S(1)}, u32[]{:S(2)}, u32[]{:S(2)}) collective-permute-start(f32[8,136,128]{2,1,0:T(8,128)S(1)} %merge.15.refs_4_.mine_ref), channel_id=1, source_target_pairs={{0,8},{2,10},{4,12},{6,14},{8,0},{10,2},{12,4},{14,6},{16,24},{18,... | collective-permute-start | bytes 1671176 | tf_op jit(solution)/shard_map/ppermute | solution.py:395
  99.8 34.9 %copy-start.12 = (f32[8,136,128]{2,1,0:T(8,128)}, f32[8,136,128]{2,1,0:T(8,128)S(1)}, u32[]{:S(2)}) copy-start(f32[8,136,128]{2,1,0:T(8,128)S(1)} %collective-permute-done.7.other_ref.refs_4_) | copy-start | bytes 1671172
  105.7 1.1 copy-start.1
  106.7 37.9 %copy-start.3 = (f32[8,136,128]{2,1,0:T(8,128)}, f32[8,136,128]{2,1,0:T(8,128)S(1)}, u32[]{:S(2)}) copy-start(f32[8,136,128]{2,1,0:T(8,128)S(1)} %collective-permute-done.6.other_ref.refs_2_) | copy-start | bytes 1671172
  107.4 25.8 %collective-permute-start.8 = (f32[8,136,128]{2,1,0:T(8,128)S(1)}, f32[8,136,128]{2,1,0:T(8,128)S(1)}, u32[]{:S(2)}, u32[]{:S(2)}) collective-permute-start(f32[8,136,128]{2,1,0:T(8,128)S(1)} %merge.17.mine_ref), channel_id=1, source_target_pairs={{0,16},{2,18},{4,20},{6,22},{8,24},{10,26},{12,28},{14,30},{16,0},... | collective-permute-start | bytes 1671176 | tf_op jit(solution)/shard_map/ppermute | solution.py:395
  107.5 29.1 %collective-permute-start.9 = (f32[8,136,128]{2,1,0:T(8,128)}, f32[8,136,128]{2,1,0:T(8,128)}, u32[]{:S(2)}, u32[]{:S(2)}) collective-permute-start(f32[8,136,128]{2,1,0:T(8,128)} %merge.16.refs_0_), channel_id=1, source_target_pairs={{0,64},{2,66},{4,68},{6,70},{8,72},{10,74},{12,76},{14,78},{16,80}... | collective-permute-start | bytes 1671176 | tf_op jit(solution)/shard_map/ppermute | solution.py:395
  133.2 11.4 %copy-start.2 = (f32[8,136,128]{2,1,0:T(8,128)}, f32[8,136,128]{2,1,0:T(8,128)S(1)}, u32[]{:S(2)}) copy-start(f32[8,136,128]{2,1,0:T(8,128)S(1)} %collective-permute-done.8.other_ref.refs_3_) | copy-start | bytes 1671172
  134.7 27.3 %collective-permute-start.10 = (f32[8,136,128]{2,1,0:T(8,128)}, f32[8,136,128]{2,1,0:T(8,128)}, u32[]{:S(2)}, u32[]{:S(2)}) collective-permute-start(f32[8,136,128]{2,1,0:T(8,128)} %merge.18.refs_6_.mine_ref), channel_id=1, source_target_pairs={{0,32},{2,34},{4,36},{6,38},{8,40},{10,42},{12,44},{14,46},{16,48}... | collective-permute-start | bytes 1671176 | tf_op jit(solution)/shard_map/ppermute | solution.py:395
  136.7 1.1 copy-start.9
  163.4 21.6 %collective-permute-start.11 = (f32[8,136,128]{2,1,0:T(8,128)S(1)}, f32[8,136,128]{2,1,0:T(8,128)S(1)}, u32[]{:S(2)}, u32[]{:S(2)}) collective-permute-start(f32[8,136,128]{2,1,0:T(8,128)S(1)} %merge.19.refs_0_), channel_id=1, source_target_pairs={{0,64},{2,66},{4,68},{6,70},{8,72},{10,74},{12,76},{14,78},{16,80}... | collective-permute-start | bytes 1671176 | tf_op jit(solution)/shard_map/ppermute | solution.py:395
  169.7 1.2 copy-start.4
  185.0 0.8 copy-start.17
  192.7 1.2 copy-start.5
  201.2 13.8 %collective-permute-start.12 = (f32[512,1024]{1,0:T(8,128)}, f32[512,1024]{1,0:T(8,128)S(1)}, u32[]{:S(2)}, u32[]{:S(2)}) collective-permute-start(f32[512,1024]{1,0:T(8,128)} %project.7), channel_id=1, source_target_pairs={{0,1},{1,0},{2,3},{3,2},{4,5},{5,4},{6,7},{7,6},{8,9},{9,8},{10,11... | collective-permute-start | bytes 6291464 | tf_op jit(solution)/shard_map/ppermute | solution.py:447
Sparse Core Ops, SparseCore 0:
  10.2 159.4 all-gather.1

commit v3 on v2

--- a/solution.py
+++ b/solution.py
@@ -392,7 +392,8 @@
             above = s >> bit
             return not (bit == seq_bits - 1 and above & 1) and not (bit == seq_bits - 2 and above == 3)
 
-        return lax.ppermute(block, "seq", [(s, s ^ 2**bit) for s in range(n_seq) if wanted(s)])
+        flip = 3 << bit - 1 if bit % 2 else 1 << bit
+        return lax.ppermute(block, "seq", [(s, s ^ flip) for s in range(n_seq) if wanted(s)])
 
     small = size // 2
     early = 4
@@ -419,32 +420,32 @@
     sums, cols, weights = prepare(log_decay, level_weights, (a[0],))
     close, token = near(0, None)
     go(a, came_a, token)
-    close, token = near(1, close, a[1])
+    b.append(own_state(keys, values, log_decay, 1, size, (a[1],)))
+    came_b.append(send(b[0], 0))
+    close, token = near(1, close, b[0])
     go(a, came_a, token)
-    b.append(own_state(keys, values, log_decay, 1, size, (a[2],)))
-    came_b.append(send(b[0], 0))
-    close, token = near(2, close, b[0])
+    go(b, came_b, a[2])
+    close, token = near(2, close, b[1])
     go(a, came_a, token)
     go(b, came_b, a[3])
-    close, token = near(3, close, b[1])
+    close, token = near(3, close, b[2])
     go(a, came_a, token)
     go(b, came_b, a[4])
-    far_a, token = far(close, 0, came_a[:early], 0, 0, False, b[2])
+    far_a, token = far(close, 0, came_a[:early], 0, 0, False, b[3])
     go(a, came_a, token)
     go(b, came_b, a[5])
-    go(b, came_b)
-    a_hi, a_lo, token = far(far_a, 0, came_a, 0, early, True, b[4])
-    far_b, token = far(close, size, came_b[:early], 1, 0, False, token)
+    far_b, token = far(close, size, came_b[:early], 1, 0, False, b[4])
     go(b, came_b, token)
+    a_hi, a_lo, _ = far(far_a, 0, came_a, 0, early, True, b[5])
 
     me = lax.axis_index("head").astype(jnp.int32)
     mine = me.reshape(1)
     theirs = (sides - 1 - me).reshape(1)
-    to_send = project(theirs, a_hi, a_lo, weight, 0, sides, None, (b[5],))
-    to_keep = project(mine, a_hi, a_lo, weight, 0, sides, None, (b[5],))
-    b_hi, b_lo, _ = far(far_b, 0, came_b, 1, early, True, to_send, to_keep)
+    to_send = project(theirs, a_hi, a_lo, weight, 0, sides)
+    b_hi, b_lo, token = far(far_b, 0, came_b, 1, early, True, to_send)
     to_send = project(theirs, b_hi, b_lo, weight, 1, sides, to_send)
     came = lax.ppermute(to_send, "head", [(s, sides - 1 - s) for s in range(sides)])
+    to_keep = project(mine, a_hi, a_lo, weight, 0, sides, None, (to_send,))
     to_keep = project(mine, b_hi, b_lo, weight, 1, sides, to_keep)
     return to_keep + came
 

time: 227 us -> 214 us (0.943)
  waiting for transfers between devices: 64 us -> 56.5 us
  starting transfers between devices: 29.4 us -> 25.8 us
    all_gather x1, waiting for transfers between devices: 5.02 us -> 0.01 us  [local(): weight = lax.all_gather(out_weight.T, 'seq', axis=0, tiled=True)]
    ppermute x12, starting transfers between devices: 22.9 us -> 20.2 us  [send(): lax.ppermute(block, 'seq', [(s, s ^ flip) for s in range(n_seq) if wanted...]
    ppermute x12, waiting for transfers between devices: 58.2 us -> 55.7 us  [send(): lax.ppermute(block, 'seq', [(s, s ^ flip) for s in range(n_seq) if wanted...]
    unnamed x36 -> x48, local copies, waits for them, and re-layouts: 6.69 us -> 6.19 us
  transfers between devices with their start and end apart: 14 -> 14, of which waited for: 9 -> 8; matrix products, arithmetic and copies ran while one was open for 0% -> 0% of each run, Pallas kernels for 42% -> 43%
where the time goes in v3:
time: 214 us; the launch traced here: 212 us
  Pallas kernels  107 us (50%)
  waiting for transfers between devices  56.5 us (26%)
  starting transfers between devices  25.8 us (12%)
  between operations  13.7 us (6%)
  local copies, waits for them, and re-layouts  6.19 us (3%)
  other arithmetic  3.57 us (2%)
    ppermute x12, waiting for transfers between devices, send(): lax.ppermute(block, 'seq', [(s, s ^ flip) for s in range(n_seq) if wanted...  55.7 us
    pallas_call x4, Pallas kernels, near_part(): pl.pallas_call(functools.partial(near_kernel, first, levels), out_shape=(...  34.3 us
    pallas_call x4, Pallas kernels, project(): pl.pallas_call(functools.partial(project_kernel, bool(more)), out_shape=j...  28.9 us
    pallas_call x4, Pallas kernels, far_part(): pl.pallas_call(functools.partial(far_kernel, first, levels, skip, last, l...  26.3 us
    ppermute x12, starting transfers between devices, send(): lax.ppermute(block, 'seq', [(s, s ^ flip) for s in range(n_seq) if wanted...  20.2 us
    pallas_call x2, Pallas kernels, own_state(): pl.pallas_call(state_kernel, out_shape=jax.ShapeDtypeStruct((heads, ROWS,...  9.56 us
    pallas_call x10, Pallas kernels, merged(): pl.pallas_call(functools.partial(merge_kernel, bit), out_shape=jax.ShapeD...  7.08 us
    unnamed x48, local copies, waits for them, and re-layouts  6.19 us
  transfers between devices with their start and end apart: 14, of which 8 were waited for; matrix products, arithmetic and copies ran while one was open for 0% of the time, Pallas kernels for 43%

profile of v3, /device:TPU:1, one launch (start us, length us, event | category | flops | bytes accessed | tf_op | source)
XLA Modules:
  0.0 212.5 jit_solution(10829028562205634855)
XLA Ops:
  8.0 4.8 %own_state.2.refs_0_.mine_ref = f32[8,136,128]{2,1,0:T(8,128)S(1)} custom-call(f32[512,2048]{1,0:T(8,128)} %k_ref.11, f32[512,2048]{1,0:T(8,128)} %v_ref.11, f32[16,512]{1,0:T(8,128)S(1)} %copy-done.20), custom_call_target="tpu_custom_call" | custom-call | flops 536870912 | bytes 4194304 | tf_op jit(solution)/shard_map/own_state/pallas_call | solution.py:88
  12.8 2.2 %collective-permute-start = (f32[8,136,128]{2,1,0:T(8,128)S(1)}, f32[8,136,128]{2,1,0:T(8,128)S(1)}, u32[]{:S(2)}, u32[]{:S(2)}) collective-permute-start(f32[8,136,128]{2,1,0:T(8,128)S(1)} %own_state.2.refs_0_.mine_ref), channel_id=1, source_target_pairs={{0,2},{2,0},{4,6},{6,4},{8,10},{10,8},{12,14},{14,12},{16,18},{18,... | collective-permute-start | bytes 1671176 | tf_op jit(solution)/shard_map/ppermute | solution.py:396
  15.6 8.6 %near.4 = (f32[512,2048]{1,0:T(8,128)}, f32[8,128]{1,0:T(8,128)S(1)}) custom-call(f32[512,2048]{1,0:T(8,128)} %q_ref.15, f32[512,2048]{1,0:T(8,128)} %k_ref.11, f32[512,2048]{1,0:T(8,128)} %v_ref.11, f32[16,1,512]{2,1,0:T(1,128)S(1)} %get-tuple-element.24.sums_ref, f32[512,128]{1,0:T(8,128)S(1)} %get-tuple-element.25.cols_ref, ...), custom_call_target="tpu_custom_call" | custom-call | flops 2013265920 | bytes 4194304 | tf_op jit(solution)/shard_map/near/pallas_call | solution.py:240
  24.1 3.1 %collective-permute-done.other_ref.refs_0_ = f32[8,136,128]{2,1,0:T(8,128)S(1)} collective-permute-done((f32[8,136,128]{2,1,0:T(8,128)S(1)}, f32[8,136,128]{2,1,0:T(8,128)S(1)}, u32[]{:S(2)}, u32[]{:S(2)}) %collective-permute-start) | collective-permute-done | bytes 557088 | tf_op jit(solution)/shard_map/ppermute | solution.py:396
  27.9 3.8 %collective-permute-start.2 = (f32[8,136,128]{2,1,0:T(8,128)S(1)}, f32[8,136,128]{2,1,0:T(8,128)S(1)}, u32[]{:S(2)}, u32[]{:S(2)}) collective-permute-start(f32[8,136,128]{2,1,0:T(8,128)S(1)} %merge.10.refs_0_.mine_ref), channel_id=1, source_target_pairs={{0,6},{2,4},{4,2},{6,0},{8,14},{10,12},{12,10},{14,8},{16,22},{18,... | collective-permute-start | bytes 1671176 | tf_op jit(solution)/shard_map/ppermute | solution.py:396
  31.8 4.8 %own_state.3.refs_1_.mine_ref = f32[8,136,128]{2,1,0:T(8,128)S(1)} custom-call(f32[512,2048]{1,0:T(8,128)} %k_ref.11, f32[512,2048]{1,0:T(8,128)} %v_ref.11, f32[16,512]{1,0:T(8,128)S(1)} %copy-done.21, f32[8,136,128]{2,1,0:T(8,128)S(1)} %merge.10.refs_0_.mine_ref), custom_call_target="tpu_custom_call" | custom-call | flops 536870912 | bytes 4194304 | tf_op jit(solution)/shard_map/own_state/pallas_call | solution.py:88
  36.6 8.6 %near.5 = (f32[512,2048]{1,0:T(8,128)}, f32[8,128]{1,0:T(8,128)S(1)}) custom-call(f32[512,2048]{1,0:T(8,128)} %q_ref.15, f32[512,2048]{1,0:T(8,128)} %k_ref.11, f32[512,2048]{1,0:T(8,128)} %v_ref.11, f32[16,1,512]{2,1,0:T(1,128)S(1)} %get-tuple-element.24.sums_ref, f32[512,128]{1,0:T(8,128)S(1)} %get-tuple-element.25.cols_ref, ...), custom_call_target="tpu_custom_call", output_to_operand_aliasing={{0}: (6, {})} | custom-call | flops 2013265920 | bytes 4194304 | tf_op jit(solution)/shard_map/near/pallas_call | solution.py:240
  47.1 3.4 %collective-permute-done.1.other_ref.refs_0_ = f32[8,136,128]{2,1,0:T(8,128)S(1)} collective-permute-done((f32[8,136,128]{2,1,0:T(8,128)S(1)}, f32[8,136,128]{2,1,0:T(8,128)S(1)}, u32[]{:S(2)}, u32[]{:S(2)}) %collective-permute-start.1) | collective-permute-done | bytes 557088 | tf_op jit(solution)/shard_map/ppermute | solution.py:396
  51.3 8.6 %near.6 = (f32[512,2048]{1,0:T(8,128)}, f32[8,128]{1,0:T(8,128)S(1)}) custom-call(f32[512,2048]{1,0:T(8,128)} %q_ref.15, f32[512,2048]{1,0:T(8,128)} %k_ref.11, f32[512,2048]{1,0:T(8,128)} %v_ref.11, f32[16,1,512]{2,1,0:T(1,128)S(1)} %get-tuple-element.24.sums_ref, f32[512,128]{1,0:T(8,128)S(1)} %get-tuple-element.25.cols_ref, ...), custom_call_target="tpu_custom_call", output_to_operand_aliasing={{0}: (6, {})} | custom-call | flops 2013265920 | bytes 4194304 | tf_op jit(solution)/shard_map/near/pallas_call | solution.py:240
  59.9 10.1 %collective-permute-done.4.other_ref.refs_2_ = f32[8,136,128]{2,1,0:T(8,128)S(1)} collective-permute-done((f32[8,136,128]{2,1,0:T(8,128)S(1)}, f32[8,136,128]{2,1,0:T(8,128)S(1)}, u32[]{:S(2)}, u32[]{:S(2)}) %collective-permute-start.4) | collective-permute-done | bytes 557088 | tf_op jit(solution)/shard_map/ppermute | solution.py:396
  70.6 1.7 collective-permute-start.6
  73.3 8.6 %near.7 = (f32[512,2048]{1,0:T(8,128)}, f32[8,128]{1,0:T(8,128)S(1)}) custom-call(f32[512,2048]{1,0:T(8,128)} %q_ref.15, f32[512,2048]{1,0:T(8,128)} %k_ref.11, f32[512,2048]{1,0:T(8,128)} %v_ref.11, f32[16,1,512]{2,1,0:T(1,128)S(1)} %get-tuple-element.24.sums_ref, f32[512,128]{1,0:T(8,128)S(1)} %get-tuple-element.25.cols_ref, ...), custom_call_target="tpu_custom_call", output_to_operand_aliasing={{0}: (6, {})} | custom-call | flops 2013265920 | bytes 4194304 | tf_op jit(solution)/shard_map/near/pallas_call | solution.py:240
  81.9 6.8 %collective-permute-done.6.other_ref.refs_3_ = f32[8,136,128]{2,1,0:T(8,128)S(1)} collective-permute-done((f32[8,136,128]{2,1,0:T(8,128)S(1)}, f32[8,136,128]{2,1,0:T(8,128)S(1)}, u32[]{:S(2)}, u32[]{:S(2)}) %collective-permute-start.6) | collective-permute-done | bytes 557088 | tf_op jit(solution)/shard_map/ppermute | solution.py:396
  89.4 2.7 %collective-permute-start.8 = (f32[8,136,128]{2,1,0:T(8,128)S(1)}, f32[8,136,128]{2,1,0:T(8,128)S(1)}, u32[]{:S(2)}, u32[]{:S(2)}) collective-permute-start(f32[8,136,128]{2,1,0:T(8,128)S(1)} %merge.15.refs_0_.mine_ref), channel_id=1, source_target_pairs={{0,32},{2,34},{4,36},{6,38},{8,40},{10,42},{12,44},{14,46},{16,48}... | collective-permute-start | bytes 1671176 | tf_op jit(solution)/shard_map/ppermute | solution.py:396
  92.8 2.3 %collective-permute-start.7 = (f32[8,136,128]{2,1,0:T(8,128)S(1)}, f32[8,136,128]{2,1,0:T(8,128)S(1)}, u32[]{:S(2)}, u32[]{:S(2)}) collective-permute-start(f32[8,136,128]{2,1,0:T(8,128)S(1)} %merge.16.refs_4_.mine_ref), channel_id=1, source_target_pairs={{0,24},{2,26},{4,28},{6,30},{8,16},{10,18},{12,20},{14,22},{16,8},... | collective-permute-start | bytes 1671176 | tf_op jit(solution)/shard_map/ppermute | solution.py:396
  95.1 6.1 %far.4 = (f32[512,1024]{1,0:T(8,128)}, f32[8,128]{1,0:T(8,128)S(1)}) custom-call(s32[6]{0:T(128)S(1)} %shift-right-arithmetic_and_fusion.upper_ref, f32[512,2048]{1,0:T(8,128)} %q_ref.15, f32[512,2048]{1,0:T(8,128)} %get-tuple-element.33.near_ref, f32[512,256]{1,0:T(8,128)S(1)} %get-tuple-element.26.w_ref, f32[1,2048]{1,0:T(1,128)S(1)} %bitcast.4, ...), custom_call_target="tpu_custom_call" | custom-call | flops 2147483648 | bytes 8388608 | tf_op jit(solution)/shard_map/far/pallas_call | solution.py:312
  101.2 14.8 %collective-permute-done.8.other_ref.refs_4_ = f32[8,136,128]{2,1,0:T(8,128)S(1)} collective-permute-done((f32[8,136,128]{2,1,0:T(8,128)S(1)}, f32[8,136,128]{2,1,0:T(8,128)S(1)}, u32[]{:S(2)}, u32[]{:S(2)}) %collective-permute-start.8) | collective-permute-done | bytes 557088 | tf_op jit(solution)/shard_map/ppermute | solution.py:396
  116.7 2.2 %collective-permute-done.7.other_ref.refs_3_ = f32[8,136,128]{2,1,0:T(8,128)S(1)} collective-permute-done((f32[8,136,128]{2,1,0:T(8,128)S(1)}, f32[8,136,128]{2,1,0:T(8,128)S(1)}, u32[]{:S(2)}, u32[]{:S(2)}) %collective-permute-start.7) | collective-permute-done | bytes 557088 | tf_op jit(solution)/shard_map/ppermute | solution.py:396
  120.6 2.7 %collective-permute-start.9 = (f32[8,136,128]{2,1,0:T(8,128)S(1)}, f32[8,136,128]{2,1,0:T(8,128)}, u32[]{:S(2)}, u32[]{:S(2)}) collective-permute-start(f32[8,136,128]{2,1,0:T(8,128)S(1)} %merge.18.refs_4_.mine_ref), channel_id=1, source_target_pairs={{0,32},{2,34},{4,36},{6,38},{8,40},{10,42},{12,44},{14,46},{16,48}... | collective-permute-start | bytes 1671176 | tf_op jit(solution)/shard_map/ppermute | solution.py:396
  123.3 2.1 collective-permute-start.11
  125.4 6.4 %far.5 = (f32[512,1024]{1,0:T(8,128)}, f32[8,128]{1,0:T(8,128)S(1)}) custom-call(s32[6]{0:T(128)S(1)} %shift-right-arithmetic_and_fusion.upper_ref, f32[512,2048]{1,0:T(8,128)} %q_ref.15, f32[512,2048]{1,0:T(8,128)} %get-tuple-element.33.near_ref, f32[512,256]{1,0:T(8,128)S(1)} %get-tuple-element.26.w_ref, f32[1,2048]{1,0:T(1,128)S(1)} %bitcast.5, ...), custom_call_target="tpu_custom_call" | custom-call | flops 2147483648 | bytes 8388608 | tf_op jit(solution)/shard_map/far/pallas_call | solution.py:312
  131.8 15.0 %collective-permute-done.9.other_ref.refs_4_ = f32[8,136,128]{2,1,0:T(8,128)} collective-permute-done((f32[8,136,128]{2,1,0:T(8,128)S(1)}, f32[8,136,128]{2,1,0:T(8,128)}, u32[]{:S(2)}, u32[]{:S(2)}) %collective-permute-start.9) | collective-permute-done | bytes 557088 | tf_op jit(solution)/shard_map/ppermute | solution.py:396
  149.0 1.3 collective-permute-start.10
  150.4 6.9 %far.6 = (bf16[512,1024]{1,0:T(8,128)(2,1)}, bf16[512,1024]{1,0:T(8,128)(2,1)}, f32[8,128]{1,0:T(8,128)}) custom-call(s32[6]{0:T(128)S(1)} %shift-right-arithmetic_and_fusion.upper_ref, f32[512,2048]{1,0:T(8,128)} %q_ref.15, f32[512,1024]{1,0:T(8,128)} %get-tuple-element.38.near_ref, f32[512,256]{1,0:T(8,128)S(1)} %get-tuple-element.26.w_ref, ...), custom_call_target="tpu_custom_call" | custom-call | flops 3221225472 | bytes 8388608 | tf_op jit(solution)/shard_map/far/pallas_call | solution.py:312
  158.6 7.0 %project.4.refs_6_.refs_0_ = f32[512,1024]{1,0:T(8,128)} custom-call(s32[1]{0:T(128)} %bitcast.2.side_ref, bf16[512,1024]{1,0:T(8,128)(2,1)S(1)} %copy-done.6, bf16[512,1024]{1,0:T(8,128)(2,1)} %get-tuple-element.40.lo_ref, f32[2048,2048]{1,0:T(8,128)} %all-gather.2.cloned.1.call-done.w_ref), custom_call_target="tpu_custom_call" | custom-call | flops 3221225472 | bytes 8388608 | tf_op jit(solution)/shard_map/project/pallas_call | solution.py:356
  166.4 6.9 %far.7 = (bf16[512,1024]{1,0:T(8,128)(2,1)}, bf16[512,1024]{1,0:T(8,128)(2,1)}, f32[8,128]{1,0:T(8,128)}) custom-call(s32[6]{0:T(128)S(1)} %shift-right-arithmetic_and_fusion.upper_ref, f32[512,2048]{1,0:T(8,128)} %q_ref.15, f32[512,1024]{1,0:T(8,128)} %get-tuple-element.36.near_ref, f32[512,256]{1,0:T(8,128)S(1)} %get-tuple-element.26.w_ref, ...), custom_call_target="tpu_custom_call" | custom-call | flops 3221225472 | bytes 8388608 | tf_op jit(solution)/shard_map/far/pallas_call | solution.py:312
  173.3 1.2 copy-done.8
  174.5 7.5 %project.5.refs_0_ = f32[512,1024]{1,0:T(8,128)} custom-call(s32[1]{0:T(128)} %bitcast.2.side_ref, bf16[512,1024]{1,0:T(8,128)(2,1)S(1)} %copy-done.8, bf16[512,1024]{1,0:T(8,128)(2,1)} %get-tuple-element.42.lo_ref, f32[2048,2048]{1,0:T(8,128)} %all-gather.2.cloned.1.call-done.w_ref, f32[512,1024]{1,0:T(8,128)} %project.4.refs_6_.refs_0_), custom_call_target="tpu_custom_call" | custom-call | flops 3221225472 | bytes 8388608 | tf_op jit(solution)/shard_map/project/pallas_call | solution.py:356
  182.0 5.6 %collective-permute-start.12 = (f32[512,1024]{1,0:T(8,128)}, f32[512,1024]{1,0:T(8,128)S(1)}, u32[]{:S(2)}, u32[]{:S(2)}) collective-permute-start(f32[512,1024]{1,0:T(8,128)} %project.5.refs_0_), channel_id=1, source_target_pairs={{0,1},{1,0},{2,3},{3,2},{4,5},{5,4},{6,7},{7,6},{8,9},{9,8},{10,11... | collective-permute-start | bytes 6291464 | tf_op jit(solution)/shard_map/ppermute | solution.py:447
  187.6 7.0 %project.6.refs_0_ = f32[512,1024]{1,0:T(8,128)} custom-call(s32[1]{0:T(128)} %bitcast.side_ref, bf16[512,1024]{1,0:T(8,128)(2,1)S(1)} %copy-done.7, bf16[512,1024]{1,0:T(8,128)(2,1)} %get-tuple-element.40.lo_ref, f32[2048,2048]{1,0:T(8,128)} %all-gather.2.cloned.1.call-done.w_ref, f32[512,1024]{1,0:T(8,128)} %project.5.refs_0_), custom_call_target="tpu_custom_call" | custom-call | flops 3221225472 | bytes 8388608 | tf_op jit(solution)/shard_map/project/pallas_call | solution.py:356
  194.6 7.4 %project.7 = f32[512,1024]{1,0:T(8,128)} custom-call(s32[1]{0:T(128)} %bitcast.side_ref, bf16[512,1024]{1,0:T(8,128)(2,1)S(1)} %copy-done.9, bf16[512,1024]{1,0:T(8,128)(2,1)} %get-tuple-element.42.lo_ref, f32[2048,2048]{1,0:T(8,128)} %all-gather.2.cloned.1.call-done.w_ref, f32[512,1024]{1,0:T(8,128)} %project.6.refs_0_), custom_call_target="tpu_custom_call" | custom-call | flops 3221225472 | bytes 8388608 | tf_op jit(solution)/shard_map/project/pallas_call | solution.py:356
  202.1 3.6 %add.3 = f32[512,1024]{1,0:T(8,128)} add(f32[512,1024]{1,0:T(8,128)} %project.7, f32[512,1024]{1,0:T(8,128)S(1)} %collective-permute-done.12) | non-fusion elementwise | flops 524288 | bytes 6291456 | tf_op jit(solution)/shard_map/add | solution.py:450
  (72 shorter events, 15.1 us)
Async XLA Ops:
  6.5 150.8 %all-gather.2.cloned.1.call-start = ((), (), s32[]{:S(2)}) async-start(), calls=%async_computation | async-start | bytes 17039360 | tf_op jit(solution)/shard_map/all_gather | solution.py:386
  8.0 7.0 %copy-start.19 = (f32[16,16,512]{2,1,0:T(8,128)S(1)}, f32[16,16,512]{2,1,0:T(8,128)}, u32[]{:S(2)}) copy-start(f32[16,16,512]{2,1,0:T(8,128)} %w_ref.1) | copy-start | bytes 1572868
  8.0 7.0 %copy-start.21 = (f32[16,512]{1,0:T(8,128)S(1)}, f32[16,512]{1,0:T(8,128)}, u32[]{:S(2)}) copy-start(f32[16,512]{1,0:T(8,128)} %ld_ref.5) | copy-start | bytes 98308
  12.8 14.4 %collective-permute-start = (f32[8,136,128]{2,1,0:T(8,128)S(1)}, f32[8,136,128]{2,1,0:T(8,128)S(1)}, u32[]{:S(2)}, u32[]{:S(2)}) collective-permute-start(f32[8,136,128]{2,1,0:T(8,128)S(1)} %own_state.2.refs_0_.mine_ref), channel_id=1, source_target_pairs={{0,2},{2,0},{4,6},{6,4},{8,10},{10,8},{12,14},{14,12},{16,18},{18,... | collective-permute-start | bytes 1671176 | tf_op jit(solution)/shard_map/ppermute | solution.py:396
  27.3 4.5 %copy-start.10 = (f32[8,136,128]{2,1,0:T(8,128)}, f32[8,136,128]{2,1,0:T(8,128)S(1)}, u32[]{:S(2)}) copy-start(f32[8,136,128]{2,1,0:T(8,128)S(1)} %collective-permute-done.other_ref.refs_0_) | copy-start | bytes 1671172
  27.9 17.7 %collective-permute-start.2 = (f32[8,136,128]{2,1,0:T(8,128)S(1)}, f32[8,136,128]{2,1,0:T(8,128)S(1)}, u32[]{:S(2)}, u32[]{:S(2)}) collective-permute-start(f32[8,136,128]{2,1,0:T(8,128)S(1)} %merge.10.refs_0_.mine_ref), channel_id=1, source_target_pairs={{0,6},{2,4},{4,2},{6,0},{8,14},{10,12},{12,10},{14,8},{16,22},{18,... | collective-permute-start | bytes 1671176 | tf_op jit(solution)/shard_map/ppermute | solution.py:396
  36.5 14.0 %collective-permute-start.1 = (f32[8,136,128]{2,1,0:T(8,128)S(1)}, f32[8,136,128]{2,1,0:T(8,128)S(1)}, u32[]{:S(2)}, u32[]{:S(2)}) collective-permute-start(f32[8,136,128]{2,1,0:T(8,128)S(1)} %own_state.3.refs_1_.mine_ref), channel_id=1, source_target_pairs={{0,2},{2,0},{4,6},{6,4},{8,10},{10,8},{12,14},{14,12},{16,18},{18,... | collective-permute-start | bytes 1671176 | tf_op jit(solution)/shard_map/ppermute | solution.py:396
  45.6 49.5 %copy-start.13 = (f32[8,136,128]{2,1,0:T(8,128)}, f32[8,136,128]{2,1,0:T(8,128)S(1)}, u32[]{:S(2)}) copy-start(f32[8,136,128]{2,1,0:T(8,128)S(1)} %collective-permute-done.2.other_ref.refs_1_) | copy-start | bytes 1671172
  46.3 23.7 %collective-permute-start.4 = (f32[8,136,128]{2,1,0:T(8,128)S(1)}, f32[8,136,128]{2,1,0:T(8,128)S(1)}, u32[]{:S(2)}, u32[]{:S(2)}) collective-permute-start(f32[8,136,128]{2,1,0:T(8,128)S(1)} %merge.11.refs_0_.mine_ref), channel_id=1, source_target_pairs={{0,8},{2,10},{4,12},{6,14},{8,0},{10,2},{12,4},{14,6},{16,24},{18,... | collective-permute-start | bytes 1671176 | tf_op jit(solution)/shard_map/ppermute | solution.py:396
  51.2 21.1 %collective-permute-start.3 = (f32[8,136,128]{2,1,0:T(8,128)S(1)}, f32[8,136,128]{2,1,0:T(8,128)S(1)}, u32[]{:S(2)}, u32[]{:S(2)}) collective-permute-start(f32[8,136,128]{2,1,0:T(8,128)S(1)} %merge.12.refs_1_.mine_ref), channel_id=1, source_target_pairs={{0,6},{2,4},{4,2},{6,0},{8,14},{10,12},{12,10},{14,8},{16,22},{18,... | collective-permute-start | bytes 1671176 | tf_op jit(solution)/shard_map/ppermute | solution.py:396
  69.9 12.0 %copy-start.15 = (f32[8,136,128]{2,1,0:T(8,128)}, f32[8,136,128]{2,1,0:T(8,128)S(1)}, u32[]{:S(2)}) copy-start(f32[8,136,128]{2,1,0:T(8,128)S(1)} %collective-permute-done.4.other_ref.refs_2_) | copy-start | bytes 1671172
  70.6 18.1 %collective-permute-start.6 = (f32[8,136,128]{2,1,0:T(8,128)S(1)}, f32[8,136,128]{2,1,0:T(8,128)S(1)}, u32[]{:S(2)}, u32[]{:S(2)}) collective-permute-start(f32[8,136,128]{2,1,0:T(8,128)S(1)} %merge.13.refs_0_.mine_ref), channel_id=1, source_target_pairs={{0,24},{2,26},{4,28},{6,30},{8,16},{10,18},{12,20},{14,22},{16,8},... | collective-permute-start | bytes 1671176 | tf_op jit(solution)/shard_map/ppermute | solution.py:396
  72.9 19.2 %collective-permute-start.5 = (f32[8,136,128]{2,1,0:T(8,128)S(1)}, f32[8,136,128]{2,1,0:T(8,128)S(1)}, u32[]{:S(2)}, u32[]{:S(2)}) collective-permute-start(f32[8,136,128]{2,1,0:T(8,128)S(1)} %merge.14.refs_1_.mine_ref), channel_id=1, source_target_pairs={{0,8},{2,10},{4,12},{6,14},{8,0},{10,2},{12,4},{14,6},{16,24},{18,... | collective-permute-start | bytes 1671176 | tf_op jit(solution)/shard_map/ppermute | solution.py:396
  73.3 21.8 %copy-start.22 = (f32[2048]{0:T(1024)S(1)}, f32[2048]{0:T(1024)}, u32[]{:S(2)}) copy-start(f32[2048]{0:T(1024)} %param.12) | copy-start | bytes 24580
  81.9 13.2 %copy-start.11 = (f32[8,136,128]{2,1,0:T(8,128)S(1)}, f32[8,136,128]{2,1,0:T(8,128)}, u32[]{:S(2)}) copy-start(f32[8,136,128]{2,1,0:T(8,128)} %copy-done.10) | copy-start | bytes 1671172
  88.7 6.4 %copy-start.16 = (f32[8,136,128]{2,1,0:T(8,128)}, f32[8,136,128]{2,1,0:T(8,128)S(1)}, u32[]{:S(2)}) copy-start(f32[8,136,128]{2,1,0:T(8,128)S(1)} %collective-permute-done.6.other_ref.refs_3_) | copy-start | bytes 1671172
  89.4 26.7 %collective-permute-start.8 = (f32[8,136,128]{2,1,0:T(8,128)S(1)}, f32[8,136,128]{2,1,0:T(8,128)S(1)}, u32[]{:S(2)}, u32[]{:S(2)}) collective-permute-start(f32[8,136,128]{2,1,0:T(8,128)S(1)} %merge.15.refs_0_.mine_ref), channel_id=1, source_target_pairs={{0,32},{2,34},{4,36},{6,38},{8,40},{10,42},{12,44},{14,46},{16,48}... | collective-permute-start | bytes 1671176 | tf_op jit(solution)/shard_map/ppermute | solution.py:396
  92.1 9.1 %copy-start.4 = (f32[8,136,128]{2,1,0:T(8,128)}, f32[8,136,128]{2,1,0:T(8,128)S(1)}, u32[]{:S(2)}) copy-start(f32[8,136,128]{2,1,0:T(8,128)S(1)} %collective-permute-done.5.other_ref.refs_2_) | copy-start | bytes 1671172
  92.8 2.3 %copy-start.2 = (f32[8,136,128]{2,1,0:T(8,128)}, f32[8,136,128]{2,1,0:T(8,128)S(1)}, u32[]{:S(2)}) copy-start(f32[8,136,128]{2,1,0:T(8,128)S(1)} %merge.16.refs_4_.mine_ref) | copy-start | bytes 1671172
  92.8 26.1 %collective-permute-start.7 = (f32[8,136,128]{2,1,0:T(8,128)S(1)}, f32[8,136,128]{2,1,0:T(8,128)S(1)}, u32[]{:S(2)}, u32[]{:S(2)}) collective-permute-start(f32[8,136,128]{2,1,0:T(8,128)S(1)} %merge.16.refs_4_.mine_ref), channel_id=1, source_target_pairs={{0,24},{2,26},{4,28},{6,30},{8,16},{10,18},{12,20},{14,22},{16,8},... | collective-permute-start | bytes 1671176 | tf_op jit(solution)/shard_map/ppermute | solution.py:396
  116.1 4.5 %copy-start.17 = (f32[8,136,128]{2,1,0:T(8,128)}, f32[8,136,128]{2,1,0:T(8,128)S(1)}, u32[]{:S(2)}) copy-start(f32[8,136,128]{2,1,0:T(8,128)S(1)} %collective-permute-done.8.other_ref.refs_4_) | copy-start | bytes 1671172
  119.9 5.5 %copy-start.5 = (f32[8,136,128]{2,1,0:T(8,128)}, f32[8,136,128]{2,1,0:T(8,128)S(1)}, u32[]{:S(2)}) copy-start(f32[8,136,128]{2,1,0:T(8,128)S(1)} %collective-permute-done.7.other_ref.refs_3_) | copy-start | bytes 1671172
  120.6 4.8 %copy-start = (f32[8,136,128]{2,1,0:T(8,128)}, f32[8,136,128]{2,1,0:T(8,128)S(1)}, u32[]{:S(2)}) copy-start(f32[8,136,128]{2,1,0:T(8,128)S(1)} %merge.18.refs_4_.mine_ref) | copy-start | bytes 1671172
  120.6 26.2 %collective-permute-start.9 = (f32[8,136,128]{2,1,0:T(8,128)S(1)}, f32[8,136,128]{2,1,0:T(8,128)}, u32[]{:S(2)}, u32[]{:S(2)}) collective-permute-start(f32[8,136,128]{2,1,0:T(8,128)S(1)} %merge.18.refs_4_.mine_ref), channel_id=1, source_target_pairs={{0,32},{2,34},{4,36},{6,38},{8,40},{10,42},{12,44},{14,46},{16,48}... | collective-permute-start | bytes 1671176 | tf_op jit(solution)/shard_map/ppermute | solution.py:396
  123.3 27.1 %collective-permute-start.11 = (f32[8,136,128]{2,1,0:T(8,128)S(1)}, f32[8,136,128]{2,1,0:T(8,128)}, u32[]{:S(2)}, u32[]{:S(2)}) collective-permute-start(f32[8,136,128]{2,1,0:T(8,128)S(1)} %merge.17.refs_0_), channel_id=1, source_target_pairs={{0,96},{2,98},{4,100},{6,102},{8,104},{10,106},{12,108},{14,110},{... | collective-permute-start | bytes 1671176 | tf_op jit(solution)/shard_map/ppermute | solution.py:396
  125.4 25.0 %copy-start.12 = (f32[8,136,128]{2,1,0:T(8,128)S(1)}, f32[8,136,128]{2,1,0:T(8,128)}, u32[]{:S(2)}) copy-start(f32[8,136,128]{2,1,0:T(8,128)} %copy-done.10) | copy-start | bytes 1671172
  125.4 25.0 %copy-start.14 = (f32[8,136,128]{2,1,0:T(8,128)S(1)}, f32[8,136,128]{2,1,0:T(8,128)}, u32[]{:S(2)}) copy-start(f32[8,136,128]{2,1,0:T(8,128)} %copy-done.13) | copy-start | bytes 1671172
  149.0 1.4 copy-start.18
  149.0 16.5 %collective-permute-start.10 = (f32[8,136,128]{2,1,0:T(8,128)S(1)}, f32[8,136,128]{2,1,0:T(8,128)S(1)}, u32[]{:S(2)}, u32[]{:S(2)}) collective-permute-start(f32[8,136,128]{2,1,0:T(8,128)S(1)} %merge.19.refs_6_), channel_id=1, source_target_pairs={{0,96},{2,98},{4,100},{6,102},{8,104},{10,106},{12,108},{14,110},{... | collective-permute-start | bytes 1671176 | tf_op jit(solution)/shard_map/ppermute | solution.py:396
  174.5 13.1 %copy-start.7 = (bf16[512,1024]{1,0:T(8,128)(2,1)S(1)}, bf16[512,1024]{1,0:T(8,128)(2,1)}, u32[]{:S(2)}) copy-start(bf16[512,1024]{1,0:T(8,128)(2,1)} %get-tuple-element.39.hi_ref) | copy-start | bytes 3145732
  182.0 20.1 %collective-permute-start.12 = (f32[512,1024]{1,0:T(8,128)}, f32[512,1024]{1,0:T(8,128)S(1)}, u32[]{:S(2)}, u32[]{:S(2)}) collective-permute-start(f32[512,1024]{1,0:T(8,128)} %project.5.refs_0_), channel_id=1, source_target_pairs={{0,1},{1,0},{2,3},{3,2},{4,5},{5,4},{6,7},{7,6},{8,9},{9,8},{10,11... | collective-permute-start | bytes 6291464 | tf_op jit(solution)/shard_map/ppermute | solution.py:447
  187.6 7.0 %copy-start.9 = (bf16[512,1024]{1,0:T(8,128)(2,1)S(1)}, bf16[512,1024]{1,0:T(8,128)(2,1)}, u32[]{:S(2)}) copy-start(bf16[512,1024]{1,0:T(8,128)(2,1)} %get-tuple-element.41.hi_ref) | copy-start | bytes 3145732
  (6 other events, 6.1 us)
Sparse Core Ops, SparseCore 0:
  10.2 136.7 all-gather.1

commit v4 on v3

--- a/solution.py
+++ b/solution.py
@@ -261,117 +261,216 @@
     )(queries, keys, values, sums, cols, weights, *more, *after)
 
 
-def far_kernel(first, levels, skip, last, count, upper_ref, q_ref, near_ref, w_ref, gain_ref, *refs):
+def add_levels(q_hi, q_lo, out, w, first_column, states):
+    parts = []
+    for state in states:
+        hi, lo = split(state)
+        parts.append(jnp.concatenate([hi, hi, lo], axis=0))
+    made = mm(jnp.concatenate([q_hi, q_lo, q_hi], axis=1), jnp.concatenate(parts, axis=1), NN)
+    for n in range(len(parts)):
+        at = first_column + n
+        out = out + w[:, at : at + 1] * made[:, n * DH : (n + 1) * DH]
+    return out
+
+
+def early_kernel(first, levels, count, upper_ref, q_ref, near_ref, w_ref, *refs):
+    out_ref, before_ref = refs[-2:]
     step = q_ref.shape[1] // DH
-    outs = 3 if last else 2
-    out_refs, token_ref = refs[-outs:-1], refs[-1]
     per = CHUNK // levels
     total = upper_ref.shape[0]
     head = first + pl.program_id(0) * step
-    token_ref[...] = jnp.zeros_like(token_ref)
     w = pltpu.roll(w_ref[...], (per - head % per) * levels, 1)
     for h in range(step):
         cols = pl.ds(h * DH, DH)
         q_hi, q_lo = split(q_ref[:, cols] * DH**-0.5)
-        out = near_ref[:, cols]
         before = jnp.zeros((1, DH), F32)
-        used = []
         states = []
         for level in range(count):
-            ref = refs[level]
             upper = upper_ref[level] == 1
-            end = ref.shape[1] - (ROWS - DH)
-            if level >= skip:
-                reach = jnp.where(upper, jnp.exp(before), 0.0)
-                hi, lo = split(ref[h, :DH, :] * reach)
-                states.append(jnp.concatenate([hi, hi, lo], axis=0))
-                used.append(h * levels + levels - total + level)
-            before = before + jnp.where(upper, ref[h, end : end + 1, :], 0.0)
-        made = mm(jnp.concatenate([q_hi, q_lo, q_hi], axis=1), jnp.concatenate(states, axis=1), NN)
-        for n, at in enumerate(used):
-            out = out + w[:, at : at + 1] * made[:, n * DH : (n + 1) * DH]
-        if last:
-            squares = jnp.concatenate(split(out * out), axis=1)
-            mean = mm(squares, jnp.full((2 * DH, DH), 1.0 / DH, BF16), NN)
-            out = out * lax.rsqrt(mean + 1e-06) * gain_ref[:, cols]
-            hi, lo = split(out)
-            out_refs[0][:, cols] = hi
-            out_refs[1][:, cols] = lo
-        else:
-            out_refs[0][:, cols] = out
-
-
-def far_part(upper, queries, so_far, at, weights, levels, gain, states, first, skip, last, after=()):
+            reach = jnp.where(upper, jnp.exp(before), 0.0)
+            states.append(refs[level][h, :DH, :] * reach)
+            before = before + jnp.where(upper, refs[level][h, DH : DH + 1, :], 0.0)
+        out_ref[:, cols] = add_levels(q_hi, q_lo, near_ref[:, cols], w, h * levels + levels - total, states)
+        before_ref[h] = jnp.broadcast_to(before, before_ref.shape[1:])
+
+
+def early_levels(upper, queries, near, weights, levels, states, first, after=()):
     heads = states[0].shape[0]
     tok = queries.shape[0]
     per = CHUNK // levels
     step = 2
-    out = jax.ShapeDtypeStruct((tok, heads * DH), BF16 if last else F32)
-    outs = 2 if last else 1
-    tail = ROWS - DH
-    return pl.pallas_call(
-        functools.partial(far_kernel, first, levels, skip, last, len(states)),
-        out_shape=(out,) * outs + (jax.ShapeDtypeStruct((8, CHUNK), F32),),
+    wide = pl.BlockSpec((tok, step * DH), lambda i: (0, first // step + i))
+    return pl.pallas_call(
+        functools.partial(early_kernel, first, levels, len(states)),
+        out_shape=(
+            jax.ShapeDtypeStruct((tok, heads * DH), F32),
+            jax.ShapeDtypeStruct((heads, 8, DH), F32),
+        ),
         grid=(heads // step,),
         in_specs=[
             SMEM,
-            pl.BlockSpec((tok, step * DH), lambda i: (0, first // step + i)),
-            pl.BlockSpec((tok, step * DH), lambda i: (0, at // step + i)),
+            wide,
+            wide,
             pl.BlockSpec((tok, CHUNK), lambda i: (0, (first + i * step) // per)),
-            pl.BlockSpec((1, step * DH), lambda i: (0, first // step + i)),
         ]
-        + [
-            pl.BlockSpec((step, ROWS, DH), lambda i: (i, 0, 0))
-            if level >= skip
-            else pl.BlockSpec((step, tail, DH), lambda i: (i, DH // tail, 0))
-            for level in range(len(states))
-        ]
+        + [pl.BlockSpec((step, ROWS, DH), lambda i: (i, 0, 0))] * len(states)
         + [ANY] * len(after),
-        out_specs=[pl.BlockSpec((tok, step * DH), lambda i: (0, i))] * outs
-        + [pl.BlockSpec((8, CHUNK), lambda i: (0, 0))],
+        out_specs=[
+            pl.BlockSpec((tok, step * DH), lambda i: (0, i)),
+            pl.BlockSpec((step, 8, DH), lambda i: (i, 0, 0)),
+        ],
         compiler_params=params(),
         cost_estimate=cost(8 * len(states) * tok * heads * DH * DH, 16 * tok * heads * DH),
-        name="far",
-    )(upper, queries, so_far, weights, gain, *states, *after)
-
-
-def project_kernel(has_more, side_ref, hi_ref, lo_ref, w_ref, *refs):
-    out_ref = refs[-1]
-    w_hi, w_lo = split(w_ref[...])
-    x_hi, x_lo = hi_ref[...], lo_ref[...]
-    made = mm(x_hi, w_hi, NT) + (mm(x_hi, w_lo, NT) + mm(x_lo, w_hi, NT))
-    if has_more:
-        made = made + refs[0][...]
-    out_ref[...] = made
-
-
-def project(side, x_hi, x_lo, weight, part, sides, so_far=None, after=()):
+        name="early",
+    )(upper, queries, near, weights, *states, *after)
+
+
+TILE = 256
+
+
+def tile_copy(side, steps, part, j, w_ref, buffer_ref, sems, slot):
+    depth = buffer_ref.shape[2]
+    rows = pl.ds(pl.multiple_of((side * steps + j) * TILE, TILE), TILE)
+    return pltpu.make_async_copy(
+        w_ref.at[rows, pl.ds(part * depth, depth)], buffer_ref.at[slot], sems.at[slot]
+    )
+
+
+def project_tiles(side, steps, part, w_ref, buffer_ref, sems, slot, x_hi, x_lo, more_ref, out_ref):
+    @pl.loop(0, steps)
+    def _(j):
+        tile_copy(side, steps, part, j, w_ref, buffer_ref, sems, slot + j).wait()
+        w_hi, w_lo = split(buffer_ref[slot + j])
+        cols = pl.ds(pl.multiple_of(j * TILE, TILE), TILE)
+        made = mm(x_hi[...], w_hi, NT) + (mm(x_hi[...], w_lo, NT) + mm(x_lo[...], w_hi, NT))
+        if more_ref is not None:
+            made = made + more_ref[:, cols]
+        out_ref[:, cols] = made
+
+
+def finish_kernel(first, levels, skip, both, more, sides_ref, upper_ref, q_ref, near_ref, before_ref, *refs):
+    w_ref, gain_ref, *refs = refs
+    total = upper_ref.shape[0]
+    states, weight_ref, refs = refs[: total - skip], refs[total - skip], refs[total - skip + 1 :]
+    more_ref = refs[0] if more else None
+    send_ref, second, third, buffer_ref, sems, q_buffer, q_sems = refs[-7:]
+    x_hi, x_lo = (refs[-9:-7]) if both else (second, third)
+    heads = states[0].shape[0]
+    steps = send_ref.shape[1] // TILE
+    part = first // heads
+    pair = 2
+
+    def q_copy(n):
+        cols = pl.ds(pl.multiple_of((first + n * pair) * DH, pair * DH), pair * DH)
+        return pltpu.make_async_copy(q_ref.at[:, cols], q_buffer.at[n], q_sems.at[n])
+
+    for n in range(heads // pair):
+        q_copy(n).start()
+    used = 2 if both else 1
+    for side in range(used):
+        for j in range(steps):
+            tile_copy(sides_ref[side], steps, part, j, weight_ref, buffer_ref, sems, side * steps + j).start()
+
+    per = CHUNK // levels
+
+    @pl.loop(0, heads // pair)
+    def _(n):
+        q_copy(n).wait()
+        group = pl.multiple_of((first + n * pair) // per * CHUNK, CHUNK)
+        w = pltpu.roll(w_ref[:, pl.ds(group, CHUNK)], (per - (first + n * pair) % per) * levels, 1)
+        for i in range(pair):
+            h = n * pair + i
+            cols = pl.ds(pl.multiple_of(h * DH, DH), DH)
+            all_cols = pl.ds(pl.multiple_of((first + h) * DH, DH), DH)
+            q_hi, q_lo = split(q_buffer[n, :, i * DH : (i + 1) * DH] * DH**-0.5)
+            before = before_ref[h, 0:1, :]
+            scaled = []
+            for m, ref in enumerate(states):
+                upper = upper_ref[skip + m] == 1
+                scaled.append(ref[h, :DH, :] * jnp.where(upper, jnp.exp(before), 0.0))
+                before = before + jnp.where(upper, ref[h, DH : DH + 1, :], 0.0)
+            column = i * levels + levels - total + skip
+            out = add_levels(q_hi, q_lo, near_ref[:, cols], w, column, scaled)
+            squares = jnp.concatenate(split(out * out), axis=1)
+            mean = mm(squares, jnp.full((2 * DH, DH), 1.0 / DH, BF16), NN)
+            out = out * lax.rsqrt(mean + 1e-06) * gain_ref[:, all_cols]
+            hi, lo = split(out)
+            x_hi[:, cols] = hi
+            x_lo[:, cols] = lo
+
+    project_tiles(
+        sides_ref[0], steps, part, weight_ref, buffer_ref, sems, 0, x_hi, x_lo, more_ref, send_ref
+    )
+    if both:
+        project_tiles(
+            sides_ref[1], steps, part, weight_ref, buffer_ref, sems, steps, x_hi, x_lo, None, second
+        )
+
+
+def finish(sides, upper, queries, near, before, weights, levels, gain, states, weight, first, both, more=None):
+    heads = states[0].shape[0]
+    tok = queries.shape[0]
+    width = weight.shape[0] // 2
+    depth = heads * DH
+    skip = upper.shape[0] - len(states)
+    used = 2 if both else 1
+    tiles = used * width // TILE
+    sums = jax.ShapeDtypeStruct((tok, width), F32)
+    half = jax.ShapeDtypeStruct((tok, depth), BF16)
+    extra = [] if more is None else [more]
+    kept = [pltpu.VMEM((tok, depth), BF16)] * 2 if both else []
+    third = [] if both else [half]
+
+    def body(*refs):
+        if both:
+            ins = refs[: 8 + len(states) + len(extra)]
+            send, keep, hi, lo, *scratch = refs[len(ins) :]
+            finish_kernel(first, levels, skip, both, bool(extra), *ins, hi, lo, send, keep, None, *scratch)
+        else:
+            finish_kernel(first, levels, skip, both, bool(extra), *refs)
+
+    return pl.pallas_call(
+        body,
+        out_shape=[sums] + ([sums] if both else [half]) + third,
+        in_specs=[SMEM, SMEM, ANY] + [VMEM] * (4 + len(states)) + [ANY] + [VMEM] * len(extra),
+        out_specs=[VMEM] * (2 + len(third)),
+        scratch_shapes=kept
+        + [
+            pltpu.VMEM((tiles, TILE, depth), F32),
+            pltpu.SemaphoreType.DMA((tiles,)),
+            pltpu.VMEM((heads // 2, tok, 2 * DH), F32),
+            pltpu.SemaphoreType.DMA((heads // 2,)),
+        ],
+        compiler_params=params(44),
+        cost_estimate=cost(6 * tok * depth * width * used, 4 * depth * width * used + 16 * tok * depth),
+        name="finish",
+    )(sides, upper, queries, near, before, weights, gain, *states, weight, *extra)
+
+
+def project_kernel(part, sides_ref, x_hi, x_lo, weight_ref, more_ref, *refs):
+    out_ref, buffer_ref, sems = refs[-3:]
+    steps = out_ref.shape[1] // TILE
+    for j in range(steps):
+        tile_copy(sides_ref[1], steps, part, j, weight_ref, buffer_ref, sems, j).start()
+    project_tiles(sides_ref[1], steps, part, weight_ref, buffer_ref, sems, 0, x_hi, x_lo, more_ref, out_ref)
+
+
+def project(sides, x_hi, x_lo, weight, part, more, after=()):
     tok, depth = x_hi.shape
-    width = weight.shape[0] // sides
-    tile = 256
-    steps = width // tile
-    whole = pl.BlockSpec((tok, depth), lambda i, side: (0, 0))
-    moving = pl.BlockSpec((tok, tile), lambda i, side: (0, i))
-    more = [] if so_far is None else [so_far]
-    return pl.pallas_call(
-        functools.partial(project_kernel, bool(more)),
+    width = weight.shape[0] // 2
+    return pl.pallas_call(
+        functools.partial(project_kernel, part),
         out_shape=jax.ShapeDtypeStruct((tok, width), F32),
-        grid_spec=pltpu.PrefetchScalarGridSpec(
-            num_scalar_prefetch=1,
-            grid=(steps,),
-            in_specs=[
-                whole,
-                whole,
-                pl.BlockSpec((tile, depth), lambda i, side: (side[0] * steps + i, part)),
-            ]
-            + [moving] * len(more)
-            + [ANY] * len(after),
-            out_specs=moving,
-        ),
-        compiler_params=params(),
+        in_specs=[SMEM, VMEM, VMEM, ANY, VMEM] + [ANY] * len(after),
+        out_specs=VMEM,
+        scratch_shapes=[
+            pltpu.VMEM((width // TILE, TILE, depth), F32),
+            pltpu.SemaphoreType.DMA((width // TILE,)),
+        ],
+        compiler_params=params(44),
         cost_estimate=cost(6 * tok * depth * width, 4 * (depth * width + 2 * tok * width)),
         name="project",
-    )(side, x_hi, x_lo, weight, *more, *after)
+    )(sides, x_hi, x_lo, weight, more, *after)
 
 
 def local(queries, keys, values, log_decay, level_weights, norm_gain, out_weight):
@@ -403,10 +502,8 @@
             queries, keys, values, sums, cols, weights, levels, n * small, small, so_far, after
         )
 
-    def far(so_far, at, states, group, skip, last, *after):
-        return far_part(
-            upper, queries, so_far, at, weights, levels, gain, states, group * size, skip, last, after
-        )
+    def first_levels(group, states, *after):
+        return early_levels(upper, queries, close, weights, levels, states, group * size, after)
 
     a, came_a, b, came_b = [], [], [], []
 
@@ -431,22 +528,22 @@
     close, token = near(3, close, b[2])
     go(a, came_a, token)
     go(b, came_b, a[4])
-    far_a, token = far(close, 0, came_a[:early], 0, 0, False, b[3])
-    go(a, came_a, token)
+    go(a, came_a, b[3])
     go(b, came_b, a[5])
-    far_b, token = far(close, size, came_b[:early], 1, 0, False, b[4])
-    go(b, came_b, token)
-    a_hi, a_lo, _ = far(far_a, 0, came_a, 0, early, True, b[5])
+    far_a, before_a = first_levels(0, came_a[: early + 1], b[4])
+    far_b, before_b = first_levels(1, came_b[:early], before_a)
+    go(b, came_b, before_b)
 
     me = lax.axis_index("head").astype(jnp.int32)
-    mine = me.reshape(1)
-    theirs = (sides - 1 - me).reshape(1)
-    to_send = project(theirs, a_hi, a_lo, weight, 0, sides)
-    b_hi, b_lo, token = far(far_b, 0, came_b, 1, early, True, to_send)
-    to_send = project(theirs, b_hi, b_lo, weight, 1, sides, to_send)
+    both = jnp.stack([sides - 1 - me, me])
+    to_send, to_keep = finish(
+        both, upper, queries, far_a, before_a, weights, levels, gain, came_a[early + 1 :], weight, 0, True
+    )
+    to_send, b_hi, b_lo = finish(
+        both, upper, queries, far_b, before_b, weights, levels, gain, came_b[early:], weight, size, False, to_send
+    )
     came = lax.ppermute(to_send, "head", [(s, sides - 1 - s) for s in range(sides)])
-    to_keep = project(mine, a_hi, a_lo, weight, 0, sides, None, (to_send,))
-    to_keep = project(mine, b_hi, b_lo, weight, 1, sides, to_keep)
+    to_keep = project(both, b_hi, b_lo, weight, 1, to_keep)
     return to_keep + came
 
 

time: 214 us -> 198 us (0.925)
  Pallas kernels: 107 us -> 96.9 us
  local copies, waits for them, and re-layouts: 6.19 us -> 2.84 us
    pallas_call x8 -> x5, Pallas kernels: 55.3 us -> 43.4 us  [the longest x2 24.4 us: finish(): pl.pallas_call(body, out_shape=[sums] + ([sums] if both else [half]) + th...]
    unnamed x48 -> x32, local copies, waits for them, and re-layouts: 6.19 us -> 2.84 us
    pallas_call x10, Pallas kernels: 7.08 us -> 9.3 us  [merged(): pl.pallas_call(functools.partial(merge_kernel, bit), out_shape=jax.ShapeD...]
  transfers between devices with their start and end apart: 14 -> 14, of which waited for: 8 -> 7; matrix products, arithmetic and copies ran while one was open for 0% -> 0% of each run, Pallas kernels for 43% -> 44%
where the time goes in v4:
time: 198 us; the launch traced here: 197 us
  Pallas kernels  96.9 us (49%)
  waiting for transfers between devices  56 us (28%)
  starting transfers between devices  26.2 us (13%)
  between operations  13.6 us (7%)
  local copies, waits for them, and re-layouts  2.84 us (1%)
    ppermute x12, waiting for transfers between devices, send(): lax.ppermute(block, 'seq', [(s, s ^ flip) for s in range(n_seq) if wanted...  55.3 us
    pallas_call x4, Pallas kernels, near_part(): pl.pallas_call(functools.partial(near_kernel, first, levels), out_shape=(...  34.2 us
    pallas_call x2, Pallas kernels, finish(): pl.pallas_call(body, out_shape=[sums] + ([sums] if both else [half]) + th...  24.4 us
    ppermute x12, starting transfers between devices, send(): lax.ppermute(block, 'seq', [(s, s ^ flip) for s in range(n_seq) if wanted...  20.7 us
    pallas_call x2, Pallas kernels, early_levels(): pl.pallas_call(functools.partial(early_kernel, first, levels, len(states)...  13 us
    pallas_call x2, Pallas kernels, own_state(): pl.pallas_call(state_kernel, out_shape=jax.ShapeDtypeStruct((heads, ROWS,...  9.53 us
    pallas_call x10, Pallas kernels, merged(): pl.pallas_call(functools.partial(merge_kernel, bit), out_shape=jax.ShapeD...  9.3 us
    pallas_call x1, Pallas kernels, project(): pl.pallas_call(functools.partial(project_kernel, part), out_shape=jax.Sha...  5.91 us
  transfers between devices with their start and end apart: 14, of which 7 were waited for; matrix products, arithmetic and copies ran while one was open for 0% of the time, Pallas kernels for 44%

profile of v4, /device:TPU:1, one launch (start us, length us, event | category | flops | bytes accessed | tf_op | source)
XLA Modules:
  0.0 197.4 jit_solution(15177786506274848104)
XLA Ops:
  7.3 0.7 copy-done.13
  8.0 4.8 %own_state.2.refs_0_.mine_ref = f32[8,136,128]{2,1,0:T(8,128)S(1)} custom-call(f32[512,2048]{1,0:T(8,128)} %k_ref.11, f32[512,2048]{1,0:T(8,128)} %v_ref.11, f32[16,512]{1,0:T(8,128)S(1)} %copy-done.13), custom_call_target="tpu_custom_call" | custom-call | flops 536870912 | bytes 4194304 | tf_op jit(solution)/shard_map/own_state/pallas_call | solution.py:88
  12.8 2.2 %collective-permute-start = (f32[8,136,128]{2,1,0:T(8,128)S(1)}, f32[8,136,128]{2,1,0:T(8,128)S(1)}, u32[]{:S(2)}, u32[]{:S(2)}) collective-permute-start(f32[8,136,128]{2,1,0:T(8,128)S(1)} %own_state.2.refs_0_.mine_ref), channel_id=1, source_target_pairs={{0,2},{2,0},{4,6},{6,4},{8,10},{10,8},{12,14},{14,12},{16,18},{18,... | collective-permute-start | bytes 1671176 | tf_op jit(solution)/shard_map/ppermute | solution.py:495
  15.6 8.5 %near.4 = (f32[512,2048]{1,0:T(8,128)}, f32[8,128]{1,0:T(8,128)S(1)}) custom-call(f32[512,2048]{1,0:T(8,128)} %refs_2_.3, f32[512,2048]{1,0:T(8,128)} %k_ref.11, f32[512,2048]{1,0:T(8,128)} %v_ref.11, f32[16,1,512]{2,1,0:T(1,128)S(1)} %get-tuple-element.25.sums_ref, f32[512,128]{1,0:T(8,128)S(1)} %get-tuple-element.26.cols_ref, ...), custom_call_target="tpu_custom_call" | custom-call | flops 2013265920 | bytes 4194304 | tf_op jit(solution)/shard_map/near/pallas_call | solution.py:240
  24.1 3.1 %collective-permute-done.other_ref.refs_0_ = f32[8,136,128]{2,1,0:T(8,128)S(1)} collective-permute-done((f32[8,136,128]{2,1,0:T(8,128)S(1)}, f32[8,136,128]{2,1,0:T(8,128)S(1)}, u32[]{:S(2)}, u32[]{:S(2)}) %collective-permute-start) | collective-permute-done | bytes 557088 | tf_op jit(solution)/shard_map/ppermute | solution.py:495
  27.9 3.8 %collective-permute-start.2 = (f32[8,136,128]{2,1,0:T(8,128)S(1)}, f32[8,136,128]{2,1,0:T(8,128)S(1)}, u32[]{:S(2)}, u32[]{:S(2)}) collective-permute-start(f32[8,136,128]{2,1,0:T(8,128)S(1)} %merge.10.refs_0_.mine_ref), channel_id=1, source_target_pairs={{0,6},{2,4},{4,2},{6,0},{8,14},{10,12},{12,10},{14,8},{16,22},{18,... | collective-permute-start | bytes 1671176 | tf_op jit(solution)/shard_map/ppermute | solution.py:495
  31.7 4.7 %own_state.3.refs_1_.mine_ref = f32[8,136,128]{2,1,0:T(8,128)S(1)} custom-call(f32[512,2048]{1,0:T(8,128)} %k_ref.11, f32[512,2048]{1,0:T(8,128)} %v_ref.11, f32[16,512]{1,0:T(8,128)S(1)} %copy-done.14, f32[8,136,128]{2,1,0:T(8,128)S(1)} %merge.10.refs_0_.mine_ref), custom_call_target="tpu_custom_call" | custom-call | flops 536870912 | bytes 4194304 | tf_op jit(solution)/shard_map/own_state/pallas_call | solution.py:88
  36.6 8.6 %near.5 = (f32[512,2048]{1,0:T(8,128)}, f32[8,128]{1,0:T(8,128)S(1)}) custom-call(f32[512,2048]{1,0:T(8,128)} %refs_2_.3, f32[512,2048]{1,0:T(8,128)} %k_ref.11, f32[512,2048]{1,0:T(8,128)} %v_ref.11, f32[16,1,512]{2,1,0:T(1,128)S(1)} %get-tuple-element.25.sums_ref, f32[512,128]{1,0:T(8,128)S(1)} %get-tuple-element.26.cols_ref, ...), custom_call_target="tpu_custom_call", output_to_operand_aliasing={{0}: (6, {})} | custom-call | flops 2013265920 | bytes 4194304 | tf_op jit(solution)/shard_map/near/pallas_call | solution.py:240
  47.0 3.4 %collective-permute-done.1.other_ref.refs_0_ = f32[8,136,128]{2,1,0:T(8,128)S(1)} collective-permute-done((f32[8,136,128]{2,1,0:T(8,128)S(1)}, f32[8,136,128]{2,1,0:T(8,128)S(1)}, u32[]{:S(2)}, u32[]{:S(2)}) %collective-permute-start.1) | collective-permute-done | bytes 557088 | tf_op jit(solution)/shard_map/ppermute | solution.py:495
  51.2 8.6 %near.6 = (f32[512,2048]{1,0:T(8,128)}, f32[8,128]{1,0:T(8,128)S(1)}) custom-call(f32[512,2048]{1,0:T(8,128)} %refs_2_.3, f32[512,2048]{1,0:T(8,128)} %k_ref.11, f32[512,2048]{1,0:T(8,128)} %v_ref.11, f32[16,1,512]{2,1,0:T(1,128)S(1)} %get-tuple-element.25.sums_ref, f32[512,128]{1,0:T(8,128)S(1)} %get-tuple-element.26.cols_ref, ...), custom_call_target="tpu_custom_call", output_to_operand_aliasing={{0}: (6, {})} | custom-call | flops 2013265920 | bytes 4194304 | tf_op jit(solution)/shard_map/near/pallas_call | solution.py:240
  59.8 10.2 %collective-permute-done.4.other_ref.refs_2_ = f32[8,136,128]{2,1,0:T(8,128)S(1)} collective-permute-done((f32[8,136,128]{2,1,0:T(8,128)S(1)}, f32[8,136,128]{2,1,0:T(8,128)S(1)}, u32[]{:S(2)}, u32[]{:S(2)}) %collective-permute-start.4) | collective-permute-done | bytes 557088 | tf_op jit(solution)/shard_map/ppermute | solution.py:495
  70.6 1.6 collective-permute-start.6
  73.3 8.6 %near.7 = (f32[512,2048]{1,0:T(8,128)}, f32[8,128]{1,0:T(8,128)S(1)}) custom-call(f32[512,2048]{1,0:T(8,128)} %refs_2_.3, f32[512,2048]{1,0:T(8,128)} %k_ref.11, f32[512,2048]{1,0:T(8,128)} %v_ref.11, f32[16,1,512]{2,1,0:T(1,128)S(1)} %get-tuple-element.25.sums_ref, f32[512,128]{1,0:T(8,128)S(1)} %get-tuple-element.26.cols_ref, ...), custom_call_target="tpu_custom_call", output_to_operand_aliasing={{0}: (6, {})} | custom-call | flops 2013265920 | bytes 4194304 | tf_op jit(solution)/shard_map/near/pallas_call | solution.py:240
  81.9 6.8 %collective-permute-done.6.other_ref.refs_3_ = f32[8,136,128]{2,1,0:T(8,128)S(1)} collective-permute-done((f32[8,136,128]{2,1,0:T(8,128)S(1)}, f32[8,136,128]{2,1,0:T(8,128)S(1)}, u32[]{:S(2)}, u32[]{:S(2)}) %collective-permute-start.6) | collective-permute-done | bytes 557088 | tf_op jit(solution)/shard_map/ppermute | solution.py:495
  89.4 2.6 %collective-permute-start.8 = (f32[8,136,128]{2,1,0:T(8,128)S(1)}, f32[8,136,128]{2,1,0:T(8,128)S(1)}, u32[]{:S(2)}, u32[]{:S(2)}) collective-permute-start(f32[8,136,128]{2,1,0:T(8,128)S(1)} %merge.15.refs_0_.mine_ref), channel_id=1, source_target_pairs={{0,32},{2,34},{4,36},{6,38},{8,40},{10,42},{12,44},{14,46},{16,48}... | collective-permute-start | bytes 1671176 | tf_op jit(solution)/shard_map/ppermute | solution.py:495
  92.9 2.0 collective-permute-start.7
  94.8 21.3 %collective-permute-done.8.other_ref.refs_4_ = f32[8,136,128]{2,1,0:T(8,128)S(1)} collective-permute-done((f32[8,136,128]{2,1,0:T(8,128)S(1)}, f32[8,136,128]{2,1,0:T(8,128)S(1)}, u32[]{:S(2)}, u32[]{:S(2)}) %collective-permute-start.8) | collective-permute-done | bytes 557088 | tf_op jit(solution)/shard_map/ppermute | solution.py:495
  116.8 2.3 %collective-permute-start.11 = (f32[8,136,128]{2,1,0:T(8,128)S(1)}, f32[8,136,128]{2,1,0:T(8,128)S(1)}, u32[]{:S(2)}, u32[]{:S(2)}) collective-permute-start(f32[8,136,128]{2,1,0:T(8,128)S(1)} %merge.17.refs_0_), channel_id=1, source_target_pairs={{0,96},{2,98},{4,100},{6,102},{8,104},{10,106},{12,108},{14,110},{... | collective-permute-start | bytes 1671176 | tf_op jit(solution)/shard_map/ppermute | solution.py:495
  119.1 2.0 %merge.18.refs_5_.mine_ref = f32[8,136,128]{2,1,0:T(8,128)} custom-call(s32[6]{0:T(128)S(1)} %shift-right-arithmetic_and_fusion.upper_ref.refs_1_, f32[8,136,128]{2,1,0:T(8,128)S(1)} %merge.16.refs_0_.mine_ref, f32[8,136,128]{2,1,0:T(8,128)} %collective-permute-done.7.other_ref.refs_3_, f32[8,136,128]{2,1,0:T(8,128)S(1)} %merge.17.refs_0_), custom_call_target="tpu_custom_call" | custom-call | flops 417792 | bytes 1671168 | tf_op jit(solution)/shard_map/merge/pallas_call | solution.py:114
  121.1 2.4 %collective-permute-start.9 = (f32[8,136,128]{2,1,0:T(8,128)}, f32[8,136,128]{2,1,0:T(8,128)S(1)}, u32[]{:S(2)}, u32[]{:S(2)}) collective-permute-start(f32[8,136,128]{2,1,0:T(8,128)} %merge.18.refs_5_.mine_ref), channel_id=1, source_target_pairs={{0,32},{2,34},{4,36},{6,38},{8,40},{10,42},{12,44},{14,46},{16,48}... | collective-permute-start | bytes 1671176 | tf_op jit(solution)/shard_map/ppermute | solution.py:495
  123.6 6.8 %early.2 = (f32[512,1024]{1,0:T(8,128)}, f32[8,8,128]{2,1,0:T(8,128)S(1)}) custom-call(s32[6]{0:T(128)S(1)} %shift-right-arithmetic_and_fusion.upper_ref.refs_1_, f32[512,2048]{1,0:T(8,128)} %refs_2_.3, f32[512,2048]{1,0:T(8,128)} %get-tuple-element.34.near_ref, f32[512,256]{1,0:T(8,128)S(1)} %get-tuple-element.27.w_ref.refs_5_, ...), custom_call_target="tpu_custom_call" | custom-call | flops 2684354560 | bytes 8388608 | tf_op jit(solution)/shard_map/early/pallas_call | solution.py:303
  130.5 6.2 %early.3 = (f32[512,1024]{1,0:T(8,128)}, f32[8,8,128]{2,1,0:T(8,128)S(1)}) custom-call(s32[6]{0:T(128)S(1)} %shift-right-arithmetic_and_fusion.upper_ref.refs_1_, f32[512,2048]{1,0:T(8,128)} %refs_2_.3, f32[512,2048]{1,0:T(8,128)} %get-tuple-element.34.near_ref, f32[512,256]{1,0:T(8,128)S(1)} %get-tuple-element.27.w_ref.refs_5_, ...), custom_call_target="tpu_custom_call" | custom-call | flops 2147483648 | bytes 8388608 | tf_op jit(solution)/shard_map/early/pallas_call | solution.py:303
  136.7 9.9 %collective-permute-done.9.other_ref.refs_7_ = f32[8,136,128]{2,1,0:T(8,128)S(1)} collective-permute-done((f32[8,136,128]{2,1,0:T(8,128)}, f32[8,136,128]{2,1,0:T(8,128)S(1)}, u32[]{:S(2)}, u32[]{:S(2)}) %collective-permute-start.9) | collective-permute-done | bytes 557088 | tf_op jit(solution)/shard_map/ppermute | solution.py:495
  146.6 2.0 %merge.19 = f32[8,136,128]{2,1,0:T(8,128)} custom-call(s32[6]{0:T(128)S(1)} %shift-right-arithmetic_and_fusion.upper_ref.refs_1_, f32[8,136,128]{2,1,0:T(8,128)} %merge.18.refs_5_.mine_ref, f32[8,136,128]{2,1,0:T(8,128)S(1)} %collective-permute-done.9.other_ref.refs_7_, f32[8,8,128]{2,1,0:T(8,128)S(1)} %get-tuple-element.38.refs_0_.refs_4_), custom_call_target="tpu_custom_call" | custom-call | flops 417792 | bytes 1671168 | tf_op jit(solution)/shard_map/merge/pallas_call | solution.py:114
  148.6 2.6 %collective-permute-start.10 = (f32[8,136,128]{2,1,0:T(8,128)}, f32[8,136,128]{2,1,0:T(8,128)}, u32[]{:S(2)}, u32[]{:S(2)}) collective-permute-start(f32[8,136,128]{2,1,0:T(8,128)} %merge.19), channel_id=1, source_target_pairs={{0,96},{2,98},{4,100},{6,102},{8,104},{10,106},{12,108},{14,110},{... | collective-permute-start | bytes 1671176 | tf_op jit(solution)/shard_map/ppermute | solution.py:495
  151.2 0.8 copy-done.10
  152.0 1.0 copy-done.11
  153.1 14.1 %finish.2 = (f32[512,1024]{1,0:T(8,128)S(1)}, f32[512,1024]{1,0:T(8,128)S(1)}) custom-call(s32[2]{0:T(128)S(1)} %pad_add_fusion.refs_0_.sides_ref, s32[6]{0:T(128)S(1)} %shift-right-arithmetic_and_fusion.upper_ref.refs_1_, f32[512,2048]{1,0:T(8,128)} %refs_2_.3, f32[512,1024]{1,0:T(8,128)S(1)} %copy-done.9, f32[8,8,128]{2,1,0:T(8,128)S(1)} %get-tuple-element.36.refs_4_, ...), custom_call_target="tpu_custom_call" | custom-call | flops 6442450944 | bytes 16777216 | tf_op jit(solution)/shard_map/finish/pallas_call | solution.py:432
  167.2 10.3 %finish.3 = (f32[512,1024]{1,0:T(8,128)S(1)}, bf16[512,1024]{1,0:T(8,128)(2,1)S(1)}, bf16[512,1024]{1,0:T(8,128)(2,1)S(1)}) custom-call(s32[2]{0:T(128)S(1)} %pad_add_fusion.refs_0_.sides_ref, s32[6]{0:T(128)S(1)} %shift-right-arithmetic_and_fusion.upper_ref.refs_1_, f32[512,2048]{1,0:T(8,128)} %refs_2_.3, f32[512,1024]{1,0:T(8,128)S(1)} %copy-done.8, ...), custom_call_target="tpu_custom_call" | custom-call | flops 3221225472 | bytes 12582912 | tf_op jit(solution)/shard_map/finish/pallas_call | solution.py:432
  177.5 5.4 %collective-permute-start.12 = (f32[512,1024]{1,0:T(8,128)S(1)}, f32[512,1024]{1,0:T(8,128)S(1)}, u32[]{:S(2)}, u32[]{:S(2)}) collective-permute-start(f32[512,1024]{1,0:T(8,128)S(1)} %get-tuple-element.44), channel_id=1, source_target_pairs={{0,1},{1,0},{2,3},{3,2},{4,5},{5,4},{6,7},{7,6},{8,9},{9,8},{10,11... | collective-permute-start | bytes 6291464 | tf_op jit(solution)/shard_map/ppermute | solution.py:545
  182.9 5.9 %project.1 = f32[512,1024]{1,0:T(8,128)S(1)} custom-call(s32[2]{0:T(128)S(1)} %pad_add_fusion.refs_0_.sides_ref, bf16[512,1024]{1,0:T(8,128)(2,1)S(1)} %get-tuple-element.41.x_hi, bf16[512,1024]{1,0:T(8,128)(2,1)S(1)} %get-tuple-element.42.x_lo, f32[2048,2048]{1,0:T(8,128)} %all-gather.2.cloned.1.call-done.refs_8_.refs_9_.weight_ref, ...), custom_call_target="tpu_custom_call" | custom-call | flops 3221225472 | bytes 8388608 | tf_op jit(solution)/shard_map/project/pallas_call | solution.py:461
  188.8 1.7 add.3
  (54 shorter events, 8.6 us)
Async XLA Ops:
  6.5 145.5 %all-gather.2.cloned.1.call-start = ((), (), s32[]{:S(2)}) async-start(), calls=%async_computation | async-start | bytes 17039360 | tf_op jit(solution)/shard_map/all_gather | solution.py:485
  7.3 0.8 copy-start.13
  8.0 7.0 %copy-start.12 = (f32[16,16,512]{2,1,0:T(8,128)S(1)}, f32[16,16,512]{2,1,0:T(8,128)}, u32[]{:S(2)}) copy-start(f32[16,16,512]{2,1,0:T(8,128)} %w_ref.1) | copy-start | bytes 1572868
  8.0 7.0 %copy-start.14 = (f32[16,512]{1,0:T(8,128)S(1)}, f32[16,512]{1,0:T(8,128)}, u32[]{:S(2)}) copy-start(f32[16,512]{1,0:T(8,128)} %ld_ref.5) | copy-start | bytes 98308
  12.8 14.4 %collective-permute-start = (f32[8,136,128]{2,1,0:T(8,128)S(1)}, f32[8,136,128]{2,1,0:T(8,128)S(1)}, u32[]{:S(2)}, u32[]{:S(2)}) collective-permute-start(f32[8,136,128]{2,1,0:T(8,128)S(1)} %own_state.2.refs_0_.mine_ref), channel_id=1, source_target_pairs={{0,2},{2,0},{4,6},{6,4},{8,10},{10,8},{12,14},{14,12},{16,18},{18,... | collective-permute-start | bytes 1671176 | tf_op jit(solution)/shard_map/ppermute | solution.py:495
  27.9 17.7 %collective-permute-start.2 = (f32[8,136,128]{2,1,0:T(8,128)S(1)}, f32[8,136,128]{2,1,0:T(8,128)S(1)}, u32[]{:S(2)}, u32[]{:S(2)}) collective-permute-start(f32[8,136,128]{2,1,0:T(8,128)S(1)} %merge.10.refs_0_.mine_ref), channel_id=1, source_target_pairs={{0,6},{2,4},{4,2},{6,0},{8,14},{10,12},{12,10},{14,8},{16,22},{18,... | collective-permute-start | bytes 1671176 | tf_op jit(solution)/shard_map/ppermute | solution.py:495
  36.5 14.0 %collective-permute-start.1 = (f32[8,136,128]{2,1,0:T(8,128)S(1)}, f32[8,136,128]{2,1,0:T(8,128)S(1)}, u32[]{:S(2)}, u32[]{:S(2)}) collective-permute-start(f32[8,136,128]{2,1,0:T(8,128)S(1)} %own_state.3.refs_1_.mine_ref), channel_id=1, source_target_pairs={{0,2},{2,0},{4,6},{6,4},{8,10},{10,8},{12,14},{14,12},{16,18},{18,... | collective-permute-start | bytes 1671176 | tf_op jit(solution)/shard_map/ppermute | solution.py:495
  46.3 23.7 %collective-permute-start.4 = (f32[8,136,128]{2,1,0:T(8,128)S(1)}, f32[8,136,128]{2,1,0:T(8,128)S(1)}, u32[]{:S(2)}, u32[]{:S(2)}) collective-permute-start(f32[8,136,128]{2,1,0:T(8,128)S(1)} %merge.11.refs_0_.mine_ref), channel_id=1, source_target_pairs={{0,8},{2,10},{4,12},{6,14},{8,0},{10,2},{12,4},{14,6},{16,24},{18,... | collective-permute-start | bytes 1671176 | tf_op jit(solution)/shard_map/ppermute | solution.py:495
  50.4 9.3 %copy-start.2 = (f32[8,136,128]{2,1,0:T(8,128)}, f32[8,136,128]{2,1,0:T(8,128)S(1)}, u32[]{:S(2)}) copy-start(f32[8,136,128]{2,1,0:T(8,128)S(1)} %collective-permute-done.1.other_ref.refs_0_) | copy-start | bytes 1671172
  51.1 21.2 %collective-permute-start.3 = (f32[8,136,128]{2,1,0:T(8,128)S(1)}, f32[8,136,128]{2,1,0:T(8,128)S(1)}, u32[]{:S(2)}, u32[]{:S(2)}) collective-permute-start(f32[8,136,128]{2,1,0:T(8,128)S(1)} %merge.12.refs_1_.mine_ref), channel_id=1, source_target_pairs={{0,6},{2,4},{4,2},{6,0},{8,14},{10,12},{12,10},{14,8},{16,22},{18,... | collective-permute-start | bytes 1671176 | tf_op jit(solution)/shard_map/ppermute | solution.py:495
  70.0 11.9 %copy-start = (f32[8,136,128]{2,1,0:T(8,128)}, f32[8,136,128]{2,1,0:T(8,128)S(1)}, u32[]{:S(2)}) copy-start(f32[8,136,128]{2,1,0:T(8,128)S(1)} %collective-permute-done.4.other_ref.refs_2_) | copy-start | bytes 1671172
  70.6 18.1 %collective-permute-start.6 = (f32[8,136,128]{2,1,0:T(8,128)S(1)}, f32[8,136,128]{2,1,0:T(8,128)S(1)}, u32[]{:S(2)}, u32[]{:S(2)}) collective-permute-start(f32[8,136,128]{2,1,0:T(8,128)S(1)} %merge.13.refs_0_.mine_ref), channel_id=1, source_target_pairs={{0,24},{2,26},{4,28},{6,30},{8,16},{10,18},{12,20},{14,22},{16,8},... | collective-permute-start | bytes 1671176 | tf_op jit(solution)/shard_map/ppermute | solution.py:495
  72.3 9.6 %copy-start.4 = (f32[8,136,128]{2,1,0:T(8,128)}, f32[8,136,128]{2,1,0:T(8,128)S(1)}, u32[]{:S(2)}) copy-start(f32[8,136,128]{2,1,0:T(8,128)S(1)} %collective-permute-done.3.other_ref.refs_1_) | copy-start | bytes 1671172
  73.0 19.1 %collective-permute-start.5 = (f32[8,136,128]{2,1,0:T(8,128)S(1)}, f32[8,136,128]{2,1,0:T(8,128)S(1)}, u32[]{:S(2)}, u32[]{:S(2)}) collective-permute-start(f32[8,136,128]{2,1,0:T(8,128)S(1)} %merge.14.refs_1_.mine_ref), channel_id=1, source_target_pairs={{0,8},{2,10},{4,12},{6,14},{8,0},{10,2},{12,4},{14,6},{16,24},{18,... | collective-permute-start | bytes 1671176 | tf_op jit(solution)/shard_map/ppermute | solution.py:495
  88.8 3.3 %copy-start.1 = (f32[8,136,128]{2,1,0:T(8,128)}, f32[8,136,128]{2,1,0:T(8,128)S(1)}, u32[]{:S(2)}) copy-start(f32[8,136,128]{2,1,0:T(8,128)S(1)} %collective-permute-done.6.other_ref.refs_3_) | copy-start | bytes 1671172
  89.4 26.7 %collective-permute-start.8 = (f32[8,136,128]{2,1,0:T(8,128)S(1)}, f32[8,136,128]{2,1,0:T(8,128)S(1)}, u32[]{:S(2)}, u32[]{:S(2)}) collective-permute-start(f32[8,136,128]{2,1,0:T(8,128)S(1)} %merge.15.refs_0_.mine_ref), channel_id=1, source_target_pairs={{0,32},{2,34},{4,36},{6,38},{8,40},{10,42},{12,44},{14,46},{16,48}... | collective-permute-start | bytes 1671176 | tf_op jit(solution)/shard_map/ppermute | solution.py:495
  92.1 0.8 copy-start.6
  92.9 26.2 %collective-permute-start.7 = (f32[8,136,128]{2,1,0:T(8,128)S(1)}, f32[8,136,128]{2,1,0:T(8,128)}, u32[]{:S(2)}, u32[]{:S(2)}) collective-permute-start(f32[8,136,128]{2,1,0:T(8,128)S(1)} %merge.16.refs_0_.mine_ref), channel_id=1, source_target_pairs={{0,24},{2,26},{4,28},{6,30},{8,16},{10,18},{12,20},{14,22},{16,8},... | collective-permute-start | bytes 1671176 | tf_op jit(solution)/shard_map/ppermute | solution.py:495
  116.2 7.4 %copy-start.7 = (f32[8,136,128]{2,1,0:T(8,128)}, f32[8,136,128]{2,1,0:T(8,128)S(1)}, u32[]{:S(2)}) copy-start(f32[8,136,128]{2,1,0:T(8,128)S(1)} %collective-permute-done.8.other_ref.refs_4_) | copy-start | bytes 1671172
  116.8 34.3 %collective-permute-start.11 = (f32[8,136,128]{2,1,0:T(8,128)S(1)}, f32[8,136,128]{2,1,0:T(8,128)S(1)}, u32[]{:S(2)}, u32[]{:S(2)}) collective-permute-start(f32[8,136,128]{2,1,0:T(8,128)S(1)} %merge.17.refs_0_), channel_id=1, source_target_pairs={{0,96},{2,98},{4,100},{6,102},{8,104},{10,106},{12,108},{14,110},{... | collective-permute-start | bytes 1671176 | tf_op jit(solution)/shard_map/ppermute | solution.py:495
  121.1 25.5 %collective-permute-start.9 = (f32[8,136,128]{2,1,0:T(8,128)}, f32[8,136,128]{2,1,0:T(8,128)S(1)}, u32[]{:S(2)}, u32[]{:S(2)}) collective-permute-start(f32[8,136,128]{2,1,0:T(8,128)} %merge.18.refs_5_.mine_ref), channel_id=1, source_target_pairs={{0,32},{2,34},{4,36},{6,38},{8,40},{10,42},{12,44},{14,46},{16,48}... | collective-permute-start | bytes 1671176 | tf_op jit(solution)/shard_map/ppermute | solution.py:495
  123.6 6.8 %copy-start.3 = (f32[8,136,128]{2,1,0:T(8,128)S(1)}, f32[8,136,128]{2,1,0:T(8,128)}, u32[]{:S(2)}) copy-start(f32[8,136,128]{2,1,0:T(8,128)} %copy-done.2) | copy-start | bytes 1671172
  123.6 6.8 %copy-start.5 = (f32[8,136,128]{2,1,0:T(8,128)S(1)}, f32[8,136,128]{2,1,0:T(8,128)}, u32[]{:S(2)}) copy-start(f32[8,136,128]{2,1,0:T(8,128)} %copy-done.4) | copy-start | bytes 1671172
  130.4 21.6 %copy-start.9 = (f32[512,1024]{1,0:T(8,128)S(1)}, f32[512,1024]{1,0:T(8,128)}, u32[]{:S(2)}) copy-start(f32[512,1024]{1,0:T(8,128)} %get-tuple-element.39.refs_3_) | copy-start | bytes 6291460
  130.4 21.6 %copy-start.15 = (f32[2048]{0:T(1024)S(1)}, f32[2048]{0:T(1024)}, u32[]{:S(2)}) copy-start(f32[2048]{0:T(1024)} %param.12) | copy-start | bytes 24580
  148.6 18.6 %collective-permute-start.10 = (f32[8,136,128]{2,1,0:T(8,128)}, f32[8,136,128]{2,1,0:T(8,128)}, u32[]{:S(2)}, u32[]{:S(2)}) collective-permute-start(f32[8,136,128]{2,1,0:T(8,128)} %merge.19), channel_id=1, source_target_pairs={{0,96},{2,98},{4,100},{6,102},{8,104},{10,106},{12,108},{14,110},{... | collective-permute-start | bytes 1671176 | tf_op jit(solution)/shard_map/ppermute | solution.py:495
  151.2 0.8 copy-start.10
  152.0 1.1 copy-start.11
  153.1 14.1 %copy-start.8 = (f32[512,1024]{1,0:T(8,128)S(1)}, f32[512,1024]{1,0:T(8,128)}, u32[]{:S(2)}) copy-start(f32[512,1024]{1,0:T(8,128)} %get-tuple-element.37.refs_3_) | copy-start | bytes 6291460
  177.5 11.3 %collective-permute-start.12 = (f32[512,1024]{1,0:T(8,128)S(1)}, f32[512,1024]{1,0:T(8,128)S(1)}, u32[]{:S(2)}, u32[]{:S(2)}) collective-permute-start(f32[512,1024]{1,0:T(8,128)S(1)} %get-tuple-element.44), channel_id=1, source_target_pairs={{0,1},{1,0},{2,3},{3,2},{4,5},{5,4},{6,7},{7,6},{8,9},{9,8},{10,11... | collective-permute-start | bytes 6291464 | tf_op jit(solution)/shard_map/ppermute | solution.py:545
Sparse Core Ops, SparseCore 0:
  10.2 135.8 all-gather.1

commit v5 on v4

--- a/solution.py
+++ b/solution.py
@@ -98,8 +98,8 @@
     )(keys, values, log_decay, *after)
 
 
-def merge_kernel(bit, upper_ref, mine_ref, other_ref, *refs):
-    out_ref = refs[-1]
+def merge_kernel(bit, carries, upper_ref, mine_ref, other_ref, *refs):
+    out_ref = refs[-2] if carries else refs[-1]
     upper = upper_ref[bit] == 1
     for h in range(mine_ref.shape[0]):
         mine, other = mine_ref[h], other_ref[h]
@@ -110,16 +110,19 @@
         out_ref[h, DH:, :] = low[DH:] + high[DH:]
 
 
-def merged(bit, upper, mine, other, after=()):
-    return pl.pallas_call(
-        functools.partial(merge_kernel, bit),
-        out_shape=jax.ShapeDtypeStruct(mine.shape, F32),
-        in_specs=[SMEM, VMEM, VMEM] + [ANY] * len(after),
-        out_specs=VMEM,
+def merged(bit, upper, mine, other, after=(), carry=None):
+    more = [] if carry is None else [carry]
+    outs = pl.pallas_call(
+        functools.partial(merge_kernel, bit, bool(more)),
+        out_shape=[jax.ShapeDtypeStruct(mine.shape, F32)] + [jax.ShapeDtypeStruct(c.shape, F32) for c in more],
+        in_specs=[SMEM, VMEM, VMEM] + [ANY] * (len(more) + len(after)),
+        out_specs=[VMEM] + [ANY] * len(more),
+        input_output_aliases={3: 1} if more else {},
         compiler_params=params(16),
         cost_estimate=cost(3 * mine.size, 12 * mine.size),
         name="merge",
-    )(upper, mine, other, *after)
+    )(upper, mine, other, *more, *after)
+    return outs if more else outs[0]
 
 
 def prepare_kernel(ld_ref, w_ref, *refs):
@@ -348,15 +351,15 @@
         out_ref[:, cols] = made
 
 
-def finish_kernel(first, levels, skip, both, more, sides_ref, upper_ref, q_ref, near_ref, before_ref, *refs):
-    w_ref, gain_ref, *refs = refs
+def finish_kernel(first, levels, skip, tiles, upper_ref, q_ref, near_ref, before_ref, w_ref, gain_ref, *refs):
     total = upper_ref.shape[0]
-    states, weight_ref, refs = refs[: total - skip], refs[total - skip], refs[total - skip + 1 :]
-    more_ref = refs[0] if more else None
-    send_ref, second, third, buffer_ref, sems, q_buffer, q_sems = refs[-7:]
-    x_hi, x_lo = (refs[-9:-7]) if both else (second, third)
+    states, refs = refs[: total - skip], refs[total - skip :]
+    if tiles:
+        sides_ref, weight_ref, more_ref, x_hi, x_lo, send_ref, q_buffer, q_sems, buffer_ref, sems = refs
+    else:
+        x_hi, x_lo, token_ref, q_buffer, q_sems = refs[-5:]
+        token_ref[...] = jnp.zeros_like(token_ref)
     heads = states[0].shape[0]
-    steps = send_ref.shape[1] // TILE
     part = first // heads
     pair = 2
 
@@ -366,10 +369,8 @@
 
     for n in range(heads // pair):
         q_copy(n).start()
-    used = 2 if both else 1
-    for side in range(used):
-        for j in range(steps):
-            tile_copy(sides_ref[side], steps, part, j, weight_ref, buffer_ref, sems, side * steps + j).start()
+    for j in range(tiles):
+        tile_copy(sides_ref[0], tiles, part, j, weight_ref, buffer_ref, sems, j).start()
 
     per = CHUNK // levels
 
@@ -398,79 +399,77 @@
             x_hi[:, cols] = hi
             x_lo[:, cols] = lo
 
-    project_tiles(
-        sides_ref[0], steps, part, weight_ref, buffer_ref, sems, 0, x_hi, x_lo, more_ref, send_ref
-    )
-    if both:
+    if tiles:
         project_tiles(
-            sides_ref[1], steps, part, weight_ref, buffer_ref, sems, steps, x_hi, x_lo, None, second
+            sides_ref[0], tiles, part, weight_ref, buffer_ref, sems, 0, x_hi, x_lo, more_ref, send_ref
         )
 
 
-def finish(sides, upper, queries, near, before, weights, levels, gain, states, weight, first, both, more=None):
+def finish(upper, queries, near, before, weights, levels, gain, states, first, sides=None, weight=None, more=None, after=()):
     heads = states[0].shape[0]
     tok = queries.shape[0]
-    width = weight.shape[0] // 2
     depth = heads * DH
     skip = upper.shape[0] - len(states)
-    used = 2 if both else 1
-    tiles = used * width // TILE
-    sums = jax.ShapeDtypeStruct((tok, width), F32)
     half = jax.ShapeDtypeStruct((tok, depth), BF16)
-    extra = [] if more is None else [more]
-    kept = [pltpu.VMEM((tok, depth), BF16)] * 2 if both else []
-    third = [] if both else [half]
-
-    def body(*refs):
-        if both:
-            ins = refs[: 8 + len(states) + len(extra)]
-            send, keep, hi, lo, *scratch = refs[len(ins) :]
-            finish_kernel(first, levels, skip, both, bool(extra), *ins, hi, lo, send, keep, None, *scratch)
-        else:
-            finish_kernel(first, levels, skip, both, bool(extra), *refs)
-
+    tiles = 0 if weight is None else more.shape[1] // TILE
+    extra = [sides, weight, more] if tiles else []
+    outs = [half, half, jax.ShapeDtypeStruct(more.shape if tiles else (8, CHUNK), F32)]
     return pl.pallas_call(
-        body,
-        out_shape=[sums] + ([sums] if both else [half]) + third,
-        in_specs=[SMEM, SMEM, ANY] + [VMEM] * (4 + len(states)) + [ANY] + [VMEM] * len(extra),
-        out_specs=[VMEM] * (2 + len(third)),
-        scratch_shapes=kept
-        + [
-            pltpu.VMEM((tiles, TILE, depth), F32),
-            pltpu.SemaphoreType.DMA((tiles,)),
+        functools.partial(finish_kernel, first, levels, skip, tiles),
+        out_shape=outs,
+        in_specs=[SMEM, ANY]
+        + [VMEM] * (4 + len(states))
+        + ([SMEM, ANY, VMEM] if tiles else [])
+        + [ANY] * len(after),
+        out_specs=[VMEM] * len(outs),
+        scratch_shapes=[
             pltpu.VMEM((heads // 2, tok, 2 * DH), F32),
             pltpu.SemaphoreType.DMA((heads // 2,)),
-        ],
+        ]
+        + ([pltpu.VMEM((tiles, TILE, depth), F32), pltpu.SemaphoreType.DMA((tiles,))] if tiles else []),
         compiler_params=params(44),
-        cost_estimate=cost(6 * tok * depth * width * used, 4 * depth * width * used + 16 * tok * depth),
+        cost_estimate=cost(8 * tok * depth * DH + 6 * tok * depth * tiles * TILE, 16 * tok * depth),
         name="finish",
-    )(sides, upper, queries, near, before, weights, gain, *states, weight, *extra)
-
-
-def project_kernel(part, sides_ref, x_hi, x_lo, weight_ref, more_ref, *refs):
-    out_ref, buffer_ref, sems = refs[-3:]
-    steps = out_ref.shape[1] // TILE
-    for j in range(steps):
-        tile_copy(sides_ref[1], steps, part, j, weight_ref, buffer_ref, sems, j).start()
-    project_tiles(sides_ref[1], steps, part, weight_ref, buffer_ref, sems, 0, x_hi, x_lo, more_ref, out_ref)
-
-
-def project(sides, x_hi, x_lo, weight, part, more, after=()):
+    )(upper, queries, near, before, weights, gain, *states, *extra, *after)
+
+
+def project_kernel(part, used, more, sides_ref, x_hi, x_lo, weight_ref, *refs):
+    *out_refs, buffer_ref, sems = refs[-(len(used) + 2) :]
+    steps = out_refs[0].shape[1] // TILE
+    for n, side in enumerate(used):
+        for j in range(steps):
+            tile_copy(sides_ref[side], steps, part, j, weight_ref, buffer_ref, sems, n * steps + j).start()
+    for n, side in enumerate(used):
+        project_tiles(
+            sides_ref[side],
+            steps,
+            part,
+            weight_ref,
+            buffer_ref,
+            sems,
+            n * steps,
+            x_hi,
+            x_lo,
+            refs[0] if more else None,
+            out_refs[n],
+        )
+
+
+def project(sides, used, x_hi, x_lo, weight, part, more=None, after=()):
     tok, depth = x_hi.shape
     width = weight.shape[0] // 2
+    tiles = len(used) * width // TILE
+    extra = [] if more is None else [more]
     return pl.pallas_call(
-        functools.partial(project_kernel, part),
-        out_shape=jax.ShapeDtypeStruct((tok, width), F32),
-        in_specs=[SMEM, VMEM, VMEM, ANY, VMEM] + [ANY] * len(after),
-        out_specs=VMEM,
-        scratch_shapes=[
-            pltpu.VMEM((width // TILE, TILE, depth), F32),
-            pltpu.SemaphoreType.DMA((width // TILE,)),
-        ],
+        functools.partial(project_kernel, part, used, bool(extra)),
+        out_shape=[jax.ShapeDtypeStruct((tok, width), F32)] * len(used),
+        in_specs=[SMEM, VMEM, VMEM, ANY] + [VMEM] * len(extra) + [ANY] * len(after),
+        out_specs=[VMEM] * len(used),
+        scratch_shapes=[pltpu.VMEM((tiles, TILE, depth), F32), pltpu.SemaphoreType.DMA((tiles,))],
         compiler_params=params(44),
-        cost_estimate=cost(6 * tok * depth * width, 4 * (depth * width + 2 * tok * width)),
+        cost_estimate=cost(6 * tok * depth * width * len(used), 4 * (depth * width + 2 * tok * width)),
         name="project",
-    )(sides, x_hi, x_lo, weight, more, *after)
+    )(sides, x_hi, x_lo, weight, *extra, *after)
 
 
 def local(queries, keys, values, log_decay, level_weights, norm_gain, out_weight):
@@ -514,36 +513,40 @@
 
     a.append(own_state(keys, values, log_decay, 0, size))
     came_a.append(send(a[0], 0))
-    sums, cols, weights = prepare(log_decay, level_weights, (a[0],))
-    close, token = near(0, None)
-    go(a, came_a, token)
-    b.append(own_state(keys, values, log_decay, 1, size, (a[1],)))
+    own_b = own_state(keys, values, log_decay, 1, size, (a[0],))
+    sums, cols, weights = prepare(log_decay, level_weights, (own_b,))
+    after_a, own_b = merged(0, upper, a[0], came_a[0], (weights,), own_b)
+    a.append(after_a)
+    came_a.append(send(a[1], 1))
+    b.append(own_b)
     came_b.append(send(b[0], 0))
-    close, token = near(1, close, b[0])
+    close, token = near(0, None, b[0])
     go(a, came_a, token)
     go(b, came_b, a[2])
-    close, token = near(2, close, b[1])
+    close, token = near(1, close, b[1])
     go(a, came_a, token)
     go(b, came_b, a[3])
-    close, token = near(3, close, b[2])
+    close, token = near(2, close, b[2])
     go(a, came_a, token)
     go(b, came_b, a[4])
-    go(a, came_a, b[3])
+    close, token = near(3, close, b[3])
+    go(a, came_a, token)
     go(b, came_b, a[5])
     far_a, before_a = first_levels(0, came_a[: early + 1], b[4])
     far_b, before_b = first_levels(1, came_b[:early], before_a)
-    go(b, came_b, before_b)
+    a_hi, a_lo, token = finish(
+        upper, queries, far_a, before_a, weights, levels, gain, came_a[early + 1 :], 0, after=(before_b,)
+    )
+    go(b, came_b, token)
 
     me = lax.axis_index("head").astype(jnp.int32)
     both = jnp.stack([sides - 1 - me, me])
-    to_send, to_keep = finish(
-        both, upper, queries, far_a, before_a, weights, levels, gain, came_a[early + 1 :], weight, 0, True
-    )
-    to_send, b_hi, b_lo = finish(
-        both, upper, queries, far_b, before_b, weights, levels, gain, came_b[early:], weight, size, False, to_send
+    to_send, to_keep = project(both, (0, 1), a_hi, a_lo, weight, 0, after=(b[5],))
+    b_hi, b_lo, to_send = finish(
+        upper, queries, far_b, before_b, weights, levels, gain, came_b[early:], size, both, weight, to_send
     )
     came = lax.ppermute(to_send, "head", [(s, sides - 1 - s) for s in range(sides)])
-    to_keep = project(both, b_hi, b_lo, weight, 1, to_keep)
+    [to_keep] = project(both, (1,), b_hi, b_lo, weight, 1, to_keep)
     return to_keep + came
 
 

time: 198 us -> 193 us (0.975)
  waiting for transfers between devices: 56 us -> 48.2 us
    ppermute x12, waiting for transfers between devices: 55.3 us -> 47.5 us  [send(): lax.ppermute(block, 'seq', [(s, s ^ flip) for s in range(n_seq) if wanted...]
    ppermute x12, starting transfers between devices: 20.7 us -> 23 us  [send(): lax.ppermute(block, 'seq', [(s, s ^ flip) for s in range(n_seq) if wanted...]
    unnamed x32 -> x42, local copies, waits for them, and re-layouts: 2.84 us -> 4.54 us
    pallas_call x13 -> x14, Pallas kernels: 39.6 us -> 38.7 us  [the longest x2 16.1 us: project(): pl.pallas_call(functools.partial(project_kernel, part, used, bool(extra))...]
  transfers between devices with their start and end apart: 14 -> 14, of which waited for: 7 -> 6; matrix products, arithmetic and copies ran while one was open for 0% -> 0% of each run, Pallas kernels for 44% -> 45%
where the time goes in v5:
time: 193 us
  Pallas kernels  96.5 us (50%)
  waiting for transfers between devices  48.2 us (25%)
  starting transfers between devices  27.8 us (14%)
  between operations  13.7 us (7%)
  local copies, waits for them, and re-layouts  4.54 us (2%)
    ppermute x12, waiting for transfers between devices, send(): lax.ppermute(block, 'seq', [(s, s ^ flip) for s in range(n_seq) if wanted...  47.5 us
    pallas_call x4, Pallas kernels, near_part(): pl.pallas_call(functools.partial(near_kernel, first, levels), out_shape=(...  34.2 us
    ppermute x12, starting transfers between devices, send(): lax.ppermute(block, 'seq', [(s, s ^ flip) for s in range(n_seq) if wanted...  23 us
    pallas_call x2, Pallas kernels, project(): pl.pallas_call(functools.partial(project_kernel, part, used, bool(extra))...  16.1 us
    pallas_call x2, Pallas kernels, finish(): pl.pallas_call(functools.partial(finish_kernel, first, levels, skip, tile...  14.1 us
    pallas_call x2, Pallas kernels, early_levels(): pl.pallas_call(functools.partial(early_kernel, first, levels, len(states)...  13.6 us
    pallas_call x2, Pallas kernels, own_state(): pl.pallas_call(state_kernel, out_shape=jax.ShapeDtypeStruct((heads, ROWS,...  9.54 us
    pallas_call x10, Pallas kernels, merged(): pl.pallas_call(functools.partial(merge_kernel, bit, bool(more)), out_shap...  8.48 us
  transfers between devices with their start and end apart: 14, of which 6 were waited for; matrix products, arithmetic and copies ran while one was open for 0% of the time, Pallas kernels for 45%

profile of v5, /device:TPU:1, one launch (start us, length us, event | category | flops | bytes accessed | tf_op | source)
XLA Modules:
  0.0 192.6 jit_solution(3191807007107401151)
XLA Ops:
  8.0 4.7 %own_state.2.refs_0_.mine_ref = f32[8,136,128]{2,1,0:T(8,128)S(1)} custom-call(f32[512,2048]{1,0:T(8,128)} %k_ref.11, f32[512,2048]{1,0:T(8,128)} %v_ref.11, f32[16,512]{1,0:T(8,128)S(1)} %copy-done.14), custom_call_target="tpu_custom_call" | custom-call | flops 536870912 | bytes 4194304 | tf_op jit(solution)/shard_map/own_state/pallas_call | solution.py:88
  12.8 2.2 %collective-permute-start = (f32[8,136,128]{2,1,0:T(8,128)S(1)}, f32[8,136,128]{2,1,0:T(8,128)S(1)}, u32[]{:S(2)}, u32[]{:S(2)}) collective-permute-start(f32[8,136,128]{2,1,0:T(8,128)S(1)} %own_state.2.refs_0_.mine_ref), channel_id=1, source_target_pairs={{0,2},{2,0},{4,6},{6,4},{8,10},{10,8},{12,14},{14,12},{16,18},{18,... | collective-permute-start | bytes 1671176 | tf_op jit(solution)/shard_map/ppermute | solution.py:494
  15.0 4.8 %own_state.3.refs_0_ = f32[8,136,128]{2,1,0:T(8,128)S(1)} custom-call(f32[512,2048]{1,0:T(8,128)} %k_ref.11, f32[512,2048]{1,0:T(8,128)} %v_ref.11, f32[16,512]{1,0:T(8,128)S(1)} %copy-done.15, f32[8,136,128]{2,1,0:T(8,128)S(1)} %own_state.2.refs_0_.mine_ref), custom_call_target="tpu_custom_call" | custom-call | flops 536870912 | bytes 4194304 | tf_op jit(solution)/shard_map/own_state/pallas_call | solution.py:88
  20.3 6.9 %collective-permute-done.other_ref.refs_0_ = f32[8,136,128]{2,1,0:T(8,128)S(1)} collective-permute-done((f32[8,136,128]{2,1,0:T(8,128)S(1)}, f32[8,136,128]{2,1,0:T(8,128)S(1)}, u32[]{:S(2)}, u32[]{:S(2)}) %collective-permute-start) | collective-permute-done | bytes 557088 | tf_op jit(solution)/shard_map/ppermute | solution.py:494
  27.8 3.8 %collective-permute-start.2 = (f32[8,136,128]{2,1,0:T(8,128)S(1)}, f32[8,136,128]{2,1,0:T(8,128)S(1)}, u32[]{:S(2)}, u32[]{:S(2)}) collective-permute-start(f32[8,136,128]{2,1,0:T(8,128)S(1)} %get-tuple-element.35.mine_ref), channel_id=1, source_target_pairs={{0,6},{2,4},{4,2},{6,0},{8,14},{10,12},{12,10},{14,8},{16,22},{18,... | collective-permute-start | bytes 1671176 | tf_op jit(solution)/shard_map/ppermute | solution.py:494
  31.7 8.5 %near.4 = (f32[512,2048]{1,0:T(8,128)}, f32[8,128]{1,0:T(8,128)S(1)}) custom-call(f32[512,2048]{1,0:T(8,128)} %q_ref.15, f32[512,2048]{1,0:T(8,128)} %k_ref.11, f32[512,2048]{1,0:T(8,128)} %v_ref.11, f32[16,1,512]{2,1,0:T(1,128)S(1)} %get-tuple-element.30.sums_ref, f32[512,128]{1,0:T(8,128)S(1)} %get-tuple-element.31.cols_ref, ...), custom_call_target="tpu_custom_call" | custom-call | flops 2013265920 | bytes 4194304 | tf_op jit(solution)/shard_map/near/pallas_call | solution.py:243
  40.2 5.5 %collective-permute-done.2.other_ref.refs_1_ = f32[8,136,128]{2,1,0:T(8,128)S(1)} collective-permute-done((f32[8,136,128]{2,1,0:T(8,128)S(1)}, f32[8,136,128]{2,1,0:T(8,128)S(1)}, u32[]{:S(2)}, u32[]{:S(2)}) %collective-permute-start.2) | collective-permute-done | bytes 557088 | tf_op jit(solution)/shard_map/ppermute | solution.py:494
  47.5 1.8 collective-permute-start.3
  49.3 8.5 %near.5 = (f32[512,2048]{1,0:T(8,128)}, f32[8,128]{1,0:T(8,128)S(1)}) custom-call(f32[512,2048]{1,0:T(8,128)} %q_ref.15, f32[512,2048]{1,0:T(8,128)} %k_ref.11, f32[512,2048]{1,0:T(8,128)} %v_ref.11, f32[16,1,512]{2,1,0:T(1,128)S(1)} %get-tuple-element.30.sums_ref, f32[512,128]{1,0:T(8,128)S(1)} %get-tuple-element.31.cols_ref, ...), custom_call_target="tpu_custom_call", output_to_operand_aliasing={{0}: (6, {})} | custom-call | flops 2013265920 | bytes 4194304 | tf_op jit(solution)/shard_map/near/pallas_call | solution.py:243
  57.8 12.2 %collective-permute-done.4.other_ref.refs_2_ = f32[8,136,128]{2,1,0:T(8,128)S(1)} collective-permute-done((f32[8,136,128]{2,1,0:T(8,128)S(1)}, f32[8,136,128]{2,1,0:T(8,128)S(1)}, u32[]{:S(2)}, u32[]{:S(2)}) %collective-permute-start.4) | collective-permute-done | bytes 557088 | tf_op jit(solution)/shard_map/ppermute | solution.py:494
  70.7 1.6 collective-permute-start.6
  73.4 8.5 %near.6 = (f32[512,2048]{1,0:T(8,128)}, f32[8,128]{1,0:T(8,128)S(1)}) custom-call(f32[512,2048]{1,0:T(8,128)} %q_ref.15, f32[512,2048]{1,0:T(8,128)} %k_ref.11, f32[512,2048]{1,0:T(8,128)} %v_ref.11, f32[16,1,512]{2,1,0:T(1,128)S(1)} %get-tuple-element.30.sums_ref, f32[512,128]{1,0:T(8,128)S(1)} %get-tuple-element.31.cols_ref, ...), custom_call_target="tpu_custom_call", output_to_operand_aliasing={{0}: (6, {})} | custom-call | flops 2013265920 | bytes 4194304 | tf_op jit(solution)/shard_map/near/pallas_call | solution.py:243
  81.9 6.6 %collective-permute-done.6.other_ref.refs_3_ = f32[8,136,128]{2,1,0:T(8,128)S(1)} collective-permute-done((f32[8,136,128]{2,1,0:T(8,128)S(1)}, f32[8,136,128]{2,1,0:T(8,128)S(1)}, u32[]{:S(2)}, u32[]{:S(2)}) %collective-permute-start.6) | collective-permute-done | bytes 557088 | tf_op jit(solution)/shard_map/ppermute | solution.py:494
  89.2 2.5 %collective-permute-start.8 = (f32[8,136,128]{2,1,0:T(8,128)S(1)}, f32[8,136,128]{2,1,0:T(8,128)S(1)}, u32[]{:S(2)}, u32[]{:S(2)}) collective-permute-start(f32[8,136,128]{2,1,0:T(8,128)S(1)} %merge.15.refs_0_.mine_ref), channel_id=1, source_target_pairs={{0,32},{2,34},{4,36},{6,38},{8,40},{10,42},{12,44},{14,46},{16,48}... | collective-permute-start | bytes 1671176 | tf_op jit(solution)/shard_map/ppermute | solution.py:494
  92.5 2.7 %collective-permute-start.7 = (f32[8,136,128]{2,1,0:T(8,128)S(1)}, f32[8,136,128]{2,1,0:T(8,128)}, u32[]{:S(2)}, u32[]{:S(2)}) collective-permute-start(f32[8,136,128]{2,1,0:T(8,128)S(1)} %merge.16.refs_1_.mine_ref), channel_id=1, source_target_pairs={{0,24},{2,26},{4,28},{6,30},{8,16},{10,18},{12,20},{14,22},{16,8},... | collective-permute-start | bytes 1671176 | tf_op jit(solution)/shard_map/ppermute | solution.py:494
  95.3 8.6 %near.7 = (f32[512,2048]{1,0:T(8,128)}, f32[8,128]{1,0:T(8,128)S(1)}) custom-call(f32[512,2048]{1,0:T(8,128)} %q_ref.15, f32[512,2048]{1,0:T(8,128)} %k_ref.11, f32[512,2048]{1,0:T(8,128)} %v_ref.11, f32[16,1,512]{2,1,0:T(1,128)S(1)} %get-tuple-element.30.sums_ref, f32[512,128]{1,0:T(8,128)S(1)} %get-tuple-element.31.cols_ref, ...), custom_call_target="tpu_custom_call", output_to_operand_aliasing={{0}: (6, {})} | custom-call | flops 2013265920 | bytes 4194304 | tf_op jit(solution)/shard_map/near/pallas_call | solution.py:243
  103.8 12.2 %collective-permute-done.8.other_ref.refs_4_ = f32[8,136,128]{2,1,0:T(8,128)S(1)} collective-permute-done((f32[8,136,128]{2,1,0:T(8,128)S(1)}, f32[8,136,128]{2,1,0:T(8,128)S(1)}, u32[]{:S(2)}, u32[]{:S(2)}) %collective-permute-start.8) | collective-permute-done | bytes 557088 | tf_op jit(solution)/shard_map/ppermute | solution.py:494
  116.7 3.4 %collective-permute-start.10 = (f32[8,136,128]{2,1,0:T(8,128)S(1)}, f32[8,136,128]{2,1,0:T(8,128)}, u32[]{:S(2)}, u32[]{:S(2)}) collective-permute-start(f32[8,136,128]{2,1,0:T(8,128)S(1)} %merge.17.refs_0_), channel_id=1, source_target_pairs={{0,96},{2,98},{4,100},{6,102},{8,104},{10,106},{12,108},{14,110},{... | collective-permute-start | bytes 1671176 | tf_op jit(solution)/shard_map/ppermute | solution.py:494
  120.1 2.1 %merge.18.refs_5_.mine_ref = f32[8,136,128]{2,1,0:T(8,128)} custom-call(s32[6]{0:T(128)S(1)} %shift-right-arithmetic_and_fusion.upper_ref, f32[8,136,128]{2,1,0:T(8,128)S(1)} %merge.16.refs_1_.mine_ref, f32[8,136,128]{2,1,0:T(8,128)} %collective-permute-done.7.other_ref.refs_3_, f32[8,136,128]{2,1,0:T(8,128)S(1)} %merge.17.refs_0_), custom_call_target="tpu_custom_call" | custom-call | flops 417792 | bytes 1671168 | tf_op jit(solution)/shard_map/merge/pallas_call | solution.py:115
  122.2 2.1 %collective-permute-start.9 = (f32[8,136,128]{2,1,0:T(8,128)}, f32[8,136,128]{2,1,0:T(8,128)S(1)}, u32[]{:S(2)}, u32[]{:S(2)}) collective-permute-start(f32[8,136,128]{2,1,0:T(8,128)} %merge.18.refs_5_.mine_ref), channel_id=1, source_target_pairs={{0,32},{2,34},{4,36},{6,38},{8,40},{10,42},{12,44},{14,46},{16,48}... | collective-permute-start | bytes 1671176 | tf_op jit(solution)/shard_map/ppermute | solution.py:494
  124.4 6.8 %early.2 = (f32[512,1024]{1,0:T(8,128)}, f32[8,8,128]{2,1,0:T(8,128)S(1)}) custom-call(s32[6]{0:T(128)S(1)} %shift-right-arithmetic_and_fusion.upper_ref, f32[512,2048]{1,0:T(8,128)} %q_ref.15, f32[512,2048]{1,0:T(8,128)} %get-tuple-element.41.near_ref, f32[512,256]{1,0:T(8,128)S(1)} %get-tuple-element.32.refs_1_.w_ref, f32[8,136,128]{2,1,0:T(8,128)S(1)} %copy-done.5, ...), custom_call_target="tpu_custom_call" | custom-call | flops 2684354560 | bytes 8388608 | tf_op jit(solution)/shard_map/early/pallas_call | solution.py:306
  131.3 6.7 %early.3 = (f32[512,1024]{1,0:T(8,128)}, f32[8,8,128]{2,1,0:T(8,128)S(1)}) custom-call(s32[6]{0:T(128)S(1)} %shift-right-arithmetic_and_fusion.upper_ref, f32[512,2048]{1,0:T(8,128)} %q_ref.15, f32[512,2048]{1,0:T(8,128)} %get-tuple-element.41.near_ref, f32[512,256]{1,0:T(8,128)S(1)} %get-tuple-element.32.refs_1_.w_ref, f32[8,136,128]{2,1,0:T(8,128)S(1)} %copy-done.7, ...), custom_call_target="tpu_custom_call" | custom-call | flops 2147483648 | bytes 8388608 | tf_op jit(solution)/shard_map/early/pallas_call | solution.py:306
  138.0 4.3 %finish.2 = (bf16[512,1024]{1,0:T(8,128)(2,1)S(1)}, bf16[512,1024]{1,0:T(8,128)(2,1)S(1)}, f32[8,128]{1,0:T(8,128)S(1)}) custom-call(s32[6]{0:T(128)S(1)} %shift-right-arithmetic_and_fusion.upper_ref, f32[512,2048]{1,0:T(8,128)S(1)} %copy-done, f32[512,1024]{1,0:T(8,128)S(1)} %copy-done.12, f32[8,8,128]{2,1,0:T(8,128)S(1)} %get-tuple-element.43.refs_4_.before_ref, ...), custom_call_target="tpu_custom_call" | custom-call | flops 536870912 | bytes 8388608 | tf_op jit(solution)/shard_map/finish/pallas_call | solution.py:417
  143.3 4.0 %collective-permute-done.9.other_ref.refs_0_ = f32[8,136,128]{2,1,0:T(8,128)S(1)} collective-permute-done((f32[8,136,128]{2,1,0:T(8,128)}, f32[8,136,128]{2,1,0:T(8,128)S(1)}, u32[]{:S(2)}, u32[]{:S(2)}) %collective-permute-start.9) | collective-permute-done | bytes 557088 | tf_op jit(solution)/shard_map/ppermute | solution.py:494
  148.5 2.2 %collective-permute-start.11 = (f32[8,136,128]{2,1,0:T(8,128)S(1)}, f32[8,136,128]{2,1,0:T(8,128)S(1)}, u32[]{:S(2)}, u32[]{:S(2)}) collective-permute-start(f32[8,136,128]{2,1,0:T(8,128)S(1)} %merge.19.refs_0_), channel_id=1, source_target_pairs={{0,96},{2,98},{4,100},{6,102},{8,104},{10,106},{12,108},{14,110},{... | collective-permute-start | bytes 1671176 | tf_op jit(solution)/shard_map/ppermute | solution.py:494
  150.8 1.2 copy-done.18
  152.0 1.2 copy-done.20
  153.2 10.1 %project.2 = (f32[512,1024]{1,0:T(8,128)S(1)}, f32[512,1024]{1,0:T(8,128)S(1)}) custom-call(s32[2]{0:T(128)S(1)} %pad_add_fusion.sides_ref.refs_2_, bf16[512,1024]{1,0:T(8,128)(2,1)S(1)} %copy-done.18, bf16[512,1024]{1,0:T(8,128)(2,1)S(1)} %copy-done.20, f32[2048,2048]{1,0:T(8,128)} %all-gather.2.cloned.1.call-done.weight_ref.refs_3_, ...), custom_call_target="tpu_custom_call" | custom-call | flops 6442450944 | bytes 8388608 | tf_op jit(solution)/shard_map/project/pallas_call | solution.py:463
  163.4 9.8 %finish.3 = (bf16[512,1024]{1,0:T(8,128)(2,1)S(1)}, bf16[512,1024]{1,0:T(8,128)(2,1)S(1)}, f32[512,1024]{1,0:T(8,128)S(1)}) custom-call(s32[6]{0:T(128)S(1)} %shift-right-arithmetic_and_fusion.upper_ref, f32[512,2048]{1,0:T(8,128)} %q_ref.15, f32[512,1024]{1,0:T(8,128)S(1)} %copy-done.11, f32[8,8,128]{2,1,0:T(8,128)S(1)} %get-tuple-element.45.refs_1_.before_ref, ...), custom_call_target="tpu_custom_call" | custom-call | flops 3758096384 | bytes 8388608 | tf_op jit(solution)/shard_map/finish/pallas_call | solution.py:417
  173.3 4.8 %collective-permute-start.12 = (f32[512,1024]{1,0:T(8,128)S(1)}, f32[512,1024]{1,0:T(8,128)S(1)}, u32[]{:S(2)}, u32[]{:S(2)}) collective-permute-start(f32[512,1024]{1,0:T(8,128)S(1)} %get-tuple-element.54), channel_id=1, source_target_pairs={{0,1},{1,0},{2,3},{3,2},{4,5},{5,4},{6,7},{7,6},{8,9},{9,8},{10,11... | collective-permute-start | bytes 6291464 | tf_op jit(solution)/shard_map/ppermute | solution.py:548
  178.0 6.0 %project.3 = f32[512,1024]{1,0:T(8,128)S(1)} custom-call(s32[2]{0:T(128)S(1)} %pad_add_fusion.sides_ref.refs_2_, bf16[512,1024]{1,0:T(8,128)(2,1)S(1)} %get-tuple-element.51.x_hi, bf16[512,1024]{1,0:T(8,128)(2,1)S(1)} %get-tuple-element.52.x_lo, f32[2048,2048]{1,0:T(8,128)} %all-gather.2.cloned.1.call-done.weight_ref.refs_3_, ...), custom_call_target="tpu_custom_call" | custom-call | flops 3221225472 | bytes 8388608 | tf_op jit(solution)/shard_map/project/pallas_call | solution.py:463
  184.0 1.7 add.3
  (65 shorter events, 10.5 us)
Async XLA Ops:
  6.5 144.2 %all-gather.2.cloned.1.call-start = ((), (), s32[]{:S(2)}) async-start(), calls=%async_computation | async-start | bytes 17039360 | tf_op jit(solution)/shard_map/all_gather | solution.py:484
  8.0 7.0 %copy-start.15 = (f32[16,512]{1,0:T(8,128)S(1)}, f32[16,512]{1,0:T(8,128)}, u32[]{:S(2)}) copy-start(f32[16,512]{1,0:T(8,128)} %ld_ref.5) | copy-start | bytes 98308
  12.8 14.4 %collective-permute-start = (f32[8,136,128]{2,1,0:T(8,128)S(1)}, f32[8,136,128]{2,1,0:T(8,128)S(1)}, u32[]{:S(2)}, u32[]{:S(2)}) collective-permute-start(f32[8,136,128]{2,1,0:T(8,128)S(1)} %own_state.2.refs_0_.mine_ref), channel_id=1, source_target_pairs={{0,2},{2,0},{4,6},{6,4},{8,10},{10,8},{12,14},{14,12},{16,18},{18,... | collective-permute-start | bytes 1671176 | tf_op jit(solution)/shard_map/ppermute | solution.py:494
  15.0 4.8 %copy-start.13 = (f32[16,16,512]{2,1,0:T(8,128)S(1)}, f32[16,16,512]{2,1,0:T(8,128)}, u32[]{:S(2)}) copy-start(f32[16,16,512]{2,1,0:T(8,128)} %w_ref.1) | copy-start | bytes 1572868
  27.2 13.0 %copy-start.4 = (f32[8,136,128]{2,1,0:T(8,128)}, f32[8,136,128]{2,1,0:T(8,128)S(1)}, u32[]{:S(2)}) copy-start(f32[8,136,128]{2,1,0:T(8,128)S(1)} %collective-permute-done.other_ref.refs_0_) | copy-start | bytes 1671172
  27.8 17.9 %collective-permute-start.2 = (f32[8,136,128]{2,1,0:T(8,128)S(1)}, f32[8,136,128]{2,1,0:T(8,128)S(1)}, u32[]{:S(2)}, u32[]{:S(2)}) collective-permute-start(f32[8,136,128]{2,1,0:T(8,128)S(1)} %get-tuple-element.35.mine_ref), channel_id=1, source_target_pairs={{0,6},{2,4},{4,2},{6,0},{8,14},{10,12},{12,10},{14,8},{16,22},{18,... | collective-permute-start | bytes 1671176 | tf_op jit(solution)/shard_map/ppermute | solution.py:494
  31.7 15.0 %collective-permute-start.1 = (f32[8,136,128]{2,1,0:T(8,128)S(1)}, f32[8,136,128]{2,1,0:T(8,128)S(1)}, u32[]{:S(2)}, u32[]{:S(2)}) collective-permute-start(f32[8,136,128]{2,1,0:T(8,128)S(1)} %get-tuple-element.33.refs_0_.mine_ref), channel_id=1, source_target_pairs={{0,2},{2,0},{4,6},{6,4},{8,10},{10,8},{12,14},{14,12},{16,18},{18,... | collective-permute-start | bytes 1671176 | tf_op jit(solution)/shard_map/ppermute | solution.py:494
  46.4 23.6 %collective-permute-start.4 = (f32[8,136,128]{2,1,0:T(8,128)S(1)}, f32[8,136,128]{2,1,0:T(8,128)S(1)}, u32[]{:S(2)}, u32[]{:S(2)}) collective-permute-start(f32[8,136,128]{2,1,0:T(8,128)S(1)} %merge.11.refs_0_.mine_ref), channel_id=1, source_target_pairs={{0,8},{2,10},{4,12},{6,14},{8,0},{10,2},{12,4},{14,6},{16,24},{18,... | collective-permute-start | bytes 1671176 | tf_op jit(solution)/shard_map/ppermute | solution.py:494
  47.5 24.8 %collective-permute-start.3 = (f32[8,136,128]{2,1,0:T(8,128)S(1)}, f32[8,136,128]{2,1,0:T(8,128)S(1)}, u32[]{:S(2)}, u32[]{:S(2)}) collective-permute-start(f32[8,136,128]{2,1,0:T(8,128)S(1)} %merge.12.refs_1_.mine_ref), channel_id=1, source_target_pairs={{0,6},{2,4},{4,2},{6,0},{8,14},{10,12},{12,10},{14,8},{16,22},{18,... | collective-permute-start | bytes 1671176 | tf_op jit(solution)/shard_map/ppermute | solution.py:494
  70.0 11.9 %copy-start.1 = (f32[8,136,128]{2,1,0:T(8,128)}, f32[8,136,128]{2,1,0:T(8,128)S(1)}, u32[]{:S(2)}) copy-start(f32[8,136,128]{2,1,0:T(8,128)S(1)} %collective-permute-done.4.other_ref.refs_2_) | copy-start | bytes 1671172
  70.7 17.8 %collective-permute-start.6 = (f32[8,136,128]{2,1,0:T(8,128)S(1)}, f32[8,136,128]{2,1,0:T(8,128)S(1)}, u32[]{:S(2)}, u32[]{:S(2)}) collective-permute-start(f32[8,136,128]{2,1,0:T(8,128)S(1)} %merge.13.refs_0_.mine_ref), channel_id=1, source_target_pairs={{0,24},{2,26},{4,28},{6,30},{8,16},{10,18},{12,20},{14,22},{16,8},... | collective-permute-start | bytes 1671176 | tf_op jit(solution)/shard_map/ppermute | solution.py:494
  72.3 9.6 %copy-start.8 = (f32[8,136,128]{2,1,0:T(8,128)}, f32[8,136,128]{2,1,0:T(8,128)S(1)}, u32[]{:S(2)}) copy-start(f32[8,136,128]{2,1,0:T(8,128)S(1)} %collective-permute-done.3.other_ref.refs_1_) | copy-start | bytes 1671172
  72.9 18.8 %collective-permute-start.5 = (f32[8,136,128]{2,1,0:T(8,128)S(1)}, f32[8,136,128]{2,1,0:T(8,128)S(1)}, u32[]{:S(2)}, u32[]{:S(2)}) collective-permute-start(f32[8,136,128]{2,1,0:T(8,128)S(1)} %merge.14.refs_1_.mine_ref), channel_id=1, source_target_pairs={{0,8},{2,10},{4,12},{6,14},{8,0},{10,2},{12,4},{14,6},{16,24},{18,... | collective-permute-start | bytes 1671176 | tf_op jit(solution)/shard_map/ppermute | solution.py:494
  88.5 3.2 %copy-start.2 = (f32[8,136,128]{2,1,0:T(8,128)}, f32[8,136,128]{2,1,0:T(8,128)S(1)}, u32[]{:S(2)}) copy-start(f32[8,136,128]{2,1,0:T(8,128)S(1)} %collective-permute-done.6.other_ref.refs_3_) | copy-start | bytes 1671172
  89.2 26.8 %collective-permute-start.8 = (f32[8,136,128]{2,1,0:T(8,128)S(1)}, f32[8,136,128]{2,1,0:T(8,128)S(1)}, u32[]{:S(2)}, u32[]{:S(2)}) collective-permute-start(f32[8,136,128]{2,1,0:T(8,128)S(1)} %merge.15.refs_0_.mine_ref), channel_id=1, source_target_pairs={{0,32},{2,34},{4,36},{6,38},{8,40},{10,42},{12,44},{14,46},{16,48}... | collective-permute-start | bytes 1671176 | tf_op jit(solution)/shard_map/ppermute | solution.py:494
  92.5 27.6 %collective-permute-start.7 = (f32[8,136,128]{2,1,0:T(8,128)S(1)}, f32[8,136,128]{2,1,0:T(8,128)}, u32[]{:S(2)}, u32[]{:S(2)}) collective-permute-start(f32[8,136,128]{2,1,0:T(8,128)S(1)} %merge.16.refs_1_.mine_ref), channel_id=1, source_target_pairs={{0,24},{2,26},{4,28},{6,30},{8,16},{10,18},{12,20},{14,22},{16,8},... | collective-permute-start | bytes 1671176 | tf_op jit(solution)/shard_map/ppermute | solution.py:494
  103.8 20.5 %copy-start.5 = (f32[8,136,128]{2,1,0:T(8,128)S(1)}, f32[8,136,128]{2,1,0:T(8,128)}, u32[]{:S(2)}) copy-start(f32[8,136,128]{2,1,0:T(8,128)} %copy-done.4) | copy-start | bytes 1671172
  116.0 8.3 %copy-start.3 = (f32[8,136,128]{2,1,0:T(8,128)}, f32[8,136,128]{2,1,0:T(8,128)S(1)}, u32[]{:S(2)}) copy-start(f32[8,136,128]{2,1,0:T(8,128)S(1)} %collective-permute-done.8.other_ref.refs_4_) | copy-start | bytes 1671172
  116.7 21.3 %collective-permute-start.10 = (f32[8,136,128]{2,1,0:T(8,128)S(1)}, f32[8,136,128]{2,1,0:T(8,128)}, u32[]{:S(2)}, u32[]{:S(2)}) collective-permute-start(f32[8,136,128]{2,1,0:T(8,128)S(1)} %merge.17.refs_0_), channel_id=1, source_target_pairs={{0,96},{2,98},{4,100},{6,102},{8,104},{10,106},{12,108},{14,110},{... | collective-permute-start | bytes 1671176 | tf_op jit(solution)/shard_map/ppermute | solution.py:494
  122.2 25.2 %collective-permute-start.9 = (f32[8,136,128]{2,1,0:T(8,128)}, f32[8,136,128]{2,1,0:T(8,128)S(1)}, u32[]{:S(2)}, u32[]{:S(2)}) collective-permute-start(f32[8,136,128]{2,1,0:T(8,128)} %merge.18.refs_5_.mine_ref), channel_id=1, source_target_pairs={{0,32},{2,34},{4,36},{6,38},{8,40},{10,42},{12,44},{14,46},{16,48}... | collective-permute-start | bytes 1671176 | tf_op jit(solution)/shard_map/ppermute | solution.py:494
  124.4 6.8 %copy-start.7 = (f32[8,136,128]{2,1,0:T(8,128)S(1)}, f32[8,136,128]{2,1,0:T(8,128)}, u32[]{:S(2)}) copy-start(f32[8,136,128]{2,1,0:T(8,128)} %copy-done.6) | copy-start | bytes 1671172
  124.4 6.8 %copy-start.9 = (f32[8,136,128]{2,1,0:T(8,128)S(1)}, f32[8,136,128]{2,1,0:T(8,128)}, u32[]{:S(2)}) copy-start(f32[8,136,128]{2,1,0:T(8,128)} %copy-done.8) | copy-start | bytes 1671172
  131.2 6.8 %copy-start = (f32[512,2048]{1,0:T(8,128)S(1)}, f32[512,2048]{1,0:T(8,128)}, u32[]{:S(2)}) copy-start(f32[512,2048]{1,0:T(8,128)} %q_ref.15) | copy-start | bytes 12582916
  131.2 6.8 %copy-start.12 = (f32[512,1024]{1,0:T(8,128)S(1)}, f32[512,1024]{1,0:T(8,128)}, u32[]{:S(2)}) copy-start(f32[512,1024]{1,0:T(8,128)} %get-tuple-element.46.near_ref) | copy-start | bytes 6291460
  131.2 6.8 %copy-start.16 = (f32[2048]{0:T(1024)S(1)}, f32[2048]{0:T(1024)}, u32[]{:S(2)}) copy-start(f32[2048]{0:T(1024)} %param.12) | copy-start | bytes 24580
  142.3 1.0 copy-start.19
  143.3 5.2 %copy-start.17 = (bf16[512,1024]{1,0:T(8,128)(2,1)}, bf16[512,1024]{1,0:T(8,128)(2,1)S(1)}, u32[]{:S(2)}) copy-start(bf16[512,1024]{1,0:T(8,128)(2,1)S(1)} %get-tuple-element.48.x_hi) | copy-start | bytes 3145732
  148.5 14.9 %collective-permute-start.11 = (f32[8,136,128]{2,1,0:T(8,128)S(1)}, f32[8,136,128]{2,1,0:T(8,128)S(1)}, u32[]{:S(2)}, u32[]{:S(2)}) collective-permute-start(f32[8,136,128]{2,1,0:T(8,128)S(1)} %merge.19.refs_0_), channel_id=1, source_target_pairs={{0,96},{2,98},{4,100},{6,102},{8,104},{10,106},{12,108},{14,110},{... | collective-permute-start | bytes 1671176 | tf_op jit(solution)/shard_map/ppermute | solution.py:494
  150.8 1.2 copy-start.18
  152.0 1.2 copy-start.20
  153.2 10.2 %copy-start.11 = (f32[512,1024]{1,0:T(8,128)S(1)}, f32[512,1024]{1,0:T(8,128)}, u32[]{:S(2)}) copy-start(f32[512,1024]{1,0:T(8,128)} %get-tuple-element.44.near_ref) | copy-start | bytes 6291460
  173.3 10.7 %collective-permute-start.12 = (f32[512,1024]{1,0:T(8,128)S(1)}, f32[512,1024]{1,0:T(8,128)S(1)}, u32[]{:S(2)}, u32[]{:S(2)}) collective-permute-start(f32[512,1024]{1,0:T(8,128)S(1)} %get-tuple-element.54), channel_id=1, source_target_pairs={{0,1},{1,0},{2,3},{3,2},{4,5},{5,4},{6,7},{7,6},{8,9},{9,8},{10,11... | collective-permute-start | bytes 6291464 | tf_op jit(solution)/shard_map/ppermute | solution.py:548
  (3 other events, 2.4 us)
Sparse Core Ops, SparseCore 0:
  10.2 136.2 all-gather.1

commit v6 on v5

--- a/solution.py
+++ b/solution.py
@@ -56,43 +56,60 @@
     return made[:DH, :DH] + (made[:DH, DH:] + made[DH:, :DH])
 
 
-def state_kernel(k_ref, v_ref, ld_ref, *refs):
-    out_ref, fade_ref = refs[-2:]
-    heads, tok = ld_ref.shape
-    step = k_ref.shape[1] // DH
-    i = pl.program_id(0)
-
-    @pl.when(i == 0)
-    def _():
-        ld = ld_ref[...]
-        later = lax.broadcasted_iota(jnp.int32, (tok, tok), 1) > lax.broadcasted_iota(jnp.int32, (tok, tok), 0)
-        later = jnp.where(later, 1.0, 0.0).astype(BF16)
-        made = mm(later, jnp.concatenate(split3(ld), axis=0), NT)
-        fade = jnp.exp(made[:, :heads] + (made[:, heads : 2 * heads] + made[:, 2 * heads :]))
-        for j in range(heads // step):
-            fade_ref[j] = fade[:, j * step : (j + 1) * step]
-
-    fade = fade_ref[i]
-    for h in range(step):
-        cols = pl.ds(h * DH, DH)
-        out_ref[h, :DH, :] = outer_sum(k_ref[:, cols] * fade[:, h : h + 1], v_ref[:, cols])
-        total = jnp.sum(ld_ref[pl.ds(i * step + h, 1), :], axis=1, keepdims=True)
-        out_ref[h, DH:, :] = jnp.broadcast_to(total, (ROWS - DH, DH))
+def state_kernel(group, heads, pair, k_ref, v_ref, ld_ref, *refs):
+    out_ref, fade_ref, k_buffer, v_buffer, k_sems, v_sems = refs[-6:]
+    tok = ld_ref.shape[1]
+    steps = heads // pair
+
+    def copies(n):
+        cols = pl.ds(pl.multiple_of((group * heads + n * pair) * DH, pair * DH), pair * DH)
+        return (
+            pltpu.make_async_copy(k_ref.at[:, cols], k_buffer.at[n], k_sems.at[n]),
+            pltpu.make_async_copy(v_ref.at[:, cols], v_buffer.at[n], v_sems.at[n]),
+        )
+
+    for n in range(steps):
+        for copy in copies(n):
+            copy.start()
+    ld = ld_ref[group * heads : (group + 1) * heads, :]
+    later = lax.broadcasted_iota(jnp.int32, (tok, tok), 1) > lax.broadcasted_iota(jnp.int32, (tok, tok), 0)
+    later = jnp.where(later, 1.0, 0.0).astype(BF16)
+    made = mm(later, jnp.concatenate(split3(ld), axis=0), NT)
+    fade = jnp.exp(made[:, :heads] + (made[:, heads : 2 * heads] + made[:, 2 * heads :]))
+    for n in range(steps):
+        fade_ref[n] = fade[:, n * pair : (n + 1) * pair]
+    totals = jnp.sum(ld, axis=1, keepdims=True)
+    for h in range(heads):
+        out_ref[h, DH:, :] = jnp.broadcast_to(totals[h : h + 1, :], (ROWS - DH, DH))
+
+    @pl.loop(0, steps)
+    def _(n):
+        for copy in copies(n):
+            copy.wait()
+        fades = fade_ref[n]
+        for h in range(pair):
+            cols = pl.ds(h * DH, DH)
+            faded = k_buffer[n, :, cols] * fades[:, h : h + 1]
+            out_ref[n * pair + h, :DH, :] = outer_sum(faded, v_buffer[n, :, cols])
 
 
 def own_state(keys, values, log_decay, group, heads, after=()):
     tok = keys.shape[0]
-    step = 2
-    steps = heads // step
-    wide = pl.BlockSpec((tok, step * DH), lambda i: (0, group * steps + i))
+    pair = 2
+    steps = heads // pair
     return pl.pallas_call(
-        state_kernel,
+        functools.partial(state_kernel, group, heads, pair),
         out_shape=jax.ShapeDtypeStruct((heads, ROWS, DH), F32),
-        grid=(steps,),
-        in_specs=[wide, wide, pl.BlockSpec((heads, tok), lambda i: (group, 0))] + [ANY] * len(after),
-        out_specs=pl.BlockSpec((step, ROWS, DH), lambda i: (i, 0, 0)),
-        scratch_shapes=[pltpu.VMEM((steps, tok, step), F32)],
-        compiler_params=params(),
+        in_specs=[ANY, ANY, VMEM] + [ANY] * len(after),
+        out_specs=VMEM,
+        scratch_shapes=[
+            pltpu.VMEM((steps, tok, pair), F32),
+            pltpu.VMEM((steps, tok, pair * DH), F32),
+            pltpu.VMEM((steps, tok, pair * DH), F32),
+            pltpu.SemaphoreType.DMA((steps,)),
+            pltpu.SemaphoreType.DMA((steps,)),
+        ],
+        compiler_params=params(60),
         cost_estimate=cost(8 * tok * heads * DH * DH, 8 * tok * heads * DH),
         name="own_state",
     )(keys, values, log_decay, *after)
@@ -351,14 +368,13 @@
         out_ref[:, cols] = made
 
 
-def finish_kernel(first, levels, skip, tiles, upper_ref, q_ref, near_ref, before_ref, w_ref, gain_ref, *refs):
+def finish_kernel(first, levels, skip, used, more, upper_ref, q_ref, near_ref, before_ref, w_ref, gain_ref, *refs):
     total = upper_ref.shape[0]
     states, refs = refs[: total - skip], refs[total - skip :]
-    if tiles:
-        sides_ref, weight_ref, more_ref, x_hi, x_lo, send_ref, q_buffer, q_sems, buffer_ref, sems = refs
-    else:
-        x_hi, x_lo, token_ref, q_buffer, q_sems = refs[-5:]
-        token_ref[...] = jnp.zeros_like(token_ref)
+    sides_ref, weight_ref, *refs = refs
+    more_ref, refs = (refs[0], refs[1:]) if more else (None, refs)
+    x_hi, x_lo, *sum_refs, q_buffer, q_sems, buffer_ref, sems = refs[-(6 + used) :]
+    tiles = sum_refs[0].shape[1] // TILE
     heads = states[0].shape[0]
     part = first // heads
     pair = 2
@@ -369,8 +385,9 @@
 
     for n in range(heads // pair):
         q_copy(n).start()
-    for j in range(tiles):
-        tile_copy(sides_ref[0], tiles, part, j, weight_ref, buffer_ref, sems, j).start()
+    for n in range(used):
+        for j in range(tiles):
+            tile_copy(sides_ref[n], tiles, part, j, weight_ref, buffer_ref, sems, n * tiles + j).start()
 
     per = CHUNK // levels
 
@@ -399,38 +416,41 @@
             x_hi[:, cols] = hi
             x_lo[:, cols] = lo
 
-    if tiles:
+    for n in range(used):
         project_tiles(
-            sides_ref[0], tiles, part, weight_ref, buffer_ref, sems, 0, x_hi, x_lo, more_ref, send_ref
+            sides_ref[n], tiles, part, weight_ref, buffer_ref, sems, n * tiles, x_hi, x_lo, more_ref, sum_refs[n]
         )
 
 
-def finish(upper, queries, near, before, weights, levels, gain, states, first, sides=None, weight=None, more=None, after=()):
+def finish(sides, used, upper, queries, near, before, weights, levels, gain, states, first, weight, more=None, after=()):
     heads = states[0].shape[0]
     tok = queries.shape[0]
     depth = heads * DH
+    width = weight.shape[0] // 2
     skip = upper.shape[0] - len(states)
     half = jax.ShapeDtypeStruct((tok, depth), BF16)
-    tiles = 0 if weight is None else more.shape[1] // TILE
-    extra = [sides, weight, more] if tiles else []
-    outs = [half, half, jax.ShapeDtypeStruct(more.shape if tiles else (8, CHUNK), F32)]
+    tiles = used * width // TILE
+    extra = [] if more is None else [more]
+    outs = [half, half] + [jax.ShapeDtypeStruct((tok, width), F32)] * used
     return pl.pallas_call(
-        functools.partial(finish_kernel, first, levels, skip, tiles),
+        functools.partial(finish_kernel, first, levels, skip, used, bool(extra)),
         out_shape=outs,
         in_specs=[SMEM, ANY]
         + [VMEM] * (4 + len(states))
-        + ([SMEM, ANY, VMEM] if tiles else [])
+        + [SMEM, ANY]
+        + [VMEM] * len(extra)
         + [ANY] * len(after),
         out_specs=[VMEM] * len(outs),
         scratch_shapes=[
             pltpu.VMEM((heads // 2, tok, 2 * DH), F32),
             pltpu.SemaphoreType.DMA((heads // 2,)),
-        ]
-        + ([pltpu.VMEM((tiles, TILE, depth), F32), pltpu.SemaphoreType.DMA((tiles,))] if tiles else []),
+            pltpu.VMEM((tiles, TILE, depth), F32),
+            pltpu.SemaphoreType.DMA((tiles,)),
+        ],
         compiler_params=params(44),
         cost_estimate=cost(8 * tok * depth * DH + 6 * tok * depth * tiles * TILE, 16 * tok * depth),
         name="finish",
-    )(upper, queries, near, before, weights, gain, *states, *extra, *after)
+    )(upper, queries, near, before, weights, gain, *states, sides, weight, *extra, *after)
 
 
 def project_kernel(part, used, more, sides_ref, x_hi, x_lo, weight_ref, *refs):
@@ -530,20 +550,18 @@
     go(a, came_a, token)
     go(b, came_b, a[4])
     close, token = near(3, close, b[3])
-    go(a, came_a, token)
-    go(b, came_b, a[5])
-    far_a, before_a = first_levels(0, came_a[: early + 1], b[4])
+    go(b, came_b, token)
+    go(a, came_a, b[4])
+    far_a, before_a = first_levels(0, came_a[: early + 1], a[5])
     far_b, before_b = first_levels(1, came_b[:early], before_a)
-    a_hi, a_lo, token = finish(
-        upper, queries, far_a, before_a, weights, levels, gain, came_a[early + 1 :], 0, after=(before_b,)
-    )
-    go(b, came_b, token)
-
+    go(b, came_b, before_b)
     me = lax.axis_index("head").astype(jnp.int32)
     both = jnp.stack([sides - 1 - me, me])
-    to_send, to_keep = project(both, (0, 1), a_hi, a_lo, weight, 0, after=(b[5],))
+    _, _, to_send, to_keep = finish(
+        both, 2, upper, queries, far_a, before_a, weights, levels, gain, came_a[early + 1 :], 0, weight, None, (b[5],)
+    )
     b_hi, b_lo, to_send = finish(
-        upper, queries, far_b, before_b, weights, levels, gain, came_b[early:], size, both, weight, to_send
+        both, 1, upper, queries, far_b, before_b, weights, levels, gain, came_b[early:], size, weight, to_send
     )
     came = lax.ppermute(to_send, "head", [(s, sides - 1 - s) for s in range(sides)])
     [to_keep] = project(both, (1,), b_hi, b_lo, weight, 1, to_keep)

time: 193 us -> 198 us (1.026)
  waiting for transfers between devices: 48.2 us -> 53.4 us
    pallas_call x4, Pallas kernels: 23.6 us -> 34.5 us  [the longest x2 24.2 us: finish(): pl.pallas_call(functools.partial(finish_kernel, first, levels, skip, used...]
    pallas_call x2 -> x1, Pallas kernels: 16.1 us -> 5.91 us  [project(): pl.pallas_call(functools.partial(project_kernel, part, used, bool(extra))...]
    ppermute x12, waiting for transfers between devices: 47.5 us -> 52.7 us  [send(): lax.ppermute(block, 'seq', [(s, s ^ flip) for s in range(n_seq) if wanted...]
    unnamed x42 -> x38, local copies, waits for them, and re-layouts: 4.54 us -> 3.51 us
  transfers between devices with their start and end apart: 14 -> 14, of which waited for: 6 -> 7; matrix products, arithmetic and copies ran while one was open for 0% -> 0% of each run, Pallas kernels for 45% -> 44%
where the time goes in v6:
time: 198 us
  Pallas kernels  96 us (48%)
  waiting for transfers between devices  53.4 us (27%)
  starting transfers between devices  29.1 us (15%)
  between operations  13.7 us (7%)
  local copies, waits for them, and re-layouts  3.51 us (2%)
    ppermute x12, waiting for transfers between devices, send(): lax.ppermute(block, 'seq', [(s, s ^ flip) for s in range(n_seq) if wanted...  52.7 us
    pallas_call x4, Pallas kernels, near_part(): pl.pallas_call(functools.partial(near_kernel, first, levels), out_shape=(...  34.3 us
    pallas_call x2, Pallas kernels, finish(): pl.pallas_call(functools.partial(finish_kernel, first, levels, skip, used...  24.2 us
    ppermute x12, starting transfers between devices, send(): lax.ppermute(block, 'seq', [(s, s ^ flip) for s in range(n_seq) if wanted...  23.9 us
    pallas_call x2, Pallas kernels, early_levels(): pl.pallas_call(functools.partial(early_kernel, first, levels, len(states)...  13 us
    pallas_call x2, Pallas kernels, own_state(): pl.pallas_call(functools.partial(state_kernel, group, heads, pair), out_s...  10.2 us
    pallas_call x10, Pallas kernels, merged(): pl.pallas_call(functools.partial(merge_kernel, bit, bool(more)), out_shap...  7.87 us
    pallas_call x1, Pallas kernels, project(): pl.pallas_call(functools.partial(project_kernel, part, used, bool(extra))...  5.91 us
  transfers between devices with their start and end apart: 14, of which 7 were waited for; matrix products, arithmetic and copies ran while one was open for 0% of the time, Pallas kernels for 44%

profile of v6, /device:TPU:1, one launch (start us, length us, event | category | flops | bytes accessed | tf_op | source)
XLA Modules:
  0.0 197.6 jit_solution(17956790171603514956)
XLA Ops:
  7.3 5.1 %own_state.2.refs_0_.mine_ref = f32[8,136,128]{2,1,0:T(8,128)} custom-call(f32[512,2048]{1,0:T(8,128)} %k_ref.11, f32[512,2048]{1,0:T(8,128)} %v_ref.11, f32[16,512]{1,0:T(8,128)} %ld_ref.5), custom_call_target="tpu_custom_call" | custom-call | flops 536870912 | bytes 4194304 | tf_op jit(solution)/shard_map/own_state/pallas_call | solution.py:100
  12.3 2.2 %collective-permute-start = (f32[8,136,128]{2,1,0:T(8,128)}, f32[8,136,128]{2,1,0:T(8,128)S(1)}, u32[]{:S(2)}, u32[]{:S(2)}) collective-permute-start(f32[8,136,128]{2,1,0:T(8,128)} %own_state.2.refs_0_.mine_ref), channel_id=1, source_target_pairs={{0,2},{2,0},{4,6},{6,4},{8,10},{10,8},{12,14},{14,12},{16,18},{18,... | collective-permute-start | bytes 1671176 | tf_op jit(solution)/shard_map/ppermute | solution.py:514
  14.5 5.2 %own_state.3.refs_0_ = f32[8,136,128]{2,1,0:T(8,128)} custom-call(f32[512,2048]{1,0:T(8,128)} %k_ref.11, f32[512,2048]{1,0:T(8,128)} %v_ref.11, f32[16,512]{1,0:T(8,128)} %ld_ref.5, f32[8,136,128]{2,1,0:T(8,128)} %own_state.2.refs_0_.mine_ref), custom_call_target="tpu_custom_call" | custom-call | flops 536870912 | bytes 4194304 | tf_op jit(solution)/shard_map/own_state/pallas_call | solution.py:100
  20.3 6.8 %collective-permute-done.other_ref.refs_0_ = f32[8,136,128]{2,1,0:T(8,128)S(1)} collective-permute-done((f32[8,136,128]{2,1,0:T(8,128)}, f32[8,136,128]{2,1,0:T(8,128)S(1)}, u32[]{:S(2)}, u32[]{:S(2)}) %collective-permute-start) | collective-permute-done | bytes 557088 | tf_op jit(solution)/shard_map/ppermute | solution.py:514
  27.7 3.6 %collective-permute-start.2 = (f32[8,136,128]{2,1,0:T(8,128)S(1)}, f32[8,136,128]{2,1,0:T(8,128)S(1)}, u32[]{:S(2)}, u32[]{:S(2)}) collective-permute-start(f32[8,136,128]{2,1,0:T(8,128)S(1)} %get-tuple-element.32.mine_ref), channel_id=1, source_target_pairs={{0,6},{2,4},{4,2},{6,0},{8,14},{10,12},{12,10},{14,8},{16,22},{18,... | collective-permute-start | bytes 1671176 | tf_op jit(solution)/shard_map/ppermute | solution.py:514
  31.3 8.5 %near.4 = (f32[512,2048]{1,0:T(8,128)}, f32[8,128]{1,0:T(8,128)S(1)}) custom-call(f32[512,2048]{1,0:T(8,128)} %q_ref.15, f32[512,2048]{1,0:T(8,128)} %k_ref.11, f32[512,2048]{1,0:T(8,128)} %v_ref.11, f32[16,1,512]{2,1,0:T(1,128)S(1)} %get-tuple-element.27.sums_ref, f32[512,128]{1,0:T(8,128)S(1)} %get-tuple-element.28.cols_ref, ...), custom_call_target="tpu_custom_call" | custom-call | flops 2013265920 | bytes 4194304 | tf_op jit(solution)/shard_map/near/pallas_call | solution.py:260
  39.9 5.6 %collective-permute-done.2.other_ref.refs_1_ = f32[8,136,128]{2,1,0:T(8,128)S(1)} collective-permute-done((f32[8,136,128]{2,1,0:T(8,128)S(1)}, f32[8,136,128]{2,1,0:T(8,128)S(1)}, u32[]{:S(2)}, u32[]{:S(2)}) %collective-permute-start.2) | collective-permute-done | bytes 557088 | tf_op jit(solution)/shard_map/ppermute | solution.py:514
  46.7 1.4 merge.12.refs_1_.mine_ref
  48.1 1.8 collective-permute-start.3
  50.0 8.6 %near.5 = (f32[512,2048]{1,0:T(8,128)}, f32[8,128]{1,0:T(8,128)S(1)}) custom-call(f32[512,2048]{1,0:T(8,128)} %q_ref.15, f32[512,2048]{1,0:T(8,128)} %k_ref.11, f32[512,2048]{1,0:T(8,128)} %v_ref.11, f32[16,1,512]{2,1,0:T(1,128)S(1)} %get-tuple-element.27.sums_ref, f32[512,128]{1,0:T(8,128)S(1)} %get-tuple-element.28.cols_ref, ...), custom_call_target="tpu_custom_call", output_to_operand_aliasing={{0}: (6, {})} | custom-call | flops 2013265920 | bytes 4194304 | tf_op jit(solution)/shard_map/near/pallas_call | solution.py:260
  58.5 11.5 %collective-permute-done.4.other_ref.refs_2_ = f32[8,136,128]{2,1,0:T(8,128)S(1)} collective-permute-done((f32[8,136,128]{2,1,0:T(8,128)S(1)}, f32[8,136,128]{2,1,0:T(8,128)S(1)}, u32[]{:S(2)}, u32[]{:S(2)}) %collective-permute-start.4) | collective-permute-done | bytes 557088 | tf_op jit(solution)/shard_map/ppermute | solution.py:514
  70.7 1.7 collective-permute-start.6
  73.5 8.5 %near.6 = (f32[512,2048]{1,0:T(8,128)}, f32[8,128]{1,0:T(8,128)S(1)}) custom-call(f32[512,2048]{1,0:T(8,128)} %q_ref.15, f32[512,2048]{1,0:T(8,128)} %k_ref.11, f32[512,2048]{1,0:T(8,128)} %v_ref.11, f32[16,1,512]{2,1,0:T(1,128)S(1)} %get-tuple-element.27.sums_ref, f32[512,128]{1,0:T(8,128)S(1)} %get-tuple-element.28.cols_ref, ...), custom_call_target="tpu_custom_call", output_to_operand_aliasing={{0}: (6, {})} | custom-call | flops 2013265920 | bytes 4194304 | tf_op jit(solution)/shard_map/near/pallas_call | solution.py:260
  82.1 6.2 %collective-permute-done.6.other_ref.refs_3_ = f32[8,136,128]{2,1,0:T(8,128)S(1)} collective-permute-done((f32[8,136,128]{2,1,0:T(8,128)S(1)}, f32[8,136,128]{2,1,0:T(8,128)S(1)}, u32[]{:S(2)}, u32[]{:S(2)}) %collective-permute-start.6) | collective-permute-done | bytes 557088 | tf_op jit(solution)/shard_map/ppermute | solution.py:514
  88.9 2.0 %collective-permute-done.5.other_ref.refs_2_ = f32[8,136,128]{2,1,0:T(8,128)S(1)} collective-permute-done((f32[8,136,128]{2,1,0:T(8,128)S(1)}, f32[8,136,128]{2,1,0:T(8,128)S(1)}, u32[]{:S(2)}, u32[]{:S(2)}) %collective-permute-start.5) | collective-permute-done | bytes 557088 | tf_op jit(solution)/shard_map/ppermute | solution.py:514
  91.6 1.5 collective-permute-start.7
  93.1 2.6 %collective-permute-start.8 = (f32[8,136,128]{2,1,0:T(8,128)S(1)}, f32[8,136,128]{2,1,0:T(8,128)}, u32[]{:S(2)}, u32[]{:S(2)}) collective-permute-start(f32[8,136,128]{2,1,0:T(8,128)S(1)} %merge.15.refs_0_.mine_ref), channel_id=1, source_target_pairs={{0,32},{2,34},{4,36},{6,38},{8,40},{10,42},{12,44},{14,46},{16,48}... | collective-permute-start | bytes 1671176 | tf_op jit(solution)/shard_map/ppermute | solution.py:514
  95.7 8.7 %near.7 = (f32[512,2048]{1,0:T(8,128)}, f32[8,128]{1,0:T(8,128)S(1)}) custom-call(f32[512,2048]{1,0:T(8,128)} %q_ref.15, f32[512,2048]{1,0:T(8,128)} %k_ref.11, f32[512,2048]{1,0:T(8,128)} %v_ref.11, f32[16,1,512]{2,1,0:T(1,128)S(1)} %get-tuple-element.27.sums_ref, f32[512,128]{1,0:T(8,128)S(1)} %get-tuple-element.28.cols_ref, ...), custom_call_target="tpu_custom_call", output_to_operand_aliasing={{0}: (6, {})} | custom-call | flops 2013265920 | bytes 4194304 | tf_op jit(solution)/shard_map/near/pallas_call | solution.py:260
  104.4 13.0 %collective-permute-done.7.other_ref.refs_3_ = f32[8,136,128]{2,1,0:T(8,128)S(1)} collective-permute-done((f32[8,136,128]{2,1,0:T(8,128)S(1)}, f32[8,136,128]{2,1,0:T(8,128)S(1)}, u32[]{:S(2)}, u32[]{:S(2)}) %collective-permute-start.7) | collective-permute-done | bytes 557088 | tf_op jit(solution)/shard_map/ppermute | solution.py:514
  118.0 2.0 %collective-permute-start.9 = (f32[8,136,128]{2,1,0:T(8,128)S(1)}, f32[8,136,128]{2,1,0:T(8,128)S(1)}, u32[]{:S(2)}, u32[]{:S(2)}) collective-permute-start(f32[8,136,128]{2,1,0:T(8,128)S(1)} %merge.17.refs_0_.mine_ref), channel_id=1, source_target_pairs={{0,32},{2,34},{4,36},{6,38},{8,40},{10,42},{12,44},{14,46},{16,48}... | collective-permute-start | bytes 1671176 | tf_op jit(solution)/shard_map/ppermute | solution.py:514
  120.0 1.2 merge.18.refs_5_
  121.3 3.4 %collective-permute-start.11 = (f32[8,136,128]{2,1,0:T(8,128)S(1)}, f32[8,136,128]{2,1,0:T(8,128)S(1)}, u32[]{:S(2)}, u32[]{:S(2)}) collective-permute-start(f32[8,136,128]{2,1,0:T(8,128)S(1)} %merge.18.refs_5_), channel_id=1, source_target_pairs={{0,96},{2,98},{4,100},{6,102},{8,104},{10,106},{12,108},{14,110},{... | collective-permute-start | bytes 1671176 | tf_op jit(solution)/shard_map/ppermute | solution.py:514
  124.8 6.9 %early.2 = (f32[512,1024]{1,0:T(8,128)}, f32[8,8,128]{2,1,0:T(8,128)S(1)}) custom-call(s32[6]{0:T(128)S(1)} %shift-right-arithmetic_and_fusion.upper_ref, f32[512,2048]{1,0:T(8,128)} %q_ref.15, f32[512,2048]{1,0:T(8,128)} %get-tuple-element.38.near_ref, f32[512,256]{1,0:T(8,128)S(1)} %get-tuple-element.29.refs_1_.w_ref, f32[8,136,128]{2,1,0:T(8,128)S(1)} %copy-done.5, ...), custom_call_target="tpu_custom_call" | custom-call | flops 2684354560 | bytes 8388608 | tf_op jit(solution)/shard_map/early/pallas_call | solution.py:323
  131.7 6.1 %early.3 = (f32[512,1024]{1,0:T(8,128)}, f32[8,8,128]{2,1,0:T(8,128)S(1)}) custom-call(s32[6]{0:T(128)S(1)} %shift-right-arithmetic_and_fusion.upper_ref, f32[512,2048]{1,0:T(8,128)} %q_ref.15, f32[512,2048]{1,0:T(8,128)} %get-tuple-element.38.near_ref, f32[512,256]{1,0:T(8,128)S(1)} %get-tuple-element.29.refs_1_.w_ref, f32[8,136,128]{2,1,0:T(8,128)S(1)} %copy-done.7, ...), custom_call_target="tpu_custom_call" | custom-call | flops 2147483648 | bytes 8388608 | tf_op jit(solution)/shard_map/early/pallas_call | solution.py:323
  137.8 7.6 %collective-permute-done.9.other_ref.refs_0_ = f32[8,136,128]{2,1,0:T(8,128)S(1)} collective-permute-done((f32[8,136,128]{2,1,0:T(8,128)S(1)}, f32[8,136,128]{2,1,0:T(8,128)S(1)}, u32[]{:S(2)}, u32[]{:S(2)}) %collective-permute-start.9) | collective-permute-done | bytes 557088 | tf_op jit(solution)/shard_map/ppermute | solution.py:514
  146.1 3.9 %collective-permute-start.10 = (f32[8,136,128]{2,1,0:T(8,128)S(1)}, f32[8,136,128]{2,1,0:T(8,128)S(1)}, u32[]{:S(2)}, u32[]{:S(2)}) collective-permute-start(f32[8,136,128]{2,1,0:T(8,128)S(1)} %merge.19.refs_3_), channel_id=1, source_target_pairs={{0,96},{2,98},{4,100},{6,102},{8,104},{10,106},{12,108},{14,110},{... | collective-permute-start | bytes 1671176 | tf_op jit(solution)/shard_map/ppermute | solution.py:514
  150.8 1.6 copy-done.16
  153.5 14.4 %finish.2 = (bf16[512,1024]{1,0:T(8,128)(2,1)}, bf16[512,1024]{1,0:T(8,128)(2,1)}, f32[512,1024]{1,0:T(8,128)S(1)}, f32[512,1024]{1,0:T(8,128)S(1)}) custom-call(s32[6]{0:T(128)S(1)} %shift-right-arithmetic_and_fusion.upper_ref, f32[512,2048]{1,0:T(8,128)} %q_ref.15, f32[512,1024]{1,0:T(8,128)S(1)} %copy-done.16, ...), custom_call_target="tpu_custom_call" | custom-call | flops 6979321856 | bytes 8388608 | tf_op jit(solution)/shard_map/finish/pallas_call | solution.py:435
  167.9 9.8 %finish.3 = (bf16[512,1024]{1,0:T(8,128)(2,1)S(1)}, bf16[512,1024]{1,0:T(8,128)(2,1)S(1)}, f32[512,1024]{1,0:T(8,128)S(1)}) custom-call(s32[6]{0:T(128)S(1)} %shift-right-arithmetic_and_fusion.upper_ref, f32[512,2048]{1,0:T(8,128)} %q_ref.15, f32[512,1024]{1,0:T(8,128)S(1)} %copy-done.12, f32[8,8,128]{2,1,0:T(8,128)S(1)} %get-tuple-element.42.refs_0_.before_ref, ...), custom_call_target="tpu_custom_call" | custom-call | flops 3758096384 | bytes 8388608 | tf_op jit(solution)/shard_map/finish/pallas_call | solution.py:435
  177.8 5.2 %collective-permute-start.12 = (f32[512,1024]{1,0:T(8,128)S(1)}, f32[512,1024]{1,0:T(8,128)S(1)}, u32[]{:S(2)}, u32[]{:S(2)}) collective-permute-start(f32[512,1024]{1,0:T(8,128)S(1)} %get-tuple-element.48), channel_id=1, source_target_pairs={{0,1},{1,0},{2,3},{3,2},{4,5},{5,4},{6,7},{7,6},{8,9},{9,8},{10,11... | collective-permute-start | bytes 6291464 | tf_op jit(solution)/shard_map/ppermute | solution.py:566
  182.9 5.9 %project.1 = f32[512,1024]{1,0:T(8,128)S(1)} custom-call(s32[2]{0:T(128)S(1)} %pad_add_fusion.refs_1_.refs_2_.sides_ref, bf16[512,1024]{1,0:T(8,128)(2,1)S(1)} %get-tuple-element.45.x_hi, bf16[512,1024]{1,0:T(8,128)(2,1)S(1)} %get-tuple-element.46.x_lo, f32[2048,2048]{1,0:T(8,128)} %all-gather.2.cloned.1.call-done.refs_2_.refs_3_.weight_ref, ...), custom_call_target="tpu_custom_call" | custom-call | flops 3221225472 | bytes 8388608 | tf_op jit(solution)/shard_map/project/pallas_call | solution.py:483
  188.8 1.9 add.3
  (60 shorter events, 9.6 us)
Async XLA Ops:
  6.5 144.3 %all-gather.2.cloned.1.call-start = ((), (), s32[]{:S(2)}) async-start(), calls=%async_computation | async-start | bytes 17039360 | tf_op jit(solution)/shard_map/all_gather | solution.py:504
  12.3 14.8 %collective-permute-start = (f32[8,136,128]{2,1,0:T(8,128)}, f32[8,136,128]{2,1,0:T(8,128)S(1)}, u32[]{:S(2)}, u32[]{:S(2)}) collective-permute-start(f32[8,136,128]{2,1,0:T(8,128)} %own_state.2.refs_0_.mine_ref), channel_id=1, source_target_pairs={{0,2},{2,0},{4,6},{6,4},{8,10},{10,8},{12,14},{14,12},{16,18},{18,... | collective-permute-start | bytes 1671176 | tf_op jit(solution)/shard_map/ppermute | solution.py:514
  14.5 5.2 %copy-start.13 = (f32[16,16,512]{2,1,0:T(8,128)S(1)}, f32[16,16,512]{2,1,0:T(8,128)}, u32[]{:S(2)}) copy-start(f32[16,16,512]{2,1,0:T(8,128)} %w_ref.1) | copy-start | bytes 1572868
  14.5 5.2 %copy-start.14 = (f32[16,512]{1,0:T(8,128)S(1)}, f32[16,512]{1,0:T(8,128)}, u32[]{:S(2)}) copy-start(f32[16,512]{1,0:T(8,128)} %ld_ref.5) | copy-start | bytes 98308
  14.5 12.5 %copy-start = (f32[8,136,128]{2,1,0:T(8,128)S(1)}, f32[8,136,128]{2,1,0:T(8,128)}, u32[]{:S(2)}) copy-start(f32[8,136,128]{2,1,0:T(8,128)} %own_state.2.refs_0_.mine_ref) | copy-start | bytes 1671172
  27.1 12.8 %copy-start.4 = (f32[8,136,128]{2,1,0:T(8,128)}, f32[8,136,128]{2,1,0:T(8,128)S(1)}, u32[]{:S(2)}) copy-start(f32[8,136,128]{2,1,0:T(8,128)S(1)} %collective-permute-done.other_ref.refs_0_) | copy-start | bytes 1671172
  27.7 17.7 %collective-permute-start.2 = (f32[8,136,128]{2,1,0:T(8,128)S(1)}, f32[8,136,128]{2,1,0:T(8,128)S(1)}, u32[]{:S(2)}, u32[]{:S(2)}) collective-permute-start(f32[8,136,128]{2,1,0:T(8,128)S(1)} %get-tuple-element.32.mine_ref), channel_id=1, source_target_pairs={{0,6},{2,4},{4,2},{6,0},{8,14},{10,12},{12,10},{14,8},{16,22},{18,... | collective-permute-start | bytes 1671176 | tf_op jit(solution)/shard_map/ppermute | solution.py:514
  31.3 15.4 %collective-permute-start.1 = (f32[8,136,128]{2,1,0:T(8,128)}, f32[8,136,128]{2,1,0:T(8,128)S(1)}, u32[]{:S(2)}, u32[]{:S(2)}) collective-permute-start(f32[8,136,128]{2,1,0:T(8,128)} %get-tuple-element.30.refs_0_.mine_ref), channel_id=1, source_target_pairs={{0,2},{2,0},{4,6},{6,4},{8,10},{10,8},{12,14},{14,12},{16,18},{18,... | collective-permute-start | bytes 1671176 | tf_op jit(solution)/shard_map/ppermute | solution.py:514
  46.1 23.9 %collective-permute-start.4 = (f32[8,136,128]{2,1,0:T(8,128)S(1)}, f32[8,136,128]{2,1,0:T(8,128)S(1)}, u32[]{:S(2)}, u32[]{:S(2)}) collective-permute-start(f32[8,136,128]{2,1,0:T(8,128)S(1)} %merge.11.refs_0_.mine_ref), channel_id=1, source_target_pairs={{0,8},{2,10},{4,12},{6,14},{8,0},{10,2},{12,4},{14,6},{16,24},{18,... | collective-permute-start | bytes 1671176 | tf_op jit(solution)/shard_map/ppermute | solution.py:514
  46.7 11.8 %copy-start.6 = (f32[8,136,128]{2,1,0:T(8,128)}, f32[8,136,128]{2,1,0:T(8,128)S(1)}, u32[]{:S(2)}) copy-start(f32[8,136,128]{2,1,0:T(8,128)S(1)} %collective-permute-done.1.other_ref.refs_0_) | copy-start | bytes 1671172
  48.1 24.3 %collective-permute-start.3 = (f32[8,136,128]{2,1,0:T(8,128)S(1)}, f32[8,136,128]{2,1,0:T(8,128)S(1)}, u32[]{:S(2)}, u32[]{:S(2)}) collective-permute-start(f32[8,136,128]{2,1,0:T(8,128)S(1)} %merge.12.refs_1_.mine_ref), channel_id=1, source_target_pairs={{0,6},{2,4},{4,2},{6,0},{8,14},{10,12},{12,10},{14,8},{16,22},{18,... | collective-permute-start | bytes 1671176 | tf_op jit(solution)/shard_map/ppermute | solution.py:514
  70.0 12.0 %copy-start.1 = (f32[8,136,128]{2,1,0:T(8,128)}, f32[8,136,128]{2,1,0:T(8,128)S(1)}, u32[]{:S(2)}) copy-start(f32[8,136,128]{2,1,0:T(8,128)S(1)} %collective-permute-done.4.other_ref.refs_2_) | copy-start | bytes 1671172
  70.7 17.6 %collective-permute-start.6 = (f32[8,136,128]{2,1,0:T(8,128)S(1)}, f32[8,136,128]{2,1,0:T(8,128)S(1)}, u32[]{:S(2)}, u32[]{:S(2)}) collective-permute-start(f32[8,136,128]{2,1,0:T(8,128)S(1)} %merge.13.refs_0_.mine_ref), channel_id=1, source_target_pairs={{0,24},{2,26},{4,28},{6,30},{8,16},{10,18},{12,20},{14,22},{16,8},... | collective-permute-start | bytes 1671176 | tf_op jit(solution)/shard_map/ppermute | solution.py:514
  72.4 9.6 %copy-start.8 = (f32[8,136,128]{2,1,0:T(8,128)}, f32[8,136,128]{2,1,0:T(8,128)S(1)}, u32[]{:S(2)}) copy-start(f32[8,136,128]{2,1,0:T(8,128)S(1)} %collective-permute-done.3.other_ref.refs_1_) | copy-start | bytes 1671172
  73.1 17.9 %collective-permute-start.5 = (f32[8,136,128]{2,1,0:T(8,128)S(1)}, f32[8,136,128]{2,1,0:T(8,128)S(1)}, u32[]{:S(2)}, u32[]{:S(2)}) collective-permute-start(f32[8,136,128]{2,1,0:T(8,128)S(1)} %merge.14.refs_1_.mine_ref), channel_id=1, source_target_pairs={{0,8},{2,10},{4,12},{6,14},{8,0},{10,2},{12,4},{14,6},{16,24},{18,... | collective-permute-start | bytes 1671176 | tf_op jit(solution)/shard_map/ppermute | solution.py:514
  88.3 3.4 %copy-start.2 = (f32[8,136,128]{2,1,0:T(8,128)}, f32[8,136,128]{2,1,0:T(8,128)S(1)}, u32[]{:S(2)}) copy-start(f32[8,136,128]{2,1,0:T(8,128)S(1)} %collective-permute-done.6.other_ref.refs_3_) | copy-start | bytes 1671172
  91.0 2.2 %copy-start.10 = (f32[8,136,128]{2,1,0:T(8,128)}, f32[8,136,128]{2,1,0:T(8,128)S(1)}, u32[]{:S(2)}) copy-start(f32[8,136,128]{2,1,0:T(8,128)S(1)} %collective-permute-done.5.other_ref.refs_2_) | copy-start | bytes 1671172
  91.6 25.7 %collective-permute-start.7 = (f32[8,136,128]{2,1,0:T(8,128)S(1)}, f32[8,136,128]{2,1,0:T(8,128)S(1)}, u32[]{:S(2)}, u32[]{:S(2)}) collective-permute-start(f32[8,136,128]{2,1,0:T(8,128)S(1)} %merge.16.refs_1_.mine_ref), channel_id=1, source_target_pairs={{0,24},{2,26},{4,28},{6,30},{8,16},{10,18},{12,20},{14,22},{16,8},... | collective-permute-start | bytes 1671176 | tf_op jit(solution)/shard_map/ppermute | solution.py:514
  93.1 26.9 %collective-permute-start.8 = (f32[8,136,128]{2,1,0:T(8,128)S(1)}, f32[8,136,128]{2,1,0:T(8,128)}, u32[]{:S(2)}, u32[]{:S(2)}) collective-permute-start(f32[8,136,128]{2,1,0:T(8,128)S(1)} %merge.15.refs_0_.mine_ref), channel_id=1, source_target_pairs={{0,32},{2,34},{4,36},{6,38},{8,40},{10,42},{12,44},{14,46},{16,48}... | collective-permute-start | bytes 1671176 | tf_op jit(solution)/shard_map/ppermute | solution.py:514
  104.4 20.4 %copy-start.5 = (f32[8,136,128]{2,1,0:T(8,128)S(1)}, f32[8,136,128]{2,1,0:T(8,128)}, u32[]{:S(2)}) copy-start(f32[8,136,128]{2,1,0:T(8,128)} %copy-done.4) | copy-start | bytes 1671172
  117.4 14.4 %copy-start.3 = (f32[8,136,128]{2,1,0:T(8,128)}, f32[8,136,128]{2,1,0:T(8,128)S(1)}, u32[]{:S(2)}) copy-start(f32[8,136,128]{2,1,0:T(8,128)S(1)} %collective-permute-done.7.other_ref.refs_3_) | copy-start | bytes 1671172
  118.0 27.4 %collective-permute-start.9 = (f32[8,136,128]{2,1,0:T(8,128)S(1)}, f32[8,136,128]{2,1,0:T(8,128)S(1)}, u32[]{:S(2)}, u32[]{:S(2)}) collective-permute-start(f32[8,136,128]{2,1,0:T(8,128)S(1)} %merge.17.refs_0_.mine_ref), channel_id=1, source_target_pairs={{0,32},{2,34},{4,36},{6,38},{8,40},{10,42},{12,44},{14,46},{16,48}... | collective-permute-start | bytes 1671176 | tf_op jit(solution)/shard_map/ppermute | solution.py:514
  121.3 3.5 %copy-start.11 = (f32[8,136,128]{2,1,0:T(8,128)}, f32[8,136,128]{2,1,0:T(8,128)S(1)}, u32[]{:S(2)}) copy-start(f32[8,136,128]{2,1,0:T(8,128)S(1)} %merge.18.refs_5_) | copy-start | bytes 1671172
  121.3 28.7 %collective-permute-start.11 = (f32[8,136,128]{2,1,0:T(8,128)S(1)}, f32[8,136,128]{2,1,0:T(8,128)S(1)}, u32[]{:S(2)}, u32[]{:S(2)}) collective-permute-start(f32[8,136,128]{2,1,0:T(8,128)S(1)} %merge.18.refs_5_), channel_id=1, source_target_pairs={{0,96},{2,98},{4,100},{6,102},{8,104},{10,106},{12,108},{14,110},{... | collective-permute-start | bytes 1671176 | tf_op jit(solution)/shard_map/ppermute | solution.py:514
  124.8 6.9 %copy-start.7 = (f32[8,136,128]{2,1,0:T(8,128)S(1)}, f32[8,136,128]{2,1,0:T(8,128)}, u32[]{:S(2)}) copy-start(f32[8,136,128]{2,1,0:T(8,128)} %copy-done.6) | copy-start | bytes 1671172
  124.8 6.9 %copy-start.9 = (f32[8,136,128]{2,1,0:T(8,128)S(1)}, f32[8,136,128]{2,1,0:T(8,128)}, u32[]{:S(2)}) copy-start(f32[8,136,128]{2,1,0:T(8,128)} %copy-done.8) | copy-start | bytes 1671172
  131.7 19.1 %copy-start.15 = (f32[2048]{0:T(1024)S(1)}, f32[2048]{0:T(1024)}, u32[]{:S(2)}) copy-start(f32[2048]{0:T(1024)} %param.12) | copy-start | bytes 24580
  146.1 21.9 %collective-permute-start.10 = (f32[8,136,128]{2,1,0:T(8,128)S(1)}, f32[8,136,128]{2,1,0:T(8,128)S(1)}, u32[]{:S(2)}, u32[]{:S(2)}) collective-permute-start(f32[8,136,128]{2,1,0:T(8,128)S(1)} %merge.19.refs_3_), channel_id=1, source_target_pairs={{0,96},{2,98},{4,100},{6,102},{8,104},{10,106},{12,108},{14,110},{... | collective-permute-start | bytes 1671176 | tf_op jit(solution)/shard_map/ppermute | solution.py:514
  150.8 1.6 copy-start.16
  152.4 1.1 copy-start.18
  153.5 14.5 %copy-start.12 = (f32[512,1024]{1,0:T(8,128)S(1)}, f32[512,1024]{1,0:T(8,128)}, u32[]{:S(2)}) copy-start(f32[512,1024]{1,0:T(8,128)} %get-tuple-element.41.near_ref) | copy-start | bytes 6291460
  177.8 11.1 %collective-permute-start.12 = (f32[512,1024]{1,0:T(8,128)S(1)}, f32[512,1024]{1,0:T(8,128)S(1)}, u32[]{:S(2)}, u32[]{:S(2)}) collective-permute-start(f32[512,1024]{1,0:T(8,128)S(1)} %get-tuple-element.48), channel_id=1, source_target_pairs={{0,1},{1,0},{2,3},{3,2},{4,5},{5,4},{6,7},{7,6},{8,9},{9,8},{10,11... | collective-permute-start | bytes 6291464 | tf_op jit(solution)/shard_map/ppermute | solution.py:566
  (1 other events, 0.8 us)
Sparse Core Ops, SparseCore 0:
  10.2 139.1 all-gather.1

commit v7 on v5

--- a/solution.py
+++ b/solution.py
@@ -530,12 +530,12 @@
     go(a, came_a, token)
     go(b, came_b, a[4])
     close, token = near(3, close, b[3])
-    go(a, came_a, token)
+    far_a, before_a = first_levels(0, came_a[:early], token)
+    go(a, came_a, before_a)
     go(b, came_b, a[5])
-    far_a, before_a = first_levels(0, came_a[: early + 1], b[4])
-    far_b, before_b = first_levels(1, came_b[:early], before_a)
+    far_b, before_b = first_levels(1, came_b[:early], b[4])
     a_hi, a_lo, token = finish(
-        upper, queries, far_a, before_a, weights, levels, gain, came_a[early + 1 :], 0, after=(before_b,)
+        upper, queries, far_a, before_a, weights, levels, gain, came_a[early:], 0, after=(before_b,)
     )
     go(b, came_b, token)
 

time: 193 us -> 193 us (level)
    unnamed x42 -> x38, local copies, waits for them, and re-layouts: 4.54 us -> 5.04 us
  transfers between devices with their start and end apart: 14 -> 14, of which waited for: 6 -> 7; matrix products, arithmetic and copies ran while one was open for 0% -> 0% of each run, Pallas kernels for 45% -> 45%
where the time goes in v7:
time: 193 us; the launch traced here: 192 us
  Pallas kernels  96.1 us (50%)
  waiting for transfers between devices  47.4 us (25%)
  starting transfers between devices  28 us (15%)
  between operations  13.7 us (7%)
  local copies, waits for them, and re-layouts  5.04 us (3%)
    ppermute x12, waiting for transfers between devices, send(): lax.ppermute(block, 'seq', [(s, s ^ flip) for s in range(n_seq) if wanted...  46.7 us
    pallas_call x4, Pallas kernels, near_part(): pl.pallas_call(functools.partial(near_kernel, first, levels), out_shape=(...  34.3 us
    ppermute x12, starting transfers between devices, send(): lax.ppermute(block, 'seq', [(s, s ^ flip) for s in range(n_seq) if wanted...  22.9 us
    pallas_call x2, Pallas kernels, project(): pl.pallas_call(functools.partial(project_kernel, part, used, bool(extra))...  16.1 us
    pallas_call x2, Pallas kernels, finish(): pl.pallas_call(functools.partial(finish_kernel, first, levels, skip, tile...  15.3 us
    pallas_call x2, Pallas kernels, early_levels(): pl.pallas_call(functools.partial(early_kernel, first, levels, len(states)...  13.1 us
    pallas_call x2, Pallas kernels, own_state(): pl.pallas_call(state_kernel, out_shape=jax.ShapeDtypeStruct((heads, ROWS,...  9.54 us
    pallas_call x10, Pallas kernels, merged(): pl.pallas_call(functools.partial(merge_kernel, bit, bool(more)), out_shap...  7.33 us
  transfers between devices with their start and end apart: 14, of which 7 were waited for; matrix products, arithmetic and copies ran while one was open for 0% of the time, Pallas kernels for 45%

profile of v7, /device:TPU:1, one launch (start us, length us, event | category | flops | bytes accessed | tf_op | source)
XLA Modules:
  0.0 192.0 jit_solution(5102130559601168142)
XLA Ops:
  8.0 4.7 %own_state.2.refs_0_.mine_ref = f32[8,136,128]{2,1,0:T(8,128)S(1)} custom-call(f32[512,2048]{1,0:T(8,128)} %k_ref.11, f32[512,2048]{1,0:T(8,128)} %v_ref.11, f32[16,512]{1,0:T(8,128)S(1)} %copy-done.12), custom_call_target="tpu_custom_call" | custom-call | flops 536870912 | bytes 4194304 | tf_op jit(solution)/shard_map/own_state/pallas_call | solution.py:88
  12.8 2.2 %collective-permute-start = (f32[8,136,128]{2,1,0:T(8,128)S(1)}, f32[8,136,128]{2,1,0:T(8,128)S(1)}, u32[]{:S(2)}, u32[]{:S(2)}) collective-permute-start(f32[8,136,128]{2,1,0:T(8,128)S(1)} %own_state.2.refs_0_.mine_ref), channel_id=1, source_target_pairs={{0,2},{2,0},{4,6},{6,4},{8,10},{10,8},{12,14},{14,12},{16,18},{18,... | collective-permute-start | bytes 1671176 | tf_op jit(solution)/shard_map/ppermute | solution.py:494
  15.0 4.8 %own_state.3.refs_0_ = f32[8,136,128]{2,1,0:T(8,128)S(1)} custom-call(f32[512,2048]{1,0:T(8,128)} %k_ref.11, f32[512,2048]{1,0:T(8,128)} %v_ref.11, f32[16,512]{1,0:T(8,128)S(1)} %copy-done.13, f32[8,136,128]{2,1,0:T(8,128)S(1)} %own_state.2.refs_0_.mine_ref), custom_call_target="tpu_custom_call" | custom-call | flops 536870912 | bytes 4194304 | tf_op jit(solution)/shard_map/own_state/pallas_call | solution.py:88
  20.3 6.9 %collective-permute-done.other_ref.refs_0_ = f32[8,136,128]{2,1,0:T(8,128)S(1)} collective-permute-done((f32[8,136,128]{2,1,0:T(8,128)S(1)}, f32[8,136,128]{2,1,0:T(8,128)S(1)}, u32[]{:S(2)}, u32[]{:S(2)}) %collective-permute-start) | collective-permute-done | bytes 557088 | tf_op jit(solution)/shard_map/ppermute | solution.py:494
  27.8 3.8 %collective-permute-start.2 = (f32[8,136,128]{2,1,0:T(8,128)S(1)}, f32[8,136,128]{2,1,0:T(8,128)S(1)}, u32[]{:S(2)}, u32[]{:S(2)}) collective-permute-start(f32[8,136,128]{2,1,0:T(8,128)S(1)} %get-tuple-element.35.mine_ref), channel_id=1, source_target_pairs={{0,6},{2,4},{4,2},{6,0},{8,14},{10,12},{12,10},{14,8},{16,22},{18,... | collective-permute-start | bytes 1671176 | tf_op jit(solution)/shard_map/ppermute | solution.py:494
  31.7 8.5 %near.4 = (f32[512,2048]{1,0:T(8,128)}, f32[8,128]{1,0:T(8,128)S(1)}) custom-call(f32[512,2048]{1,0:T(8,128)} %q_ref.15, f32[512,2048]{1,0:T(8,128)} %k_ref.11, f32[512,2048]{1,0:T(8,128)} %v_ref.11, f32[16,1,512]{2,1,0:T(1,128)S(1)} %get-tuple-element.30.sums_ref, f32[512,128]{1,0:T(8,128)S(1)} %get-tuple-element.31.cols_ref, ...), custom_call_target="tpu_custom_call" | custom-call | flops 2013265920 | bytes 4194304 | tf_op jit(solution)/shard_map/near/pallas_call | solution.py:243
  40.2 5.5 %collective-permute-done.2.other_ref.refs_1_ = f32[8,136,128]{2,1,0:T(8,128)S(1)} collective-permute-done((f32[8,136,128]{2,1,0:T(8,128)S(1)}, f32[8,136,128]{2,1,0:T(8,128)S(1)}, u32[]{:S(2)}, u32[]{:S(2)}) %collective-permute-start.2) | collective-permute-done | bytes 557088 | tf_op jit(solution)/shard_map/ppermute | solution.py:494
  47.3 1.9 collective-permute-start.3
  49.2 8.5 %near.5 = (f32[512,2048]{1,0:T(8,128)}, f32[8,128]{1,0:T(8,128)S(1)}) custom-call(f32[512,2048]{1,0:T(8,128)} %q_ref.15, f32[512,2048]{1,0:T(8,128)} %k_ref.11, f32[512,2048]{1,0:T(8,128)} %v_ref.11, f32[16,1,512]{2,1,0:T(1,128)S(1)} %get-tuple-element.30.sums_ref, f32[512,128]{1,0:T(8,128)S(1)} %get-tuple-element.31.cols_ref, ...), custom_call_target="tpu_custom_call", output_to_operand_aliasing={{0}: (6, {})} | custom-call | flops 2013265920 | bytes 4194304 | tf_op jit(solution)/shard_map/near/pallas_call | solution.py:243
  57.7 12.3 %collective-permute-done.4.other_ref.refs_2_ = f32[8,136,128]{2,1,0:T(8,128)S(1)} collective-permute-done((f32[8,136,128]{2,1,0:T(8,128)S(1)}, f32[8,136,128]{2,1,0:T(8,128)S(1)}, u32[]{:S(2)}, u32[]{:S(2)}) %collective-permute-start.4) | collective-permute-done | bytes 557088 | tf_op jit(solution)/shard_map/ppermute | solution.py:494
  70.7 1.6 collective-permute-start.6
  73.4 8.6 %near.6 = (f32[512,2048]{1,0:T(8,128)}, f32[8,128]{1,0:T(8,128)S(1)}) custom-call(f32[512,2048]{1,0:T(8,128)} %q_ref.15, f32[512,2048]{1,0:T(8,128)} %k_ref.11, f32[512,2048]{1,0:T(8,128)} %v_ref.11, f32[16,1,512]{2,1,0:T(1,128)S(1)} %get-tuple-element.30.sums_ref, f32[512,128]{1,0:T(8,128)S(1)} %get-tuple-element.31.cols_ref, ...), custom_call_target="tpu_custom_call", output_to_operand_aliasing={{0}: (6, {})} | custom-call | flops 2013265920 | bytes 4194304 | tf_op jit(solution)/shard_map/near/pallas_call | solution.py:243
  81.9 6.6 %collective-permute-done.6.other_ref.refs_3_ = f32[8,136,128]{2,1,0:T(8,128)S(1)} collective-permute-done((f32[8,136,128]{2,1,0:T(8,128)S(1)}, f32[8,136,128]{2,1,0:T(8,128)S(1)}, u32[]{:S(2)}, u32[]{:S(2)}) %collective-permute-start.6) | collective-permute-done | bytes 557088 | tf_op jit(solution)/shard_map/ppermute | solution.py:494
  89.2 2.5 %collective-permute-start.8 = (f32[8,136,128]{2,1,0:T(8,128)S(1)}, f32[8,136,128]{2,1,0:T(8,128)S(1)}, u32[]{:S(2)}, u32[]{:S(2)}) collective-permute-start(f32[8,136,128]{2,1,0:T(8,128)S(1)} %merge.15.refs_0_.mine_ref), channel_id=1, source_target_pairs={{0,32},{2,34},{4,36},{6,38},{8,40},{10,42},{12,44},{14,46},{16,48}... | collective-permute-start | bytes 1671176 | tf_op jit(solution)/shard_map/ppermute | solution.py:494
  92.4 3.0 %collective-permute-start.7 = (f32[8,136,128]{2,1,0:T(8,128)S(1)}, f32[8,136,128]{2,1,0:T(8,128)S(1)}, u32[]{:S(2)}, u32[]{:S(2)}) collective-permute-start(f32[8,136,128]{2,1,0:T(8,128)S(1)} %merge.16.refs_1_.mine_ref), channel_id=1, source_target_pairs={{0,24},{2,26},{4,28},{6,30},{8,16},{10,18},{12,20},{14,22},{16,8},... | collective-permute-start | bytes 1671176 | tf_op jit(solution)/shard_map/ppermute | solution.py:494
  95.4 8.7 %near.7 = (f32[512,2048]{1,0:T(8,128)}, f32[8,128]{1,0:T(8,128)S(1)}) custom-call(f32[512,2048]{1,0:T(8,128)} %q_ref.15, f32[512,2048]{1,0:T(8,128)} %k_ref.11, f32[512,2048]{1,0:T(8,128)} %v_ref.11, f32[16,1,512]{2,1,0:T(1,128)S(1)} %get-tuple-element.30.sums_ref, f32[512,128]{1,0:T(8,128)S(1)} %get-tuple-element.31.cols_ref, ...), custom_call_target="tpu_custom_call", output_to_operand_aliasing={{0}: (6, {})} | custom-call | flops 2013265920 | bytes 4194304 | tf_op jit(solution)/shard_map/near/pallas_call | solution.py:243
  104.0 6.0 %early.2 = (f32[512,1024]{1,0:T(8,128)}, f32[8,8,128]{2,1,0:T(8,128)S(1)}) custom-call(s32[6]{0:T(128)S(1)} %shift-right-arithmetic_and_fusion.upper_ref, f32[512,2048]{1,0:T(8,128)} %q_ref.15, f32[512,2048]{1,0:T(8,128)} %get-tuple-element.41.near_ref, f32[512,256]{1,0:T(8,128)S(1)} %get-tuple-element.32.refs_1_.w_ref, f32[8,136,128]{2,1,0:T(8,128)S(1)} %copy-done.8, ...), custom_call_target="tpu_custom_call" | custom-call | flops 2147483648 | bytes 8388608 | tf_op jit(solution)/shard_map/early/pallas_call | solution.py:306
  110.0 6.0 %collective-permute-done.8.other_ref.refs_0_ = f32[8,136,128]{2,1,0:T(8,128)S(1)} collective-permute-done((f32[8,136,128]{2,1,0:T(8,128)S(1)}, f32[8,136,128]{2,1,0:T(8,128)S(1)}, u32[]{:S(2)}, u32[]{:S(2)}) %collective-permute-start.8) | collective-permute-done | bytes 557088 | tf_op jit(solution)/shard_map/ppermute | solution.py:494
  116.0 1.5 merge.17.refs_0_
  117.5 3.5 %collective-permute-start.10 = (f32[8,136,128]{2,1,0:T(8,128)}, f32[8,136,128]{2,1,0:T(8,128)}, u32[]{:S(2)}, u32[]{:S(2)}) collective-permute-start(f32[8,136,128]{2,1,0:T(8,128)} %merge.17.refs_0_), channel_id=1, source_target_pairs={{0,96},{2,98},{4,100},{6,102},{8,104},{10,106},{12,108},{14,110},{... | collective-permute-start | bytes 1671176 | tf_op jit(solution)/shard_map/ppermute | solution.py:494
  122.4 1.9 collective-permute-start.9
  124.4 7.1 %early.3 = (f32[512,1024]{1,0:T(8,128)}, f32[8,8,128]{2,1,0:T(8,128)S(1)}) custom-call(s32[6]{0:T(128)S(1)} %shift-right-arithmetic_and_fusion.upper_ref, f32[512,2048]{1,0:T(8,128)} %q_ref.15, f32[512,2048]{1,0:T(8,128)} %get-tuple-element.41.near_ref, f32[512,256]{1,0:T(8,128)S(1)} %get-tuple-element.32.refs_1_.w_ref, ...), custom_call_target="tpu_custom_call" | custom-call | flops 2147483648 | bytes 8388608 | tf_op jit(solution)/shard_map/early/pallas_call | solution.py:306
  131.5 5.6 %collective-permute-done.10.refs_1_ = f32[8,136,128]{2,1,0:T(8,128)} collective-permute-done((f32[8,136,128]{2,1,0:T(8,128)}, f32[8,136,128]{2,1,0:T(8,128)}, u32[]{:S(2)}, u32[]{:S(2)}) %collective-permute-start.10) | collective-permute-done | bytes 557088 | tf_op jit(solution)/shard_map/ppermute | solution.py:494
  137.1 5.4 %finish.2 = (bf16[512,1024]{1,0:T(8,128)(2,1)S(1)}, bf16[512,1024]{1,0:T(8,128)(2,1)S(1)}, f32[8,128]{1,0:T(8,128)S(1)}) custom-call(s32[6]{0:T(128)S(1)} %shift-right-arithmetic_and_fusion.upper_ref, f32[512,2048]{1,0:T(8,128)S(1)} %copy-done, f32[512,1024]{1,0:T(8,128)S(1)} %copy-done.9, f32[8,8,128]{2,1,0:T(8,128)S(1)} %get-tuple-element.43.refs_0_.before_ref, ...), custom_call_target="tpu_custom_call" | custom-call | flops 536870912 | bytes 8388608 | tf_op jit(solution)/shard_map/finish/pallas_call | solution.py:417
  143.6 3.7 %collective-permute-done.9.other_ref.refs_0_ = f32[8,136,128]{2,1,0:T(8,128)S(1)} collective-permute-done((f32[8,136,128]{2,1,0:T(8,128)S(1)}, f32[8,136,128]{2,1,0:T(8,128)S(1)}, u32[]{:S(2)}, u32[]{:S(2)}) %collective-permute-start.9) | collective-permute-done | bytes 557088 | tf_op jit(solution)/shard_map/ppermute | solution.py:494
  148.0 1.9 collective-permute-start.11
  151.2 1.2 copy-done.18
  152.4 10.1 %project.2 = (f32[512,1024]{1,0:T(8,128)S(1)}, f32[512,1024]{1,0:T(8,128)S(1)}) custom-call(s32[2]{0:T(128)S(1)} %pad_add_fusion.sides_ref.refs_2_, bf16[512,1024]{1,0:T(8,128)(2,1)S(1)} %copy-done.16, bf16[512,1024]{1,0:T(8,128)(2,1)S(1)} %copy-done.18, f32[2048,2048]{1,0:T(8,128)} %all-gather.2.cloned.1.call-done.weight_ref.refs_3_, ...), custom_call_target="tpu_custom_call" | custom-call | flops 6442450944 | bytes 8388608 | tf_op jit(solution)/shard_map/project/pallas_call | solution.py:463
  162.6 9.8 %finish.3 = (bf16[512,1024]{1,0:T(8,128)(2,1)S(1)}, bf16[512,1024]{1,0:T(8,128)(2,1)S(1)}, f32[512,1024]{1,0:T(8,128)S(1)}) custom-call(s32[6]{0:T(128)S(1)} %shift-right-arithmetic_and_fusion.upper_ref, f32[512,2048]{1,0:T(8,128)} %q_ref.15, f32[512,1024]{1,0:T(8,128)S(1)} %copy-done.10, f32[8,8,128]{2,1,0:T(8,128)S(1)} %get-tuple-element.45.refs_2_.before_ref, ...), custom_call_target="tpu_custom_call" | custom-call | flops 3758096384 | bytes 8388608 | tf_op jit(solution)/shard_map/finish/pallas_call | solution.py:417
  172.4 5.1 %collective-permute-start.12 = (f32[512,1024]{1,0:T(8,128)S(1)}, f32[512,1024]{1,0:T(8,128)S(1)}, u32[]{:S(2)}, u32[]{:S(2)}) collective-permute-start(f32[512,1024]{1,0:T(8,128)S(1)} %get-tuple-element.54), channel_id=1, source_target_pairs={{0,1},{1,0},{2,3},{3,2},{4,5},{5,4},{6,7},{7,6},{8,9},{9,8},{10,11... | collective-permute-start | bytes 6291464 | tf_op jit(solution)/shard_map/ppermute | solution.py:548
  177.5 5.9 %project.3 = f32[512,1024]{1,0:T(8,128)S(1)} custom-call(s32[2]{0:T(128)S(1)} %pad_add_fusion.sides_ref.refs_2_, bf16[512,1024]{1,0:T(8,128)(2,1)S(1)} %get-tuple-element.51.x_hi, bf16[512,1024]{1,0:T(8,128)(2,1)S(1)} %get-tuple-element.52.x_lo, f32[2048,2048]{1,0:T(8,128)} %all-gather.2.cloned.1.call-done.weight_ref.refs_3_, ...), custom_call_target="tpu_custom_call" | custom-call | flops 3221225472 | bytes 8388608 | tf_op jit(solution)/shard_map/project/pallas_call | solution.py:463
  183.4 1.7 add.3
  (61 shorter events, 11.7 us)
Async XLA Ops:
  6.5 143.4 %all-gather.2.cloned.1.call-start = ((), (), s32[]{:S(2)}) async-start(), calls=%async_computation | async-start | bytes 17039360 | tf_op jit(solution)/shard_map/all_gather | solution.py:484
  8.0 7.0 %copy-start.13 = (f32[16,512]{1,0:T(8,128)S(1)}, f32[16,512]{1,0:T(8,128)}, u32[]{:S(2)}) copy-start(f32[16,512]{1,0:T(8,128)} %ld_ref.5) | copy-start | bytes 98308
  12.8 14.4 %collective-permute-start = (f32[8,136,128]{2,1,0:T(8,128)S(1)}, f32[8,136,128]{2,1,0:T(8,128)S(1)}, u32[]{:S(2)}, u32[]{:S(2)}) collective-permute-start(f32[8,136,128]{2,1,0:T(8,128)S(1)} %own_state.2.refs_0_.mine_ref), channel_id=1, source_target_pairs={{0,2},{2,0},{4,6},{6,4},{8,10},{10,8},{12,14},{14,12},{16,18},{18,... | collective-permute-start | bytes 1671176 | tf_op jit(solution)/shard_map/ppermute | solution.py:494
  15.0 4.8 %copy-start.11 = (f32[16,16,512]{2,1,0:T(8,128)S(1)}, f32[16,16,512]{2,1,0:T(8,128)}, u32[]{:S(2)}) copy-start(f32[16,16,512]{2,1,0:T(8,128)} %w_ref.1) | copy-start | bytes 1572868
  27.2 13.0 %copy-start.7 = (f32[8,136,128]{2,1,0:T(8,128)}, f32[8,136,128]{2,1,0:T(8,128)S(1)}, u32[]{:S(2)}) copy-start(f32[8,136,128]{2,1,0:T(8,128)S(1)} %collective-permute-done.other_ref.refs_0_) | copy-start | bytes 1671172
  27.8 17.9 %collective-permute-start.2 = (f32[8,136,128]{2,1,0:T(8,128)S(1)}, f32[8,136,128]{2,1,0:T(8,128)S(1)}, u32[]{:S(2)}, u32[]{:S(2)}) collective-permute-start(f32[8,136,128]{2,1,0:T(8,128)S(1)} %get-tuple-element.35.mine_ref), channel_id=1, source_target_pairs={{0,6},{2,4},{4,2},{6,0},{8,14},{10,12},{12,10},{14,8},{16,22},{18,... | collective-permute-start | bytes 1671176 | tf_op jit(solution)/shard_map/ppermute | solution.py:494
  31.7 15.0 %collective-permute-start.1 = (f32[8,136,128]{2,1,0:T(8,128)S(1)}, f32[8,136,128]{2,1,0:T(8,128)S(1)}, u32[]{:S(2)}, u32[]{:S(2)}) collective-permute-start(f32[8,136,128]{2,1,0:T(8,128)S(1)} %get-tuple-element.33.refs_0_.mine_ref), channel_id=1, source_target_pairs={{0,2},{2,0},{4,6},{6,4},{8,10},{10,8},{12,14},{14,12},{16,18},{18,... | collective-permute-start | bytes 1671176 | tf_op jit(solution)/shard_map/ppermute | solution.py:494
  46.4 23.6 %collective-permute-start.4 = (f32[8,136,128]{2,1,0:T(8,128)S(1)}, f32[8,136,128]{2,1,0:T(8,128)S(1)}, u32[]{:S(2)}, u32[]{:S(2)}) collective-permute-start(f32[8,136,128]{2,1,0:T(8,128)S(1)} %merge.11.refs_0_.mine_ref), channel_id=1, source_target_pairs={{0,8},{2,10},{4,12},{6,14},{8,0},{10,2},{12,4},{14,6},{16,24},{18,... | collective-permute-start | bytes 1671176 | tf_op jit(solution)/shard_map/ppermute | solution.py:494
  47.3 25.0 %collective-permute-start.3 = (f32[8,136,128]{2,1,0:T(8,128)S(1)}, f32[8,136,128]{2,1,0:T(8,128)S(1)}, u32[]{:S(2)}, u32[]{:S(2)}) collective-permute-start(f32[8,136,128]{2,1,0:T(8,128)S(1)} %merge.12.refs_1_.mine_ref), channel_id=1, source_target_pairs={{0,6},{2,4},{4,2},{6,0},{8,14},{10,12},{12,10},{14,8},{16,22},{18,... | collective-permute-start | bytes 1671176 | tf_op jit(solution)/shard_map/ppermute | solution.py:494
  70.0 11.9 %copy-start.5 = (f32[8,136,128]{2,1,0:T(8,128)}, f32[8,136,128]{2,1,0:T(8,128)S(1)}, u32[]{:S(2)}) copy-start(f32[8,136,128]{2,1,0:T(8,128)S(1)} %collective-permute-done.4.other_ref.refs_2_) | copy-start | bytes 1671172
  70.7 17.8 %collective-permute-start.6 = (f32[8,136,128]{2,1,0:T(8,128)S(1)}, f32[8,136,128]{2,1,0:T(8,128)S(1)}, u32[]{:S(2)}, u32[]{:S(2)}) collective-permute-start(f32[8,136,128]{2,1,0:T(8,128)S(1)} %merge.13.refs_0_.mine_ref), channel_id=1, source_target_pairs={{0,24},{2,26},{4,28},{6,30},{8,16},{10,18},{12,20},{14,22},{16,8},... | collective-permute-start | bytes 1671176 | tf_op jit(solution)/shard_map/ppermute | solution.py:494
  72.9 18.7 %collective-permute-start.5 = (f32[8,136,128]{2,1,0:T(8,128)S(1)}, f32[8,136,128]{2,1,0:T(8,128)S(1)}, u32[]{:S(2)}, u32[]{:S(2)}) collective-permute-start(f32[8,136,128]{2,1,0:T(8,128)S(1)} %merge.14.refs_1_.mine_ref), channel_id=1, source_target_pairs={{0,8},{2,10},{4,12},{6,14},{8,0},{10,2},{12,4},{14,6},{16,24},{18,... | collective-permute-start | bytes 1671176 | tf_op jit(solution)/shard_map/ppermute | solution.py:494
  88.5 15.5 %copy-start.6 = (f32[8,136,128]{2,1,0:T(8,128)}, f32[8,136,128]{2,1,0:T(8,128)S(1)}, u32[]{:S(2)}) copy-start(f32[8,136,128]{2,1,0:T(8,128)S(1)} %collective-permute-done.6.other_ref.refs_3_) | copy-start | bytes 1671172
  89.2 26.8 %collective-permute-start.8 = (f32[8,136,128]{2,1,0:T(8,128)S(1)}, f32[8,136,128]{2,1,0:T(8,128)S(1)}, u32[]{:S(2)}, u32[]{:S(2)}) collective-permute-start(f32[8,136,128]{2,1,0:T(8,128)S(1)} %merge.15.refs_0_.mine_ref), channel_id=1, source_target_pairs={{0,32},{2,34},{4,36},{6,38},{8,40},{10,42},{12,44},{14,46},{16,48}... | collective-permute-start | bytes 1671176 | tf_op jit(solution)/shard_map/ppermute | solution.py:494
  91.7 12.3 %copy-start.3 = (f32[8,136,128]{2,1,0:T(8,128)}, f32[8,136,128]{2,1,0:T(8,128)S(1)}, u32[]{:S(2)}) copy-start(f32[8,136,128]{2,1,0:T(8,128)S(1)} %collective-permute-done.5.other_ref.refs_2_) | copy-start | bytes 1671172
  92.4 28.6 %collective-permute-start.7 = (f32[8,136,128]{2,1,0:T(8,128)S(1)}, f32[8,136,128]{2,1,0:T(8,128)S(1)}, u32[]{:S(2)}, u32[]{:S(2)}) collective-permute-start(f32[8,136,128]{2,1,0:T(8,128)S(1)} %merge.16.refs_1_.mine_ref), channel_id=1, source_target_pairs={{0,24},{2,26},{4,28},{6,30},{8,16},{10,18},{12,20},{14,22},{16,8},... | collective-permute-start | bytes 1671176 | tf_op jit(solution)/shard_map/ppermute | solution.py:494
  95.4 8.7 %copy-start.8 = (f32[8,136,128]{2,1,0:T(8,128)S(1)}, f32[8,136,128]{2,1,0:T(8,128)}, u32[]{:S(2)}) copy-start(f32[8,136,128]{2,1,0:T(8,128)} %copy-done.7) | copy-start | bytes 1671172
  117.5 19.6 %collective-permute-start.10 = (f32[8,136,128]{2,1,0:T(8,128)}, f32[8,136,128]{2,1,0:T(8,128)}, u32[]{:S(2)}, u32[]{:S(2)}) collective-permute-start(f32[8,136,128]{2,1,0:T(8,128)} %merge.17.refs_0_), channel_id=1, source_target_pairs={{0,96},{2,98},{4,100},{6,102},{8,104},{10,106},{12,108},{14,110},{... | collective-permute-start | bytes 1671176 | tf_op jit(solution)/shard_map/ppermute | solution.py:494
  121.6 0.8 copy-start.4
  122.4 2.0 %copy-start.1 = (f32[8,136,128]{2,1,0:T(8,128)}, f32[8,136,128]{2,1,0:T(8,128)S(1)}, u32[]{:S(2)}) copy-start(f32[8,136,128]{2,1,0:T(8,128)S(1)} %merge.18.refs_4_.mine_ref) | copy-start | bytes 1671172
  122.4 24.9 %collective-permute-start.9 = (f32[8,136,128]{2,1,0:T(8,128)S(1)}, f32[8,136,128]{2,1,0:T(8,128)S(1)}, u32[]{:S(2)}, u32[]{:S(2)}) collective-permute-start(f32[8,136,128]{2,1,0:T(8,128)S(1)} %merge.18.refs_4_.mine_ref), channel_id=1, source_target_pairs={{0,32},{2,34},{4,36},{6,38},{8,40},{10,42},{12,44},{14,46},{16,48}... | collective-permute-start | bytes 1671176 | tf_op jit(solution)/shard_map/ppermute | solution.py:494
  124.4 12.7 %copy-start = (f32[512,2048]{1,0:T(8,128)S(1)}, f32[512,2048]{1,0:T(8,128)}, u32[]{:S(2)}) copy-start(f32[512,2048]{1,0:T(8,128)} %q_ref.15) | copy-start | bytes 12582916
  124.4 12.7 %copy-start.9 = (f32[512,1024]{1,0:T(8,128)S(1)}, f32[512,1024]{1,0:T(8,128)}, u32[]{:S(2)}) copy-start(f32[512,1024]{1,0:T(8,128)} %get-tuple-element.46.near_ref) | copy-start | bytes 6291460
  124.4 12.7 %copy-start.14 = (f32[2048]{0:T(1024)S(1)}, f32[2048]{0:T(1024)}, u32[]{:S(2)}) copy-start(f32[2048]{0:T(1024)} %param.12) | copy-start | bytes 24580
  131.5 15.8 %copy-start.2 = (f32[8,136,128]{2,1,0:T(8,128)S(1)}, f32[8,136,128]{2,1,0:T(8,128)}, u32[]{:S(2)}) copy-start(f32[8,136,128]{2,1,0:T(8,128)} %copy-done.1) | copy-start | bytes 1671172
  142.6 1.0 copy-start.17
  143.6 4.4 %copy-start.15 = (bf16[512,1024]{1,0:T(8,128)(2,1)}, bf16[512,1024]{1,0:T(8,128)(2,1)S(1)}, u32[]{:S(2)}) copy-start(bf16[512,1024]{1,0:T(8,128)(2,1)S(1)} %get-tuple-element.48.x_hi) | copy-start | bytes 3145732
  148.0 14.5 %collective-permute-start.11 = (f32[8,136,128]{2,1,0:T(8,128)S(1)}, f32[8,136,128]{2,1,0:T(8,128)S(1)}, u32[]{:S(2)}, u32[]{:S(2)}) collective-permute-start(f32[8,136,128]{2,1,0:T(8,128)S(1)} %merge.19.refs_0_), channel_id=1, source_target_pairs={{0,96},{2,98},{4,100},{6,102},{8,104},{10,106},{12,108},{14,110},{... | collective-permute-start | bytes 1671176 | tf_op jit(solution)/shard_map/ppermute | solution.py:494
  149.9 1.2 copy-start.16
  151.2 1.2 copy-start.18
  152.4 10.2 %copy-start.10 = (f32[512,1024]{1,0:T(8,128)S(1)}, f32[512,1024]{1,0:T(8,128)}, u32[]{:S(2)}) copy-start(f32[512,1024]{1,0:T(8,128)} %get-tuple-element.44.near_ref) | copy-start | bytes 6291460
  172.4 11.0 %collective-permute-start.12 = (f32[512,1024]{1,0:T(8,128)S(1)}, f32[512,1024]{1,0:T(8,128)S(1)}, u32[]{:S(2)}, u32[]{:S(2)}) collective-permute-start(f32[512,1024]{1,0:T(8,128)S(1)} %get-tuple-element.54), channel_id=1, source_target_pairs={{0,1},{1,0},{2,3},{3,2},{4,5},{5,4},{6,7},{7,6},{8,9},{9,8},{10,11... | collective-permute-start | bytes 6291464 | tf_op jit(solution)/shard_map/ppermute | solution.py:548
  (1 other events, 0.8 us)
Sparse Core Ops, SparseCore 0:
  10.2 136.2 all-gather.1

commit v8 on v7

--- a/solution.py
+++ b/solution.py
@@ -537,7 +537,7 @@
     a_hi, a_lo, token = finish(
         upper, queries, far_a, before_a, weights, levels, gain, came_a[early:], 0, after=(before_b,)
     )
-    go(b, came_b, token)
+    go(b, came_b, token, weight[:8, :CHUNK])
 
     me = lax.axis_index("head").astype(jnp.int32)
     both = jnp.stack([sides - 1 - me, me])

time: 193 us -> 193 us (level)
    ppermute x12, starting transfers between devices: 22.9 us -> 26.5 us  [send(): lax.ppermute(block, 'seq', [(s, s ^ flip) for s in range(n_seq) if wanted...]
    ppermute x12, waiting for transfers between devices: 46.7 us -> 43.2 us  [send(): lax.ppermute(block, 'seq', [(s, s ^ flip) for s in range(n_seq) if wanted...]
    ppermute x1, starting transfers between devices: 5.09 us -> 1.83 us  [local(): lax.ppermute(to_send, 'head', [(s, sides - 1 - s) for s in range(sides)])]
    all_gather x1, waiting for transfers between devices: 0.02 us -> 2.36 us  [local(): weight = lax.all_gather(out_weight.T, 'seq', axis=0, tiled=True)]
    unnamed x38 -> x30, local copies, waits for them, and re-layouts: 5.04 us -> 3.83 us
  transfers between devices with their start and end apart: 14 -> 14, of which waited for: 7 -> 8; matrix products, arithmetic and copies ran while one was open for 0% -> 0% of each run, Pallas kernels for 45% -> 45%
where the time goes in v8:
time: 193 us; the launch traced here: 192 us
  Pallas kernels  96.8 us (50%)
  waiting for transfers between devices  46.3 us (24%)
  starting transfers between devices  28.4 us (15%)
  between operations  13.6 us (7%)
  local copies, waits for them, and re-layouts  4.5 us (2%)
  other arithmetic  1.96 us (1%)
    ppermute x12, waiting for transfers between devices, send(): lax.ppermute(block, 'seq', [(s, s ^ flip) for s in range(n_seq) if wanted...  43.2 us
    pallas_call x4, Pallas kernels, near_part(): pl.pallas_call(functools.partial(near_kernel, first, levels), out_shape=(...  34.3 us
    ppermute x12, starting transfers between devices, send(): lax.ppermute(block, 'seq', [(s, s ^ flip) for s in range(n_seq) if wanted...  26.5 us
    pallas_call x2, Pallas kernels, project(): pl.pallas_call(functools.partial(project_kernel, part, used, bool(extra))...  16.1 us
    pallas_call x2, Pallas kernels, finish(): pl.pallas_call(functools.partial(finish_kernel, first, levels, skip, tile...  15.3 us
    pallas_call x2, Pallas kernels, early_levels(): pl.pallas_call(functools.partial(early_kernel, first, levels, len(states)...  13.2 us
    pallas_call x2, Pallas kernels, own_state(): pl.pallas_call(state_kernel, out_shape=jax.ShapeDtypeStruct((heads, ROWS,...  9.56 us
    pallas_call x10, Pallas kernels, merged(): pl.pallas_call(functools.partial(merge_kernel, bit, bool(more)), out_shap...  7.87 us
  transfers between devices with their start and end apart: 14, of which 8 were waited for; matrix products, arithmetic and copies ran while one was open for 0% of the time, Pallas kernels for 45%

profile of v8, /device:TPU:1, one launch (start us, length us, event | category | flops | bytes accessed | tf_op | source)
XLA Modules:
  0.0 191.5 jit_solution(1329277063102618339)
XLA Ops:
  8.0 4.8 %own_state.2.refs_0_.mine_ref = f32[8,136,128]{2,1,0:T(8,128)S(1)} custom-call(f32[512,2048]{1,0:T(8,128)} %k_ref.11, f32[512,2048]{1,0:T(8,128)} %v_ref.11, f32[16,512]{1,0:T(8,128)S(1)} %copy-done.10), custom_call_target="tpu_custom_call" | custom-call | flops 536870912 | bytes 4194304 | tf_op jit(solution)/shard_map/own_state/pallas_call | solution.py:88
  12.8 2.2 %collective-permute-start = (f32[8,136,128]{2,1,0:T(8,128)S(1)}, f32[8,136,128]{2,1,0:T(8,128)S(1)}, u32[]{:S(2)}, u32[]{:S(2)}) collective-permute-start(f32[8,136,128]{2,1,0:T(8,128)S(1)} %own_state.2.refs_0_.mine_ref), channel_id=1, source_target_pairs={{0,2},{2,0},{4,6},{6,4},{8,10},{10,8},{12,14},{14,12},{16,18},{18,... | collective-permute-start | bytes 1671176 | tf_op jit(solution)/shard_map/ppermute | solution.py:494
  15.0 4.8 %own_state.3.refs_0_ = f32[8,136,128]{2,1,0:T(8,128)S(1)} custom-call(f32[512,2048]{1,0:T(8,128)} %k_ref.11, f32[512,2048]{1,0:T(8,128)} %v_ref.11, f32[16,512]{1,0:T(8,128)S(1)} %copy-done.11, f32[8,136,128]{2,1,0:T(8,128)S(1)} %own_state.2.refs_0_.mine_ref), custom_call_target="tpu_custom_call" | custom-call | flops 536870912 | bytes 4194304 | tf_op jit(solution)/shard_map/own_state/pallas_call | solution.py:88
  20.3 6.9 %collective-permute-done.other_ref.refs_0_ = f32[8,136,128]{2,1,0:T(8,128)S(1)} collective-permute-done((f32[8,136,128]{2,1,0:T(8,128)S(1)}, f32[8,136,128]{2,1,0:T(8,128)S(1)}, u32[]{:S(2)}, u32[]{:S(2)}) %collective-permute-start) | collective-permute-done | bytes 557088 | tf_op jit(solution)/shard_map/ppermute | solution.py:494
  27.9 3.8 %collective-permute-start.2 = (f32[8,136,128]{2,1,0:T(8,128)S(1)}, f32[8,136,128]{2,1,0:T(8,128)S(1)}, u32[]{:S(2)}, u32[]{:S(2)}) collective-permute-start(f32[8,136,128]{2,1,0:T(8,128)S(1)} %get-tuple-element.35.mine_ref), channel_id=1, source_target_pairs={{0,6},{2,4},{4,2},{6,0},{8,14},{10,12},{12,10},{14,8},{16,22},{18,... | collective-permute-start | bytes 1671176 | tf_op jit(solution)/shard_map/ppermute | solution.py:494
  31.7 8.5 %near.4 = (f32[512,2048]{1,0:T(8,128)}, f32[8,128]{1,0:T(8,128)S(1)}) custom-call(f32[512,2048]{1,0:T(8,128)} %q_ref.15, f32[512,2048]{1,0:T(8,128)} %k_ref.11, f32[512,2048]{1,0:T(8,128)} %v_ref.11, f32[16,1,512]{2,1,0:T(1,128)S(1)} %get-tuple-element.30.sums_ref, f32[512,128]{1,0:T(8,128)S(1)} %get-tuple-element.31.cols_ref, ...), custom_call_target="tpu_custom_call" | custom-call | flops 2013265920 | bytes 4194304 | tf_op jit(solution)/shard_map/near/pallas_call | solution.py:243
  40.2 5.5 %collective-permute-done.2.other_ref.refs_1_ = f32[8,136,128]{2,1,0:T(8,128)S(1)} collective-permute-done((f32[8,136,128]{2,1,0:T(8,128)S(1)}, f32[8,136,128]{2,1,0:T(8,128)S(1)}, u32[]{:S(2)}, u32[]{:S(2)}) %collective-permute-start.2) | collective-permute-done | bytes 557088 | tf_op jit(solution)/shard_map/ppermute | solution.py:494
  47.3 1.9 collective-permute-start.3
  49.2 8.5 %near.5 = (f32[512,2048]{1,0:T(8,128)}, f32[8,128]{1,0:T(8,128)S(1)}) custom-call(f32[512,2048]{1,0:T(8,128)} %q_ref.15, f32[512,2048]{1,0:T(8,128)} %k_ref.11, f32[512,2048]{1,0:T(8,128)} %v_ref.11, f32[16,1,512]{2,1,0:T(1,128)S(1)} %get-tuple-element.30.sums_ref, f32[512,128]{1,0:T(8,128)S(1)} %get-tuple-element.31.cols_ref, ...), custom_call_target="tpu_custom_call", output_to_operand_aliasing={{0}: (6, {})} | custom-call | flops 2013265920 | bytes 4194304 | tf_op jit(solution)/shard_map/near/pallas_call | solution.py:243
  57.7 12.3 %collective-permute-done.4.other_ref.refs_2_ = f32[8,136,128]{2,1,0:T(8,128)S(1)} collective-permute-done((f32[8,136,128]{2,1,0:T(8,128)S(1)}, f32[8,136,128]{2,1,0:T(8,128)S(1)}, u32[]{:S(2)}, u32[]{:S(2)}) %collective-permute-start.4) | collective-permute-done | bytes 557088 | tf_op jit(solution)/shard_map/ppermute | solution.py:494
  70.7 1.6 collective-permute-start.6
  73.4 8.6 %near.6 = (f32[512,2048]{1,0:T(8,128)}, f32[8,128]{1,0:T(8,128)S(1)}) custom-call(f32[512,2048]{1,0:T(8,128)} %q_ref.15, f32[512,2048]{1,0:T(8,128)} %k_ref.11, f32[512,2048]{1,0:T(8,128)} %v_ref.11, f32[16,1,512]{2,1,0:T(1,128)S(1)} %get-tuple-element.30.sums_ref, f32[512,128]{1,0:T(8,128)S(1)} %get-tuple-element.31.cols_ref, ...), custom_call_target="tpu_custom_call", output_to_operand_aliasing={{0}: (6, {})} | custom-call | flops 2013265920 | bytes 4194304 | tf_op jit(solution)/shard_map/near/pallas_call | solution.py:243
  82.0 6.6 %collective-permute-done.6.other_ref.refs_3_ = f32[8,136,128]{2,1,0:T(8,128)S(1)} collective-permute-done((f32[8,136,128]{2,1,0:T(8,128)S(1)}, f32[8,136,128]{2,1,0:T(8,128)S(1)}, u32[]{:S(2)}, u32[]{:S(2)}) %collective-permute-start.6) | collective-permute-done | bytes 557088 | tf_op jit(solution)/shard_map/ppermute | solution.py:494
  89.2 2.5 %collective-permute-start.8 = (f32[8,136,128]{2,1,0:T(8,128)S(1)}, f32[8,136,128]{2,1,0:T(8,128)S(1)}, u32[]{:S(2)}, u32[]{:S(2)}) collective-permute-start(f32[8,136,128]{2,1,0:T(8,128)S(1)} %merge.15.refs_0_.mine_ref), channel_id=1, source_target_pairs={{0,32},{2,34},{4,36},{6,38},{8,40},{10,42},{12,44},{14,46},{16,48}... | collective-permute-start | bytes 1671176 | tf_op jit(solution)/shard_map/ppermute | solution.py:494
  92.3 3.0 %collective-permute-start.7 = (f32[8,136,128]{2,1,0:T(8,128)S(1)}, f32[8,136,128]{2,1,0:T(8,128)S(1)}, u32[]{:S(2)}, u32[]{:S(2)}) collective-permute-start(f32[8,136,128]{2,1,0:T(8,128)S(1)} %merge.16.refs_1_.mine_ref), channel_id=1, source_target_pairs={{0,24},{2,26},{4,28},{6,30},{8,16},{10,18},{12,20},{14,22},{16,8},... | collective-permute-start | bytes 1671176 | tf_op jit(solution)/shard_map/ppermute | solution.py:494
  95.4 8.6 %near.7 = (f32[512,2048]{1,0:T(8,128)}, f32[8,128]{1,0:T(8,128)S(1)}) custom-call(f32[512,2048]{1,0:T(8,128)} %q_ref.15, f32[512,2048]{1,0:T(8,128)} %k_ref.11, f32[512,2048]{1,0:T(8,128)} %v_ref.11, f32[16,1,512]{2,1,0:T(1,128)S(1)} %get-tuple-element.30.sums_ref, f32[512,128]{1,0:T(8,128)S(1)} %get-tuple-element.31.cols_ref, ...), custom_call_target="tpu_custom_call", output_to_operand_aliasing={{0}: (6, {})} | custom-call | flops 2013265920 | bytes 4194304 | tf_op jit(solution)/shard_map/near/pallas_call | solution.py:243
  104.0 6.0 %early.2 = (f32[512,1024]{1,0:T(8,128)}, f32[8,8,128]{2,1,0:T(8,128)S(1)}) custom-call(s32[6]{0:T(128)S(1)} %shift-right-arithmetic_and_fusion.upper_ref, f32[512,2048]{1,0:T(8,128)} %q_ref.15, f32[512,2048]{1,0:T(8,128)} %get-tuple-element.41.near_ref, f32[512,256]{1,0:T(8,128)S(1)} %get-tuple-element.32.refs_1_.w_ref, f32[8,136,128]{2,1,0:T(8,128)S(1)} %copy-done.6, ...), custom_call_target="tpu_custom_call" | custom-call | flops 2147483648 | bytes 8388608 | tf_op jit(solution)/shard_map/early/pallas_call | solution.py:306
  110.1 5.9 %collective-permute-done.8.other_ref.refs_0_ = f32[8,136,128]{2,1,0:T(8,128)S(1)} collective-permute-done((f32[8,136,128]{2,1,0:T(8,128)S(1)}, f32[8,136,128]{2,1,0:T(8,128)S(1)}, u32[]{:S(2)}, u32[]{:S(2)}) %collective-permute-start.8) | collective-permute-done | bytes 557088 | tf_op jit(solution)/shard_map/ppermute | solution.py:494
  116.7 3.9 %collective-permute-start.10 = (f32[8,136,128]{2,1,0:T(8,128)S(1)}, f32[8,136,128]{2,1,0:T(8,128)}, u32[]{:S(2)}, u32[]{:S(2)}) collective-permute-start(f32[8,136,128]{2,1,0:T(8,128)S(1)} %merge.17.refs_0_), channel_id=1, source_target_pairs={{0,96},{2,98},{4,100},{6,102},{8,104},{10,106},{12,108},{14,110},{... | collective-permute-start | bytes 1671176 | tf_op jit(solution)/shard_map/ppermute | solution.py:494
  120.5 1.5 merge.18.refs_4_.mine_ref
  122.8 1.9 collective-permute-start.9
  124.8 7.1 %early.3 = (f32[512,1024]{1,0:T(8,128)}, f32[8,8,128]{2,1,0:T(8,128)S(1)}) custom-call(s32[6]{0:T(128)S(1)} %shift-right-arithmetic_and_fusion.upper_ref, f32[512,2048]{1,0:T(8,128)} %q_ref.15, f32[512,2048]{1,0:T(8,128)} %get-tuple-element.41.near_ref, f32[512,256]{1,0:T(8,128)S(1)} %get-tuple-element.32.refs_1_.w_ref, ...), custom_call_target="tpu_custom_call" | custom-call | flops 2147483648 | bytes 8388608 | tf_op jit(solution)/shard_map/early/pallas_call | solution.py:306
  131.9 5.2 %collective-permute-done.10.refs_1_ = f32[8,136,128]{2,1,0:T(8,128)} collective-permute-done((f32[8,136,128]{2,1,0:T(8,128)S(1)}, f32[8,136,128]{2,1,0:T(8,128)}, u32[]{:S(2)}, u32[]{:S(2)}) %collective-permute-start.10) | collective-permute-done | bytes 557088 | tf_op jit(solution)/shard_map/ppermute | solution.py:494
  137.2 5.5 %finish.2 = (bf16[512,1024]{1,0:T(8,128)(2,1)S(1)}, bf16[512,1024]{1,0:T(8,128)(2,1)S(1)}, f32[8,128]{1,0:T(8,128)S(1)}) custom-call(s32[6]{0:T(128)S(1)} %shift-right-arithmetic_and_fusion.upper_ref, f32[512,2048]{1,0:T(8,128)S(1)} %copy-done, f32[512,1024]{1,0:T(8,128)S(1)} %copy-done.7, f32[8,8,128]{2,1,0:T(8,128)S(1)} %get-tuple-element.43.refs_0_.before_ref, ...), custom_call_target="tpu_custom_call" | custom-call | flops 536870912 | bytes 8388608 | tf_op jit(solution)/shard_map/finish/pallas_call | solution.py:417
  143.6 2.4 %all-gather.2.cloned.1.call-done.weight_ref.refs_3_ = f32[2048,2048]{1,0:T(8,128)} async-done(((f32[32,2048]{1,0:T(8,128)}), f32[2048,2048]{1,0:T(8,128)}) %all-gather.2.cloned.1.call-update) | async-done | bytes 16777232 | tf_op jit(solution)/shard_map/all_gather | solution.py:484
  148.6 5.1 %collective-permute-start.11 = (f32[8,136,128]{2,1,0:T(8,128)S(1)}, f32[8,136,128]{2,1,0:T(8,128)S(1)}, u32[]{:S(2)}, u32[]{:S(2)}) collective-permute-start(f32[8,136,128]{2,1,0:T(8,128)S(1)} %merge.19.refs_0_), channel_id=1, source_target_pairs={{0,96},{2,98},{4,100},{6,102},{8,104},{10,106},{12,108},{14,110},{... | collective-permute-start | bytes 1671176 | tf_op jit(solution)/shard_map/ppermute | solution.py:494
  153.7 1.2 copy-done.14
  155.0 10.2 %project.2 = (f32[512,1024]{1,0:T(8,128)S(1)}, f32[512,1024]{1,0:T(8,128)S(1)}) custom-call(s32[2]{0:T(128)S(1)} %pad_add_fusion.sides_ref.refs_2_, bf16[512,1024]{1,0:T(8,128)(2,1)S(1)} %get-tuple-element.48.x_hi, bf16[512,1024]{1,0:T(8,128)(2,1)S(1)} %copy-done.14, f32[2048,2048]{1,0:T(8,128)} %all-gather.2.cloned.1.call-done.weight_ref.refs_3_, ...), custom_call_target="tpu_custom_call" | custom-call | flops 6442450944 | bytes 8388608 | tf_op jit(solution)/shard_map/project/pallas_call | solution.py:463
  165.2 9.8 %finish.3 = (bf16[512,1024]{1,0:T(8,128)(2,1)S(1)}, bf16[512,1024]{1,0:T(8,128)(2,1)S(1)}, f32[512,1024]{1,0:T(8,128)S(1)}) custom-call(s32[6]{0:T(128)S(1)} %shift-right-arithmetic_and_fusion.upper_ref, f32[512,2048]{1,0:T(8,128)} %q_ref.15, f32[512,1024]{1,0:T(8,128)S(1)} %copy-done.8, f32[8,8,128]{2,1,0:T(8,128)S(1)} %get-tuple-element.45.refs_2_.before_ref, ...), custom_call_target="tpu_custom_call" | custom-call | flops 3758096384 | bytes 8388608 | tf_op jit(solution)/shard_map/finish/pallas_call | solution.py:417
  175.0 1.8 collective-permute-start.12
  176.8 5.9 %project.3 = f32[512,1024]{1,0:T(8,128)S(1)} custom-call(s32[2]{0:T(128)S(1)} %pad_add_fusion.sides_ref.refs_2_, bf16[512,1024]{1,0:T(8,128)(2,1)S(1)} %get-tuple-element.51.x_hi, bf16[512,1024]{1,0:T(8,128)(2,1)S(1)} %get-tuple-element.52.x_lo, f32[2048,2048]{1,0:T(8,128)} %all-gather.2.cloned.1.call-done.weight_ref.refs_3_, ...), custom_call_target="tpu_custom_call" | custom-call | flops 3221225472 | bytes 8388608 | tf_op jit(solution)/shard_map/project/pallas_call | solution.py:463
  182.8 1.9 add.3
  (54 shorter events, 12.4 us)
Async XLA Ops:
  6.5 139.5 %all-gather.2.cloned.1.call-start = ((), (), s32[]{:S(2)}) async-start(), calls=%async_computation | async-start | bytes 17039360 | tf_op jit(solution)/shard_map/all_gather | solution.py:484
  7.3 0.8 copy-start.10
  8.0 7.0 %copy-start.11 = (f32[16,512]{1,0:T(8,128)S(1)}, f32[16,512]{1,0:T(8,128)}, u32[]{:S(2)}) copy-start(f32[16,512]{1,0:T(8,128)} %ld_ref.5) | copy-start | bytes 98308
  12.8 14.4 %collective-permute-start = (f32[8,136,128]{2,1,0:T(8,128)S(1)}, f32[8,136,128]{2,1,0:T(8,128)S(1)}, u32[]{:S(2)}, u32[]{:S(2)}) collective-permute-start(f32[8,136,128]{2,1,0:T(8,128)S(1)} %own_state.2.refs_0_.mine_ref), channel_id=1, source_target_pairs={{0,2},{2,0},{4,6},{6,4},{8,10},{10,8},{12,14},{14,12},{16,18},{18,... | collective-permute-start | bytes 1671176 | tf_op jit(solution)/shard_map/ppermute | solution.py:494
  15.0 4.8 %copy-start.9 = (f32[16,16,512]{2,1,0:T(8,128)S(1)}, f32[16,16,512]{2,1,0:T(8,128)}, u32[]{:S(2)}) copy-start(f32[16,16,512]{2,1,0:T(8,128)} %w_ref.1) | copy-start | bytes 1572868
  27.2 13.0 %copy-start.5 = (f32[8,136,128]{2,1,0:T(8,128)}, f32[8,136,128]{2,1,0:T(8,128)S(1)}, u32[]{:S(2)}) copy-start(f32[8,136,128]{2,1,0:T(8,128)S(1)} %collective-permute-done.other_ref.refs_0_) | copy-start | bytes 1671172
  27.9 17.9 %collective-permute-start.2 = (f32[8,136,128]{2,1,0:T(8,128)S(1)}, f32[8,136,128]{2,1,0:T(8,128)S(1)}, u32[]{:S(2)}, u32[]{:S(2)}) collective-permute-start(f32[8,136,128]{2,1,0:T(8,128)S(1)} %get-tuple-element.35.mine_ref), channel_id=1, source_target_pairs={{0,6},{2,4},{4,2},{6,0},{8,14},{10,12},{12,10},{14,8},{16,22},{18,... | collective-permute-start | bytes 1671176 | tf_op jit(solution)/shard_map/ppermute | solution.py:494
  31.7 14.9 %collective-permute-start.1 = (f32[8,136,128]{2,1,0:T(8,128)S(1)}, f32[8,136,128]{2,1,0:T(8,128)S(1)}, u32[]{:S(2)}, u32[]{:S(2)}) collective-permute-start(f32[8,136,128]{2,1,0:T(8,128)S(1)} %get-tuple-element.33.refs_0_.mine_ref), channel_id=1, source_target_pairs={{0,2},{2,0},{4,6},{6,4},{8,10},{10,8},{12,14},{14,12},{16,18},{18,... | collective-permute-start | bytes 1671176 | tf_op jit(solution)/shard_map/ppermute | solution.py:494
  46.4 23.6 %collective-permute-start.4 = (f32[8,136,128]{2,1,0:T(8,128)S(1)}, f32[8,136,128]{2,1,0:T(8,128)S(1)}, u32[]{:S(2)}, u32[]{:S(2)}) collective-permute-start(f32[8,136,128]{2,1,0:T(8,128)S(1)} %merge.11.refs_0_.mine_ref), channel_id=1, source_target_pairs={{0,8},{2,10},{4,12},{6,14},{8,0},{10,2},{12,4},{14,6},{16,24},{18,... | collective-permute-start | bytes 1671176 | tf_op jit(solution)/shard_map/ppermute | solution.py:494
  47.3 25.0 %collective-permute-start.3 = (f32[8,136,128]{2,1,0:T(8,128)S(1)}, f32[8,136,128]{2,1,0:T(8,128)S(1)}, u32[]{:S(2)}, u32[]{:S(2)}) collective-permute-start(f32[8,136,128]{2,1,0:T(8,128)S(1)} %merge.12.refs_1_.mine_ref), channel_id=1, source_target_pairs={{0,6},{2,4},{4,2},{6,0},{8,14},{10,12},{12,10},{14,8},{16,22},{18,... | collective-permute-start | bytes 1671176 | tf_op jit(solution)/shard_map/ppermute | solution.py:494
  70.0 11.9 %copy-start.3 = (f32[8,136,128]{2,1,0:T(8,128)}, f32[8,136,128]{2,1,0:T(8,128)S(1)}, u32[]{:S(2)}) copy-start(f32[8,136,128]{2,1,0:T(8,128)S(1)} %collective-permute-done.4.other_ref.refs_2_) | copy-start | bytes 1671172
  70.7 17.8 %collective-permute-start.6 = (f32[8,136,128]{2,1,0:T(8,128)S(1)}, f32[8,136,128]{2,1,0:T(8,128)S(1)}, u32[]{:S(2)}, u32[]{:S(2)}) collective-permute-start(f32[8,136,128]{2,1,0:T(8,128)S(1)} %merge.13.refs_0_.mine_ref), channel_id=1, source_target_pairs={{0,24},{2,26},{4,28},{6,30},{8,16},{10,18},{12,20},{14,22},{16,8},... | collective-permute-start | bytes 1671176 | tf_op jit(solution)/shard_map/ppermute | solution.py:494
  72.9 18.7 %collective-permute-start.5 = (f32[8,136,128]{2,1,0:T(8,128)S(1)}, f32[8,136,128]{2,1,0:T(8,128)S(1)}, u32[]{:S(2)}, u32[]{:S(2)}) collective-permute-start(f32[8,136,128]{2,1,0:T(8,128)S(1)} %merge.14.refs_1_.mine_ref), channel_id=1, source_target_pairs={{0,8},{2,10},{4,12},{6,14},{8,0},{10,2},{12,4},{14,6},{16,24},{18,... | collective-permute-start | bytes 1671176 | tf_op jit(solution)/shard_map/ppermute | solution.py:494
  88.5 15.5 %copy-start.4 = (f32[8,136,128]{2,1,0:T(8,128)}, f32[8,136,128]{2,1,0:T(8,128)S(1)}, u32[]{:S(2)}) copy-start(f32[8,136,128]{2,1,0:T(8,128)S(1)} %collective-permute-done.6.other_ref.refs_3_) | copy-start | bytes 1671172
  89.2 26.8 %collective-permute-start.8 = (f32[8,136,128]{2,1,0:T(8,128)S(1)}, f32[8,136,128]{2,1,0:T(8,128)S(1)}, u32[]{:S(2)}, u32[]{:S(2)}) collective-permute-start(f32[8,136,128]{2,1,0:T(8,128)S(1)} %merge.15.refs_0_.mine_ref), channel_id=1, source_target_pairs={{0,32},{2,34},{4,36},{6,38},{8,40},{10,42},{12,44},{14,46},{16,48}... | collective-permute-start | bytes 1671176 | tf_op jit(solution)/shard_map/ppermute | solution.py:494
  91.7 12.4 %copy-start.1 = (f32[8,136,128]{2,1,0:T(8,128)}, f32[8,136,128]{2,1,0:T(8,128)S(1)}, u32[]{:S(2)}) copy-start(f32[8,136,128]{2,1,0:T(8,128)S(1)} %collective-permute-done.5.other_ref.refs_2_) | copy-start | bytes 1671172
  92.3 28.2 %collective-permute-start.7 = (f32[8,136,128]{2,1,0:T(8,128)S(1)}, f32[8,136,128]{2,1,0:T(8,128)S(1)}, u32[]{:S(2)}, u32[]{:S(2)}) collective-permute-start(f32[8,136,128]{2,1,0:T(8,128)S(1)} %merge.16.refs_1_.mine_ref), channel_id=1, source_target_pairs={{0,24},{2,26},{4,28},{6,30},{8,16},{10,18},{12,20},{14,22},{16,8},... | collective-permute-start | bytes 1671176 | tf_op jit(solution)/shard_map/ppermute | solution.py:494
  95.4 8.7 %copy-start.6 = (f32[8,136,128]{2,1,0:T(8,128)S(1)}, f32[8,136,128]{2,1,0:T(8,128)}, u32[]{:S(2)}) copy-start(f32[8,136,128]{2,1,0:T(8,128)} %copy-done.5) | copy-start | bytes 1671172
  116.7 20.5 %collective-permute-start.10 = (f32[8,136,128]{2,1,0:T(8,128)S(1)}, f32[8,136,128]{2,1,0:T(8,128)}, u32[]{:S(2)}, u32[]{:S(2)}) collective-permute-start(f32[8,136,128]{2,1,0:T(8,128)S(1)} %merge.17.refs_0_), channel_id=1, source_target_pairs={{0,96},{2,98},{4,100},{6,102},{8,104},{10,106},{12,108},{14,110},{... | collective-permute-start | bytes 1671176 | tf_op jit(solution)/shard_map/ppermute | solution.py:494
  122.0 0.9 copy-start.2
  122.8 24.6 %collective-permute-start.9 = (f32[8,136,128]{2,1,0:T(8,128)}, f32[8,136,128]{2,1,0:T(8,128)S(1)}, u32[]{:S(2)}, u32[]{:S(2)}) collective-permute-start(f32[8,136,128]{2,1,0:T(8,128)} %merge.18.refs_4_.mine_ref), channel_id=1, source_target_pairs={{0,32},{2,34},{4,36},{6,38},{8,40},{10,42},{12,44},{14,46},{16,48}... | collective-permute-start | bytes 1671176 | tf_op jit(solution)/shard_map/ppermute | solution.py:494
  124.8 12.4 %copy-start = (f32[512,2048]{1,0:T(8,128)S(1)}, f32[512,2048]{1,0:T(8,128)}, u32[]{:S(2)}) copy-start(f32[512,2048]{1,0:T(8,128)} %q_ref.15) | copy-start | bytes 12582916
  124.8 12.4 %copy-start.7 = (f32[512,1024]{1,0:T(8,128)S(1)}, f32[512,1024]{1,0:T(8,128)}, u32[]{:S(2)}) copy-start(f32[512,1024]{1,0:T(8,128)} %get-tuple-element.46.near_ref) | copy-start | bytes 6291460
  124.8 12.4 %copy-start.12 = (f32[2048]{0:T(1024)S(1)}, f32[2048]{0:T(1024)}, u32[]{:S(2)}) copy-start(f32[2048]{0:T(1024)} %param.12) | copy-start | bytes 24580
  142.7 1.0 copy-start.13
  148.6 16.5 %collective-permute-start.11 = (f32[8,136,128]{2,1,0:T(8,128)S(1)}, f32[8,136,128]{2,1,0:T(8,128)S(1)}, u32[]{:S(2)}, u32[]{:S(2)}) collective-permute-start(f32[8,136,128]{2,1,0:T(8,128)S(1)} %merge.19.refs_0_), channel_id=1, source_target_pairs={{0,96},{2,98},{4,100},{6,102},{8,104},{10,106},{12,108},{14,110},{... | collective-permute-start | bytes 1671176 | tf_op jit(solution)/shard_map/ppermute | solution.py:494
  153.7 1.2 copy-start.14
  154.9 10.2 %copy-start.8 = (f32[512,1024]{1,0:T(8,128)S(1)}, f32[512,1024]{1,0:T(8,128)}, u32[]{:S(2)}) copy-start(f32[512,1024]{1,0:T(8,128)} %get-tuple-element.44.near_ref) | copy-start | bytes 6291460
  175.0 7.8 %collective-permute-start.12 = (f32[512,1024]{1,0:T(8,128)S(1)}, f32[512,1024]{1,0:T(8,128)S(1)}, u32[]{:S(2)}, u32[]{:S(2)}) collective-permute-start(f32[512,1024]{1,0:T(8,128)S(1)} %get-tuple-element.54), channel_id=1, source_target_pairs={{0,1},{1,0},{2,3},{3,2},{4,5},{5,4},{6,7},{7,6},{8,9},{9,8},{10,11... | collective-permute-start | bytes 6291464 | tf_op jit(solution)/shard_map/ppermute | solution.py:548
Sparse Core Ops, SparseCore 0:
  10.2 135.7 all-gather.1
